TPU v7x, 32 devices: a whole 2x2x4 slice. The times are simulated.
32 devices in a mesh: tok: 8 (over z, x), head: 4 (over y, core).
Axes of the slice: x: 2, y: 2, z: 4, core: 2. Of those that a mesh axis runs over, the one named last changes fastest.
Arguments:
- queries: bfloat16 [3072, 4096], P('tok', 'head'), may hold values from -100 to 100
- keys: bfloat16 [3072, 1024], P('tok', 'head'), may hold values from -5 to 5
- values: bfloat16 [3072, 1024], P('tok', 'head'), may hold values from -6 to 6
- lengths: int32 [16], replicated, may hold values from 1 to 1536, 3072 in all
- out_weight: bfloat16 [4096, 4096], P('head', 'tok'), may hold values from -0.09375 to 0.09375
Outputs:
- mixed: bfloat16 [3072, 4096], P('tok', 'head')
Inputs may be any that keep to these rules, and one draw needn't show every extreme that they name: Every document has at most 1536 tokens and the lengths sum to 3072.
All inputs are finite; a program needn't handle non-finite values.
Results may differ from a plain program's by a relative error of at most 0.015.
Values may be sent and summed in bfloat16 or wider, within the bound.
No kernel may reach another device: no remote copies, remote signals or barrier semaphores. Data moves between devices by JAX's collectives and lax.ppermute only.
A program may use at most 64 MiB of HBM per device.

v0:
```python
import math

import jax
import jax.numpy as jnp
from jax import lax
from jax.sharding import PartitionSpec as P

QH = 32
KVH = 8
HD = 128


def passed_along(value, axis, steps):
    count = lax.axis_size(axis)
    first, last = (max(0, -steps), min(count, count - steps))
    return lax.ppermute(value, axis, [(source, source + steps) for source in range(first, last)])


def doc_index(lengths, positions):
    ends = jnp.cumsum(lengths)
    return jnp.sum((positions[:, None] >= ends[None, :]).astype(jnp.int32), axis=1)


def body(queries, keys, values, lengths, out_weight):
    rows = queries.shape[0]
    groups = keys.shape[1] // HD
    ratio = QH // KVH
    scale = 1.0 / HD**0.5
    mine = lax.axis_index("tok")
    qpos = mine * rows + jnp.arange(rows, dtype=jnp.int32)
    qdoc = doc_index(lengths, qpos)
    qlocal = queries.reshape(rows, groups, ratio, HD)

    def absorb_block(carry, kpiece, vpiece, start):
        running, total, accum = carry
        count = kpiece.shape[0]
        kpos = start + jnp.arange(count, dtype=jnp.int32)
        kdoc = doc_index(lengths, kpos)
        allowed = (
            (qdoc[:, None] == kdoc[None, :])
            & (kpos[None, :] <= qpos[:, None])
            & (kpos[None, :] >= 0)
        )
        scores = (
            jnp.einsum(
                "qgrd,kgd->grqk",
                qlocal,
                kpiece.reshape(count, groups, HD),
                preferred_element_type=jnp.float32,
            )
            * scale
        )
        scores = jnp.where(allowed[None, None], scores, jnp.float32(-1e30))
        newtop = jnp.maximum(running, jnp.max(scores, axis=-1))
        weights = jnp.where(
            allowed[None, None], jnp.exp(scores - newtop[..., None]), jnp.float32(0.0)
        )
        factor = jnp.exp(running - newtop)
        total = total * factor + jnp.sum(weights, axis=-1)
        added = jnp.einsum(
            "grqk,kgd->grqd",
            weights.astype(jnp.bfloat16),
            vpiece.reshape(count, groups, HD),
            preferred_element_type=jnp.float32,
        )
        accum = accum * factor[..., None] + added
        return (newtop, total, accum)

    def absorb(carry, piece, start):
        kpiece, vpiece = piece
        count = kpiece.shape[0]
        width = math.gcd(count, 512)
        turns = count // width

        def one_turn(step, inner):
            offset = step * width
            kpart = lax.dynamic_slice_in_dim(kpiece, offset, width, 0)
            vpart = lax.dynamic_slice_in_dim(vpiece, offset, width, 0)
            return absorb_block(inner, kpart, vpart, start + offset)

        return lax.fori_loop(0, turns, one_turn, carry)

    start_state = (
        jnp.full((groups, ratio, rows), -1e30, jnp.float32),
        jnp.zeros((groups, ratio, rows), jnp.float32),
        jnp.zeros((groups, ratio, rows, HD), jnp.float32),
    )
    reach = lax.axis_size("tok") // 2
    state = absorb(start_state, (keys, values), mine * rows)

    def advance(step, carried):
        pieces, inner = carried
        pieces = passed_along((pieces[0], pieces[1]), "tok", 1)
        inner = absorb(inner, pieces, (mine - step) * rows)
        return (pieces, inner)

    final = lax.fori_loop(1, reach + 1, advance, ((keys, values), state))
    state = final[1]
    running, total, accum = state
    result = accum / total[..., None]
    attn = (
        jnp.transpose(result, (2, 0, 1, 3)).reshape(rows, groups * ratio * HD).astype(jnp.bfloat16)
    )
    terms = jnp.dot(
        attn,
        lax.all_gather(out_weight, "tok", axis=1, tiled=True),
        preferred_element_type=jnp.float32,
    )
    return lax.psum_scatter(terms.astype(jnp.bfloat16), "head", scatter_dimension=1, tiled=True)


def solution(mesh):
    placed = (P("tok", "head"), P("tok", "head"), P("tok", "head"), P(), P("head", "tok"))
    return jax.shard_map(
        body, mesh=mesh, in_specs=placed, out_specs=P("tok", "head"), check_vma=False
    )
```

profile of v0, /device:TPU:17, one launch (start us, length us, event | category | flops | bytes accessed | tf_op | source)
XLA Modules:
  0.0 215.3 jit_solution(2744692512182165840)
XLA Ops:
  10.5 15.1 %while.83 = (s32[]{:T(128)}, f32[2,4,384]{2,1,0:T(4,128)S(1)}, f32[2,4,384]{2,1,0:T(4,128)S(1)}, f32[2,4,384,128]{3,2,1,0:T(8,128)S(1)}, s32[384]{0:T(512)S(1)},...) while((s32[]{:T(128)}, f32[2,4,384]{2,1,0:T(4,128)S(1)}, ...), condition=%wide.region_6.7_spmd.clone.clone.clone, body=%wide.region_2.6_spmd.clone.clone.clone.sunk | while | flops 206263936 | bytes 15736375 | solution.py:81
  17.4 2.0 fusion.49
  25.6 116.7 %while.82 = (s32[]{:T(128)}, bf16[384,256]{0,1:T(8,128)(2,1)S(1)}, bf16[384,256]{0,1:T(8,128)(2,1)S(1)}, f32[2,4,384]{2,1,0:T(4,128)S(1)}, f32[2,4,384]{2,1,0:T(...) while((s32[]{:T(128)}, bf16[384,256]{0,1:T(8,128)(2,1)S(1)}, ...), condition=%wide.region_13.14_spmd.clone, body=%wide.region_7.13_spmd.clone.sunk | while | flops 205861504 | bytes 11804580 | solution.py:97
  25.6 3.1 %collective-permute-start = (bf16[384,256]{0,1:T(8,128)(2,1)S(1)}, bf16[384,256]{0,1:T(8,128)(2,1)S(1)}, u32[]{:S(2)}, u32[]{:S(2)}) collective-permute-start(bf16[384,256]{0,1:T(8,128)(2,1)S(1)} %get-tuple-element.1389), channel_id=1, source_target_pairs={{0,4},{4,8},{8,12},{12,16},{16,20},{20,24},{24,28},{1,5},{5,9},{9,... | collective-permute-start | bytes 589832 | tf_op jit(solution)/shard_map/while/body/eval_jaxpr/ppermute | solution.py:16
  28.7 3.2 %collective-permute-start.1 = (bf16[384,256]{0,1:T(8,128)(2,1)S(1)}, bf16[384,256]{0,1:T(8,128)(2,1)S(1)}, u32[]{:S(2)}, u32[]{:S(2)}) collective-permute-start(bf16[384,256]{0,1:T(8,128)(2,1)S(1)} %get-tuple-element.1390), channel_id=1, source_target_pairs={{0,4},{4,8},{8,12},{12,16},{16,20},{20,24},{24,28},{1,5},{5,9},{9,... | collective-permute-start | bytes 589832 | tf_op jit(solution)/shard_map/while/body/eval_jaxpr/ppermute | solution.py:16
  31.9 7.7 %collective-permute-done = bf16[384,256]{0,1:T(8,128)(2,1)S(1)} collective-permute-done((bf16[384,256]{0,1:T(8,128)(2,1)S(1)}, bf16[384,256]{0,1:T(8,128)(2,1)S(1)}, u32[]{:S(2)}, u32[]{:S(2)}) %collective-permute-start) | collective-permute-done | bytes 196640 | tf_op jit(solution)/shard_map/while/body/eval_jaxpr/ppermute | solution.py:16
  39.6 12.4 %collective-permute-done.1 = bf16[384,256]{0,1:T(8,128)(2,1)S(1)} collective-permute-done((bf16[384,256]{0,1:T(8,128)(2,1)S(1)}, bf16[384,256]{0,1:T(8,128)(2,1)S(1)}, u32[]{:S(2)}, u32[]{:S(2)}) %collective-permute-start.1) | collective-permute-done | bytes 196640 | tf_op jit(solution)/shard_map/while/body/eval_jaxpr/ppermute | solution.py:16
  52.0 6.4 %while.84 = (s32[]{:T(128)}, f32[2,4,384]{2,1,0:T(4,128)S(1)}, f32[2,4,384]{2,1,0:T(4,128)S(1)}, f32[2,4,384,128]{3,2,1,0:T(8,128)S(1)}, s32[384]{0:T(512)S(1)},...) while((s32[]{:T(128)}, f32[2,4,384]{2,1,0:T(4,128)S(1)}, ...), condition=%wide.region_12.12_spmd, body=%wide.region_8.11_spmd.sunk | while | flops 205861120 | bytes 9443347 | solution.py:81
  60.4 3.1 %collective-permute-start.1 = (bf16[384,256]{0,1:T(8,128)(2,1)S(1)}, bf16[384,256]{0,1:T(8,128)(2,1)S(1)}, u32[]{:S(2)}, u32[]{:S(2)}) collective-permute-start(bf16[384,256]{0,1:T(8,128)(2,1)S(1)} %get-tuple-element.1390), channel_id=1, source_target_pairs={{0,4},{4,8},{8,12},{12,16},{16,20},{20,24},{24,28},{1,5},{5,9},{9,... | collective-permute-start | bytes 589832 | tf_op jit(solution)/shard_map/while/body/eval_jaxpr/ppermute | solution.py:16
  63.5 3.7 %collective-permute-done = bf16[384,256]{0,1:T(8,128)(2,1)S(1)} collective-permute-done((bf16[384,256]{0,1:T(8,128)(2,1)S(1)}, bf16[384,256]{0,1:T(8,128)(2,1)S(1)}, u32[]{:S(2)}, u32[]{:S(2)}) %collective-permute-start) | collective-permute-done | bytes 196640 | tf_op jit(solution)/shard_map/while/body/eval_jaxpr/ppermute | solution.py:16
  67.3 4.2 %collective-permute-done.1 = bf16[384,256]{0,1:T(8,128)(2,1)S(1)} collective-permute-done((bf16[384,256]{0,1:T(8,128)(2,1)S(1)}, bf16[384,256]{0,1:T(8,128)(2,1)S(1)}, u32[]{:S(2)}, u32[]{:S(2)}) %collective-permute-start.1) | collective-permute-done | bytes 196640 | tf_op jit(solution)/shard_map/while/body/eval_jaxpr/ppermute | solution.py:16
  71.5 6.4 %while.84 = (s32[]{:T(128)}, f32[2,4,384]{2,1,0:T(4,128)S(1)}, f32[2,4,384]{2,1,0:T(4,128)S(1)}, f32[2,4,384,128]{3,2,1,0:T(8,128)S(1)}, s32[384]{0:T(512)S(1)},...) while((s32[]{:T(128)}, f32[2,4,384]{2,1,0:T(4,128)S(1)}, ...), condition=%wide.region_12.12_spmd, body=%wide.region_8.11_spmd.sunk | while | flops 205861120 | bytes 9443347 | solution.py:81
  79.9 3.7 %collective-permute-start.1 = (bf16[384,256]{0,1:T(8,128)(2,1)S(1)}, bf16[384,256]{0,1:T(8,128)(2,1)S(1)}, u32[]{:S(2)}, u32[]{:S(2)}) collective-permute-start(bf16[384,256]{0,1:T(8,128)(2,1)S(1)} %get-tuple-element.1390), channel_id=1, source_target_pairs={{0,4},{4,8},{8,12},{12,16},{16,20},{20,24},{24,28},{1,5},{5,9},{9,... | collective-permute-start | bytes 589832 | tf_op jit(solution)/shard_map/while/body/eval_jaxpr/ppermute | solution.py:16
  83.6 11.7 %collective-permute-done = bf16[384,256]{0,1:T(8,128)(2,1)S(1)} collective-permute-done((bf16[384,256]{0,1:T(8,128)(2,1)S(1)}, bf16[384,256]{0,1:T(8,128)(2,1)S(1)}, u32[]{:S(2)}, u32[]{:S(2)}) %collective-permute-start) | collective-permute-done | bytes 196640 | tf_op jit(solution)/shard_map/while/body/eval_jaxpr/ppermute | solution.py:16
  95.3 8.5 %collective-permute-done.1 = bf16[384,256]{0,1:T(8,128)(2,1)S(1)} collective-permute-done((bf16[384,256]{0,1:T(8,128)(2,1)S(1)}, bf16[384,256]{0,1:T(8,128)(2,1)S(1)}, u32[]{:S(2)}, u32[]{:S(2)}) %collective-permute-start.1) | collective-permute-done | bytes 196640 | tf_op jit(solution)/shard_map/while/body/eval_jaxpr/ppermute | solution.py:16
  103.8 6.4 %while.84 = (s32[]{:T(128)}, f32[2,4,384]{2,1,0:T(4,128)S(1)}, f32[2,4,384]{2,1,0:T(4,128)S(1)}, f32[2,4,384,128]{3,2,1,0:T(8,128)S(1)}, s32[384]{0:T(512)S(1)},...) while((s32[]{:T(128)}, f32[2,4,384]{2,1,0:T(4,128)S(1)}, ...), condition=%wide.region_12.12_spmd, body=%wide.region_8.11_spmd.sunk | while | flops 205861120 | bytes 9443347 | solution.py:81
  110.3 6.9 %collective-permute-start = (bf16[384,256]{0,1:T(8,128)(2,1)S(1)}, bf16[384,256]{0,1:T(8,128)(2,1)S(1)}, u32[]{:S(2)}, u32[]{:S(2)}) collective-permute-start(bf16[384,256]{0,1:T(8,128)(2,1)S(1)} %get-tuple-element.1389), channel_id=1, source_target_pairs={{0,4},{4,8},{8,12},{12,16},{16,20},{20,24},{24,28},{1,5},{5,9},{9,... | collective-permute-start | bytes 589832 | tf_op jit(solution)/shard_map/while/body/eval_jaxpr/ppermute | solution.py:16
  117.3 5.6 %collective-permute-start.1 = (bf16[384,256]{0,1:T(8,128)(2,1)S(1)}, bf16[384,256]{0,1:T(8,128)(2,1)S(1)}, u32[]{:S(2)}, u32[]{:S(2)}) collective-permute-start(bf16[384,256]{0,1:T(8,128)(2,1)S(1)} %get-tuple-element.1390), channel_id=1, source_target_pairs={{0,4},{4,8},{8,12},{12,16},{16,20},{20,24},{24,28},{1,5},{5,9},{9,... | collective-permute-start | bytes 589832 | tf_op jit(solution)/shard_map/while/body/eval_jaxpr/ppermute | solution.py:16
  122.9 4.6 %collective-permute-done = bf16[384,256]{0,1:T(8,128)(2,1)S(1)} collective-permute-done((bf16[384,256]{0,1:T(8,128)(2,1)S(1)}, bf16[384,256]{0,1:T(8,128)(2,1)S(1)}, u32[]{:S(2)}, u32[]{:S(2)}) %collective-permute-start) | collective-permute-done | bytes 196640 | tf_op jit(solution)/shard_map/while/body/eval_jaxpr/ppermute | solution.py:16
  127.5 8.3 %collective-permute-done.1 = bf16[384,256]{0,1:T(8,128)(2,1)S(1)} collective-permute-done((bf16[384,256]{0,1:T(8,128)(2,1)S(1)}, bf16[384,256]{0,1:T(8,128)(2,1)S(1)}, u32[]{:S(2)}, u32[]{:S(2)}) %collective-permute-start.1) | collective-permute-done | bytes 196640 | tf_op jit(solution)/shard_map/while/body/eval_jaxpr/ppermute | solution.py:16
  135.8 6.4 %while.84 = (s32[]{:T(128)}, f32[2,4,384]{2,1,0:T(4,128)S(1)}, f32[2,4,384]{2,1,0:T(4,128)S(1)}, f32[2,4,384,128]{3,2,1,0:T(8,128)S(1)}, s32[384]{0:T(512)S(1)},...) while((s32[]{:T(128)}, f32[2,4,384]{2,1,0:T(4,128)S(1)}, ...), condition=%wide.region_12.12_spmd, body=%wide.region_8.11_spmd.sunk | while | flops 205861120 | bytes 9443347 | solution.py:81
  142.9 17.9 %all-gather.2.cloned.1.call-done = bf16[1024,4096]{1,0:T(8,128)(2,1)} async-done(((bf16[1024,512]{1,0:T(8,128)(2,1)}), bf16[1024,4096]{1,0:T(8,128)(2,1)}) %all-gather.2.cloned.1.call-update) | async-done | bytes 8388624 | tf_op jit(solution)/shard_map/all_gather | solution.py:106
  160.8 8.6 %convolution_convert_fusion = bf16[384,4096]{1,0:T(8,128)(2,1)} fusion(bf16[384,1024]{0,1:T(8,128)(2,1)S(1)} %bitcast.93, bf16[1024,4096]{1,0:T(8,128)(2,1)} %all-gather.2.cloned.1.call-done), kind=kOutput, calls=%fused_computation.41 | convolution fusion | flops 3222798336 | bytes 12320768 | tf_op jit(solution)/shard_map/dot_general | solution.py:104
  169.5 39.0 %reduce-scatter.2.cloned.1.call-done = bf16[384,1024]{1,0:T(8,128)(2,1)} async-done(((bf16[384,4096]{1,0:T(8,128)(2,1)}), bf16[384,1024]{1,0:T(8,128)(2,1)}) %reduce-scatter.2.cloned.1.call-update) | async-done | bytes 786448 | tf_op jit(solution)/shard_map/reduce_scatter | solution.py:109
  (207 shorter events, 46.2 us)
Async XLA Ops:
  6.5 1.7 copy-start.1
  6.5 154.3 %all-gather.2.cloned.1.call-start = ((), (), s32[]{:S(2)}) async-start(), calls=%async_computation.1 | async-start | bytes 9437184 | tf_op jit(solution)/shard_map/all_gather | solution.py:106
  7.3 201.2 %reduce-scatter.2.cloned.1.call-start = ((), (), s32[]{:S(2)}) async-start(), calls=%async_computation.2 | async-start | bytes 3932160 | tf_op jit(solution)/shard_map/reduce_scatter | solution.py:109
  8.2 0.9 copy-start.2
  12.5 1.9 copy-start
  17.4 2.2 %copy-start = (f32[2,4,384,128]{2,3,1,0:T(8,128)S(1)}, f32[2,4,384,128]{2,3,1,0:T(8,128)}, u32[]{:S(2)}) copy-start(f32[2,4,384,128]{2,3,1,0:T(8,128)} %get-tuple-element.1262) | copy-start | bytes 4718596 | tf_op jit(solution)/shard_map/while
  22.6 1.9 copy-start
  25.6 14.0 %collective-permute-start = (bf16[384,256]{0,1:T(8,128)(2,1)S(1)}, bf16[384,256]{0,1:T(8,128)(2,1)S(1)}, u32[]{:S(2)}, u32[]{:S(2)}) collective-permute-start(bf16[384,256]{0,1:T(8,128)(2,1)S(1)} %get-tuple-element.1389), channel_id=1, source_target_pairs={{0,4},{4,8},{8,12},{12,16},{16,20},{20,24},{24,28},{1,5},{5,9},{9,... | collective-permute-start | bytes 589832 | tf_op jit(solution)/shard_map/while/body/eval_jaxpr/ppermute | solution.py:16
  28.7 23.2 %collective-permute-start.1 = (bf16[384,256]{0,1:T(8,128)(2,1)S(1)}, bf16[384,256]{0,1:T(8,128)(2,1)S(1)}, u32[]{:S(2)}, u32[]{:S(2)}) collective-permute-start(bf16[384,256]{0,1:T(8,128)(2,1)S(1)} %get-tuple-element.1390), channel_id=1, source_target_pairs={{0,4},{4,8},{8,12},{12,16},{16,20},{20,24},{24,28},{1,5},{5,9},{9,... | collective-permute-start | bytes 589832 | tf_op jit(solution)/shard_map/while/body/eval_jaxpr/ppermute | solution.py:16
  58.5 8.8 %collective-permute-start = (bf16[384,256]{0,1:T(8,128)(2,1)S(1)}, bf16[384,256]{0,1:T(8,128)(2,1)S(1)}, u32[]{:S(2)}, u32[]{:S(2)}) collective-permute-start(bf16[384,256]{0,1:T(8,128)(2,1)S(1)} %get-tuple-element.1389), channel_id=1, source_target_pairs={{0,4},{4,8},{8,12},{12,16},{16,20},{20,24},{24,28},{1,5},{5,9},{9,... | collective-permute-start | bytes 589832 | tf_op jit(solution)/shard_map/while/body/eval_jaxpr/ppermute | solution.py:16
  60.4 11.1 %collective-permute-start.1 = (bf16[384,256]{0,1:T(8,128)(2,1)S(1)}, bf16[384,256]{0,1:T(8,128)(2,1)S(1)}, u32[]{:S(2)}, u32[]{:S(2)}) collective-permute-start(bf16[384,256]{0,1:T(8,128)(2,1)S(1)} %get-tuple-element.1390), channel_id=1, source_target_pairs={{0,4},{4,8},{8,12},{12,16},{16,20},{20,24},{24,28},{1,5},{5,9},{9,... | collective-permute-start | bytes 589832 | tf_op jit(solution)/shard_map/while/body/eval_jaxpr/ppermute | solution.py:16
  78.0 17.3 %collective-permute-start = (bf16[384,256]{0,1:T(8,128)(2,1)S(1)}, bf16[384,256]{0,1:T(8,128)(2,1)S(1)}, u32[]{:S(2)}, u32[]{:S(2)}) collective-permute-start(bf16[384,256]{0,1:T(8,128)(2,1)S(1)} %get-tuple-element.1389), channel_id=1, source_target_pairs={{0,4},{4,8},{8,12},{12,16},{16,20},{20,24},{24,28},{1,5},{5,9},{9,... | collective-permute-start | bytes 589832 | tf_op jit(solution)/shard_map/while/body/eval_jaxpr/ppermute | solution.py:16
  79.9 23.9 %collective-permute-start.1 = (bf16[384,256]{0,1:T(8,128)(2,1)S(1)}, bf16[384,256]{0,1:T(8,128)(2,1)S(1)}, u32[]{:S(2)}, u32[]{:S(2)}) collective-permute-start(bf16[384,256]{0,1:T(8,128)(2,1)S(1)} %get-tuple-element.1390), channel_id=1, source_target_pairs={{0,4},{4,8},{8,12},{12,16},{16,20},{20,24},{24,28},{1,5},{5,9},{9,... | collective-permute-start | bytes 589832 | tf_op jit(solution)/shard_map/while/body/eval_jaxpr/ppermute | solution.py:16
  110.3 17.1 %collective-permute-start = (bf16[384,256]{0,1:T(8,128)(2,1)S(1)}, bf16[384,256]{0,1:T(8,128)(2,1)S(1)}, u32[]{:S(2)}, u32[]{:S(2)}) collective-permute-start(bf16[384,256]{0,1:T(8,128)(2,1)S(1)} %get-tuple-element.1389), channel_id=1, source_target_pairs={{0,4},{4,8},{8,12},{12,16},{16,20},{20,24},{24,28},{1,5},{5,9},{9,... | collective-permute-start | bytes 589832 | tf_op jit(solution)/shard_map/while/body/eval_jaxpr/ppermute | solution.py:16
  117.3 18.5 %collective-permute-start.1 = (bf16[384,256]{0,1:T(8,128)(2,1)S(1)}, bf16[384,256]{0,1:T(8,128)(2,1)S(1)}, u32[]{:S(2)}, u32[]{:S(2)}) collective-permute-start(bf16[384,256]{0,1:T(8,128)(2,1)S(1)} %get-tuple-element.1390), channel_id=1, source_target_pairs={{0,4},{4,8},{8,12},{12,16},{16,20},{20,24},{24,28},{1,5},{5,9},{9,... | collective-permute-start | bytes 589832 | tf_op jit(solution)/shard_map/while/body/eval_jaxpr/ppermute | solution.py:16
Sparse Core Ops, SparseCore 0:
  9.4 151.3 all-gather.1
  169.6 38.8 reduce-scatter.1
where the time goes:
time: 217 us; the launch traced here: 215 us
  waiting for transfers between devices  119 us (55%)
  matrix products  34.7 us (16%)
  starting transfers between devices  29.5 us (14%)
  other arithmetic  14.1 us (6%)
  between operations  13.5 us (6%)
  local copies, waits for them, and re-layouts  3.36 us (2%)
    ppermute x8, waiting for transfers between devices, passed_along(): lax.ppermute(value, axis, [(source, source + steps) for source in range(f...  61.1 us
    reduce_scatter x1, waiting for transfers between devices, body(): lax.psum_scatter(terms.astype(jnp.bfloat16), 'head', scatter_dimension=1,...  39 us
    ppermute x8, starting transfers between devices, passed_along(): lax.ppermute(value, axis, [(source, source + steps) for source in range(f...  29.4 us
    all_gather x1, waiting for transfers between devices, body(): lax.all_gather(out_weight, 'tok', axis=1, tiled=True)  17.9 us
    dot_general x15, matrix products, absorb_block(): jnp.einsum('grqk,kgd->grqd', weights.astype(jnp.bfloat16), vpiece.reshape...  15.3 us
    dot_general x15, matrix products, absorb_block(): jnp.einsum('qgrd,kgd->grqk', qlocal, kpiece.reshape(count, groups, HD), p...  10.8 us
    reduce_sum x15, other arithmetic, absorb_block(): total = total * factor + jnp.sum(weights, axis=-1)  9.32 us
    dot_general x1, matrix products, body(): jnp.dot(attn, lax.all_gather(out_weight, 'tok', axis=1, tiled=True), pref...  8.61 us
  transfers between devices with their start and end apart: 10, of which 10 were waited for; matrix products, arithmetic and copies ran while one was open for 20% of the time, Pallas kernels for 0%

commit v1 on v0

v1 whole, which is shorter than its diff:
```python
import functools
import math

import jax
import jax.numpy as jnp
from jax import lax
from jax.experimental import pallas as pl
from jax.experimental.pallas import tpu as pltpu
from jax.sharding import PartitionSpec as P

QH = 32
KVH = 8
HD = 128
RATIO = QH // KVH
SCALE = 1.0 / HD**0.5
LOW = -1e30


def doc_ends(lengths):
    order = jnp.arange(lengths.shape[0], dtype=jnp.int32)
    return jnp.sum(jnp.where(order[None, :] <= order[:, None], lengths[None, :], 0), axis=1)


def doc_starts(lengths, positions):
    ends = doc_ends(lengths)[None, :]
    return jnp.max(jnp.where(ends <= positions[:, None], ends, 0), axis=1)


def attend_kernel(count, own, resume, last, bases, q_ref, start_ref, *refs):
    keys, vals = refs[:count], refs[count : 2 * count]
    refs = refs[2 * count :]
    if resume:
        acc_in, top_in = refs[:2]
        refs = refs[2:]
    query = q_ref[...]
    start = start_ref[...]
    rows = query.shape[0]
    factor = SCALE * math.log2(math.e)
    scores = []
    top = top_in[:, :1] if resume else None
    for i in range(count):
        s = lax.dot_general(
            query, keys[i][...], (((1,), (1,)), ((), ())), preferred_element_type=jnp.float32
        )
        column = lax.broadcasted_iota(jnp.int32, s.shape, 1)
        allowed = column >= start - bases[i]
        if own and i == 0:
            allowed = allowed & (column <= lax.broadcasted_iota(jnp.int32, s.shape, 0))
        s = jnp.where(allowed, s, LOW)
        high = jnp.max(s, axis=1, keepdims=True)
        top = high if top is None else jnp.maximum(top, high)
        scores.append(s)
    acc = None
    for i in range(count):
        weights = jnp.exp2((scores[i] - top) * factor).astype(jnp.bfloat16)
        value = vals[i][...]
        wide = jnp.concatenate([value, jnp.ones_like(value)], axis=1)
        part = jnp.dot(weights, wide, preferred_element_type=jnp.float32)
        acc = part if acc is None else acc + part
    if resume:
        acc = acc + acc_in[...] * jnp.exp2((top_in[:, :1] - top) * factor)
    if last:
        out_ref = refs[0]
        out_ref[...] = (acc[:, :HD] / acc[:, HD:]).astype(out_ref.dtype)
    else:
        acc_out, top_out = refs
        acc_out[...] = acc
        top_out[...] = jnp.broadcast_to(top, (rows, HD))


def attend(queries, start, pieces, bases, own, state, last):
    rows, width = queries.shape
    heads = width // HD
    groups = heads // RATIO
    count = len(pieces)
    resume = state is not None
    specs = [
        pl.BlockSpec((rows, HD), lambda h, b: (0, h)),
        pl.BlockSpec((rows, 1), lambda h, b: (0, 0)),
    ]
    specs += [pl.BlockSpec((p.shape[0], HD), lambda h, b: (0, h // RATIO)) for p in pieces]
    specs += [
        pl.BlockSpec((p.shape[0], HD), lambda h, b, g=groups: (0, g + h // RATIO)) for p in pieces
    ]
    state_specs = [
        pl.BlockSpec((rows, 2 * HD), lambda h, b: (0, h)),
        pl.BlockSpec((rows, HD), lambda h, b: (0, h)),
    ]
    if resume:
        specs += state_specs
    if last:
        out_shape = jax.ShapeDtypeStruct((rows, width), jnp.bfloat16)
        out_specs = pl.BlockSpec((rows, HD), lambda h, b: (0, h))
    else:
        out_shape = (
            jax.ShapeDtypeStruct((rows, 2 * width), jnp.float32),
            jax.ShapeDtypeStruct((rows, width), jnp.float32),
        )
        out_specs = tuple(state_specs)
    seen = sum(p.shape[0] for p in pieces)
    return pl.pallas_call(
        functools.partial(attend_kernel, count, own, resume, last),
        grid_spec=pltpu.PrefetchScalarGridSpec(
            num_scalar_prefetch=1,
            grid=(heads,),
            in_specs=specs,
            out_specs=out_specs,
        ),
        out_shape=out_shape,
        compiler_params=pltpu.CompilerParams(vmem_limit_bytes=40 * 2**20),
        cost_estimate=pl.CostEstimate(
            flops=6 * rows * seen * width,
            bytes_accessed=4 * rows * width,
            transcendentals=rows * seen * heads,
        ),
    )(bases, queries, start, *pieces, *pieces, *(state or ()))


def moved(value, axes, sizes, where):
    count, heads = sizes
    pairs = []
    for t in range(count):
        for h in range(heads):
            target = where(t, h)
            if target is not None:
                pairs.append((t * heads + h, target[0] * heads + target[1]))
    return lax.ppermute(value, axes, pairs)


def paired_body(queries, keys, values, lengths, out_weight):
    rows, width = queries.shape
    axes = ("tok", "head")
    sizes = count, heads = (lax.axis_size("tok"), lax.axis_size("head"))
    tok, head = lax.axis_index("tok"), lax.axis_index("head")
    side, level = tok % 2, tok // 2
    parity, core, half = level % 2, head % 2, head // 2
    send = functools.partial(moved, axes=axes, sizes=sizes)

    own = jnp.concatenate([keys, values], axis=1)
    back2 = send(own, where=lambda t, h: (t + 2, h) if t + 2 < count else None)
    weight_side = send(out_weight, where=lambda t, h: (t ^ 1, h))
    back4 = send(back2, where=lambda t, h: (t + 2, h) if t + 2 < count else None)
    back2_side = send(back2, where=lambda t, h: (t ^ 1, h))
    rest = jnp.where(side == 0, own, back4)
    rest = send(rest, where=lambda t, h: (t ^ 1, h))
    weight_far = send(out_weight, where=lambda t, h: (t ^ 4, h))
    weight_far_side = send(weight_far, where=lambda t, h: (t ^ 1, h))

    qpos = tok * rows + jnp.arange(rows, dtype=jnp.int32)
    start = doc_starts(lengths, qpos)[:, None]
    shift = lambda k: (tok - k) * rows
    near = jnp.stack([shift(0), shift(2), shift(2) + rows * (1 - 2 * side)])
    far = jnp.stack([shift(4), jnp.where(side == 0, shift(3), shift(1))])
    state = attend(queries, start, [own, back2, back2_side], near, True, None, False)
    attn = attend(queries, start, [back4, rest], far, False, state, True)
    attn_pair = send(attn, where=lambda t, h: (t ^ 2, h))

    mine = core == parity
    keep_rows = jnp.where(mine, attn, attn_pair)
    send_rows = jnp.where(mine, attn_pair, attn)

    def unit(weight, far_off):
        keeper = lambda t: (t // 4) ^ (1 if far_off else 0)
        keep = jnp.dot(keep_rows, weight, preferred_element_type=jnp.float32)
        away = jnp.dot(send_rows, weight, preferred_element_type=jnp.float32).astype(jnp.bfloat16)
        summed = keep + send(away, where=lambda t, h: (t, h ^ 1))
        low = summed.astype(jnp.bfloat16)
        got = send(low, where=lambda t, h: (t, h ^ 2) if (h // 2) != keeper(t) else None)
        total = (summed + got).astype(jnp.bfloat16)
        over = send(
            total,
            where=lambda t, h: (t ^ 2, h ^ 1)
            if (h // 2) == keeper(t) and (h % 2) != (t // 2) % 2
            else None,
        )
        return jnp.where(mine, total, over)

    near_same = unit(out_weight, False)
    near_side = unit(weight_side, False)
    far_same = unit(weight_far, True)
    far_side = unit(weight_far_side, True)
    is_near = half == level // 2
    same = jnp.where(is_near, near_same, far_same)
    other = jnp.where(is_near, near_side, far_side)
    return jnp.where(
        side == 0,
        jnp.concatenate([same, other], axis=1),
        jnp.concatenate([other, same], axis=1),
    )


def ring_body(queries, keys, values, lengths, out_weight):
    rows = queries.shape[0]
    count = lax.axis_size("tok")
    tok = lax.axis_index("tok")
    qpos = tok * rows + jnp.arange(rows, dtype=jnp.int32)
    start = doc_starts(lengths, qpos)[:, None]
    piece = jnp.concatenate([keys, values], axis=1)
    state = attend(queries, start, [piece], (tok * rows)[None], True, None, False)

    def advance(step, carried):
        piece, state = carried
        piece = lax.ppermute(piece, "tok", [(i, i + 1) for i in range(count - 1)])
        state = attend(queries, start, [piece], ((tok - step) * rows)[None], False, state, False)
        return piece, state

    piece, (acc, _) = lax.fori_loop(1, count // 2 + 1, advance, (piece, state))
    acc = acc.reshape(rows, -1, 2, HD)
    attn = (acc[:, :, 0] / acc[:, :, 1]).reshape(rows, -1).astype(jnp.bfloat16)
    terms = jnp.dot(
        attn,
        lax.all_gather(out_weight, "tok", axis=1, tiled=True),
        preferred_element_type=jnp.float32,
    )
    return lax.psum_scatter(terms.astype(jnp.bfloat16), "head", scatter_dimension=1, tiled=True)


def solution(mesh):
    count, heads = mesh.shape["tok"], mesh.shape["head"]
    body = paired_body if (count, heads) == (8, 4) else ring_body
    placed = (P("tok", "head"), P("tok", "head"), P("tok", "head"), P(), P("head", "tok"))
    return jax.shard_map(
        body, mesh=mesh, in_specs=placed, out_specs=P("tok", "head"), check_vma=False
    )
```

time: 217 us -> 146 us (0.67)
  waiting for transfers between devices: 119 us -> 49.8 us
  starting transfers between devices: 29.5 us -> 57.5 us
  matrix products: 34.7 us -> 9.51 us
  Pallas kernels: 0 us -> 23.1 us
  between operations: 13.5 us -> 0.36 us
  other arithmetic: 14.1 us -> 3.63 us
    reduce_scatter x1 -> x0, waiting for transfers between devices: 39 us -> none  [body(): lax.psum_scatter(terms.astype(jnp.bfloat16), 'head', scatter_dimension=1,...]
    ppermute x8 -> x20, starting transfers between devices: 29.4 us -> 57.5 us  [moved(): return lax.ppermute(value, axes, pairs)]
    dot_general x31 -> x8, matrix products: 34.7 us -> 9.51 us  [the longest x4 4.77 us: unit(): keep = jnp.dot(keep_rows, weight, preferred_element_type=jnp.float32)]
    pallas_call x0 -> x2, Pallas kernels: none -> 23.1 us  [attend(): pl.pallas_call(functools.partial(attend_kernel, count, own, resume, last)...]
    all_gather x1 -> x0, waiting for transfers between devices: 17.9 us -> none  [body(): lax.all_gather(out_weight, 'tok', axis=1, tiled=True)]
    ppermute x8 -> x20, waiting for transfers between devices: 61.1 us -> 49.8 us  [moved(): return lax.ppermute(value, axes, pairs)]
    reduce_sum x31 -> x1, other arithmetic: 10.7 us -> 0.77 us  [doc_ends(): jnp.sum(jnp.where(order[None, :] <= order[:, None], lengths[None, :], 0),...]
  transfers between devices with their start and end apart: 10 -> 20, of which waited for: 10 -> 6; matrix products, arithmetic and copies ran while one was open for 20% -> 8% of each run, Pallas kernels for 0% -> 16%
where the time goes in v1:
time: 146 us
  starting transfers between devices  57.5 us (39%)
  waiting for transfers between devices  49.8 us (34%)
  Pallas kernels  23.1 us (16%)
  matrix products  9.51 us (7%)
  other arithmetic  3.63 us (2%)
  local copies, waits for them, and re-layouts  2.06 us (1%)
    ppermute x20, starting transfers between devices, moved(): return lax.ppermute(value, axes, pairs)  57.5 us
    ppermute x20, waiting for transfers between devices, moved(): return lax.ppermute(value, axes, pairs)  49.8 us
    pallas_call x2, Pallas kernels, attend(): pl.pallas_call(functools.partial(attend_kernel, count, own, resume, last)...  23.1 us
    dot_general x4, matrix products, unit(): keep = jnp.dot(keep_rows, weight, preferred_element_type=jnp.float32)  4.77 us
    dot_general x4, matrix products, unit(): jnp.dot(send_rows, weight, preferred_element_type=jnp.float32)  4.74 us
  transfers between devices with their start and end apart: 20, of which 6 were waited for; matrix products, arithmetic and copies ran while one was open for 8% of the time, Pallas kernels for 16%

profile of v1, /device:TPU:17, one launch (start us, length us, event | category | flops | bytes accessed | tf_op | source)
XLA Modules:
  0.0 145.9 jit_solution(4758036553390963834)
XLA Ops:
  2.0 3.2 %collective-permute-start = (bf16[384,512]{1,0:T(8,128)(2,1)S(1)}, bf16[384,512]{1,0:T(8,128)(2,1)S(1)}, u32[]{:S(2)}, u32[]{:S(2)}) collective-permute-start(bf16[384,512]{1,0:T(8,128)(2,1)S(1)} %constant_dynamic-update-slice_fusion.refs_0_.refs_3_), channel_id=1, source_target_pairs={{0,8},{1,9},{2,10},{3,11},{4,12},{5,13},{6,14},{7,15},{8,16},{9,17... | collective-permute-start | bytes 1179656 | tf_op jit(solution)/shard_map/ppermute | solution.py:127
  5.2 8.7 %collective-permute-done.refs_1_.refs_4_ = bf16[384,512]{1,0:T(8,128)(2,1)S(1)} collective-permute-done((bf16[384,512]{1,0:T(8,128)(2,1)S(1)}, bf16[384,512]{1,0:T(8,128)(2,1)S(1)}, u32[]{:S(2)}, u32[]{:S(2)}) %collective-permute-start) | collective-permute-done | bytes 393248 | tf_op jit(solution)/shard_map/ppermute | solution.py:127
  13.8 3.2 %collective-permute-start.1 = (bf16[384,512]{1,0:T(8,128)(2,1)S(1)}, bf16[384,512]{1,0:T(8,128)(2,1)S(1)}, u32[]{:S(2)}, u32[]{:S(2)}) collective-permute-start(bf16[384,512]{1,0:T(8,128)(2,1)S(1)} %collective-permute-done.refs_1_.refs_4_), channel_id=1, source_target_pairs={{0,8},{1,9},{2,10},{3,11},{4,12},{5,13},{6,14},{7,15},{8,16},{9,17... | collective-permute-start | bytes 1179656 | tf_op jit(solution)/shard_map/ppermute | solution.py:127
  18.0 1.3 collective-permute-start.3
  19.3 5.6 %collective-permute-done.1.refs_0_.refs_2_ = bf16[384,512]{1,0:T(8,128)(2,1)S(1)} collective-permute-done((bf16[384,512]{1,0:T(8,128)(2,1)S(1)}, bf16[384,512]{1,0:T(8,128)(2,1)S(1)}, u32[]{:S(2)}, u32[]{:S(2)}) %collective-permute-start.1) | collective-permute-done | bytes 393248 | tf_op jit(solution)/shard_map/ppermute | solution.py:127
  27.2 11.7 %shard_map.55 = (f32[384,2048]{1,0:T(8,128)S(1)}, f32[384,1024]{1,0:T(8,128)S(1)}) custom-call(s32[3]{0:T(128)S(1)} %pad_add_fusion.1.bases, bf16[384,1024]{1,0:T(8,128)(2,1)S(1)} %copy-done, s32[384,1]{1,0:T(8,128)S(1)} %broadcast_in_dim.34.start_ref, bf16[384,512]{1,0:T(8,128)(2,1)S(1)} %constant_dynamic-update-slice_fusion.refs_0_.refs_3_, ...), custom_call_target="tpu_custom_call" | custom-call | flops 2717908992 | bytes 1572864 | tf_op jit(solution)/shard_map/pallas_call | solution.py:101
  38.9 11.4 %shard_map.56 = bf16[384,1024]{1,0:T(8,128)(2,1)S(1)} custom-call(s32[2]{0:T(128)S(1)} %pad_add_fusion.bases, bf16[384,1024]{1,0:T(8,128)(2,1)S(1)} %copy-done, s32[384,1]{1,0:T(8,128)S(1)} %broadcast_in_dim.34.start_ref, bf16[384,512]{1,0:T(8,128)(2,1)S(1)} %collective-permute-done.1.refs_0_.refs_2_, ...), custom_call_target="tpu_custom_call" | custom-call | flops 1811939328 | bytes 1572864 | tf_op jit(solution)/shard_map/pallas_call | solution.py:101
  50.3 1.2 collective-permute-start.4
  52.3 9.5 %collective-permute-done.8 = bf16[1024,512]{1,0:T(8,128)(2,1)} collective-permute-done((bf16[1024,512]{1,0:T(8,128)(2,1)}, bf16[1024,512]{1,0:T(8,128)(2,1)}, u32[]{:S(2)}, u32[]{:S(2)}) %collective-permute-start.8) | collective-permute-done | bytes 1048608 | tf_op jit(solution)/shard_map/ppermute | solution.py:127
  63.0 17.1 %collective-permute-done.4 = bf16[384,1024]{1,0:T(8,128)(2,1)S(1)} collective-permute-done((bf16[384,1024]{1,0:T(8,128)(2,1)S(1)}, bf16[384,1024]{1,0:T(8,128)(2,1)S(1)}, u32[]{:S(2)}, u32[]{:S(2)}) %collective-permute-start.4) | collective-permute-done | bytes 786464 | tf_op jit(solution)/shard_map/ppermute | solution.py:127
  80.2 1.8 %convolution_convert_fusion.3 = bf16[384,512]{1,0:T(8,128)(2,1)S(1)} fusion(bf16[384,1024]{1,0:T(8,128)(2,1)S(1)} %get-tuple-element.9, bf16[1024,512]{1,0:T(8,128)(2,1)} %param.9), kind=kOutput, calls=%fused_computation.7 | convolution fusion | flops 402849792 | bytes 2228224 | tf_op jit(solution)/shard_map/dot_general | solution.py:165
  82.0 9.5 %collective-permute-start.5 = (bf16[384,512]{1,0:T(8,128)(2,1)S(1)}, bf16[384,512]{1,0:T(8,128)(2,1)S(1)}, u32[]{:S(2)}, u32[]{:S(2)}) collective-permute-start(bf16[384,512]{1,0:T(8,128)(2,1)S(1)} %convolution_convert_fusion.3), channel_id=1, source_target_pairs={{0,1},{1,0},{2,3},{3,2},{4,5},{5,4},{6,7},{7,6},{8,9},{9,8},{10,11... | collective-permute-start | bytes 1179656 | tf_op jit(solution)/shard_map/ppermute | solution.py:127
  91.5 1.8 %convolution_convert_fusion.2 = bf16[384,512]{1,0:T(8,128)(2,1)S(1)} fusion(bf16[384,1024]{1,0:T(8,128)(2,1)S(1)} %get-tuple-element.9, bf16[1024,512]{1,0:T(8,128)(2,1)} %collective-permute-done.8), kind=kOutput, calls=%fused_computation.6 | convolution fusion | flops 402849792 | bytes 2228224 | tf_op jit(solution)/shard_map/dot_general | solution.py:165
  95.1 9.5 %collective-permute-start.17 = (bf16[384,512]{1,0:T(8,128)(2,1)S(1)}, bf16[384,512]{1,0:T(8,128)(2,1)S(1)}, u32[]{:S(2)}, u32[]{:S(2)}) collective-permute-start(bf16[384,512]{1,0:T(8,128)(2,1)S(1)} %convolution_convert_fusion), channel_id=1, source_target_pairs={{0,1},{1,0},{2,3},{3,2},{4,5},{5,4},{6,7},{7,6},{8,9},{9,8},{10,11... | collective-permute-start | bytes 1179656 | tf_op jit(solution)/shard_map/ppermute | solution.py:127
  104.6 1.8 %fusion.3 = (bf16[384,512]{1,0:T(8,128)(2,1)S(1)}, f32[384,512]{1,0:T(8,128)S(1)}) fusion(bf16[384,512]{1,0:T(8,128)(2,1)S(1)} %collective-permute-done.5, bf16[384,1024]{1,0:T(8,128)(2,1)S(1)} %get-tuple-element.10, bf16[1024,512]{1,0:T(8,128)(2,1)} %param.9), kind=kOutput, calls=%fused_computation.29 | convolution fusion | flops 403243008 | bytes 3407872 | tf_op jit(solution)/shard_map/dot_general | solution.py:164
  106.5 3.2 %collective-permute-start.6 = (bf16[384,512]{1,0:T(8,128)(2,1)S(1)}, bf16[384,512]{1,0:T(8,128)(2,1)S(1)}, u32[]{:S(2)}, u32[]{:S(2)}) collective-permute-start(bf16[384,512]{1,0:T(8,128)(2,1)S(1)} %get-tuple-element.17), channel_id=1, source_target_pairs={{2,0},{3,1},{6,4},{7,5},{10,8},{11,9},{14,12},{15,13},{16,18},{17,... | collective-permute-start | bytes 1179656 | tf_op jit(solution)/shard_map/ppermute | solution.py:127
  109.6 1.8 %fusion.2 = (bf16[384,512]{1,0:T(8,128)(2,1)S(1)}, f32[384,512]{1,0:T(8,128)S(1)}) fusion(bf16[384,512]{1,0:T(8,128)(2,1)S(1)} %collective-permute-done.9, bf16[384,1024]{1,0:T(8,128)(2,1)S(1)} %get-tuple-element.10, bf16[1024,512]{1,0:T(8,128)(2,1)} %collective-permute-done.8), kind=kOutput, calls=%fused_computation.28 | convolution fusion | flops 403243008 | bytes 3407872 | tf_op jit(solution)/shard_map/dot_general | solution.py:164
  111.5 1.3 collective-permute-start.10
  113.4 4.0 %collective-permute-start.14 = (bf16[384,512]{1,0:T(8,128)(2,1)S(1)}, bf16[384,512]{1,0:T(8,128)(2,1)S(1)}, u32[]{:S(2)}, u32[]{:S(2)}) collective-permute-start(bf16[384,512]{1,0:T(8,128)(2,1)S(1)} %get-tuple-element.13), channel_id=1, source_target_pairs={{2,0},{3,1},{6,4},{7,5},{10,8},{11,9},{14,12},{15,13},{16,18},{17,... | collective-permute-start | bytes 1179656 | tf_op jit(solution)/shard_map/ppermute | solution.py:127
  118.0 1.3 collective-permute-start.18
  120.1 3.6 %collective-permute-done.10 = bf16[384,512]{1,0:T(8,128)(2,1)S(1)} collective-permute-done((bf16[384,512]{1,0:T(8,128)(2,1)S(1)}, bf16[384,512]{1,0:T(8,128)(2,1)S(1)}, u32[]{:S(2)}, u32[]{:S(2)}) %collective-permute-start.10) | collective-permute-done | bytes 393248 | tf_op jit(solution)/shard_map/ppermute | solution.py:127
  123.9 7.7 %collective-permute-start.11 = (bf16[384,512]{1,0:T(8,128)(2,1)S(1)}, bf16[384,512]{1,0:T(8,128)(2,1)S(1)}, u32[]{:S(2)}, u32[]{:S(2)}) collective-permute-start(bf16[384,512]{1,0:T(8,128)(2,1)S(1)} %add_convert_fusion.2), channel_id=1, source_target_pairs={{3,10},{7,14},{10,3},{14,7},{17,24},{21,28},{24,17},{28,21}} | collective-permute-start | bytes 1179656 | tf_op jit(solution)/shard_map/ppermute | solution.py:127
  132.6 6.7 %collective-permute-start.19 = (bf16[384,512]{1,0:T(8,128)(2,1)S(1)}, bf16[384,512]{1,0:T(8,128)(2,1)S(1)}, u32[]{:S(2)}, u32[]{:S(2)}) collective-permute-start(bf16[384,512]{1,0:T(8,128)(2,1)S(1)} %add_convert_fusion), channel_id=1, source_target_pairs={{3,10},{7,14},{10,3},{14,7},{17,24},{21,28},{24,17},{28,21}} | collective-permute-start | bytes 1179656 | tf_op jit(solution)/shard_map/ppermute | solution.py:127
  139.5 5.3 %collective-permute-done.19 = bf16[384,512]{1,0:T(8,128)(2,1)S(1)} collective-permute-done((bf16[384,512]{1,0:T(8,128)(2,1)S(1)}, bf16[384,512]{1,0:T(8,128)(2,1)S(1)}, u32[]{:S(2)}, u32[]{:S(2)}) %collective-permute-start.19) | collective-permute-done | bytes 393248 | tf_op jit(solution)/shard_map/ppermute | solution.py:127
  (45 shorter events, 13.4 us)
Async XLA Ops:
  0.0 27.2 %copy-start = (bf16[384,1024]{1,0:T(8,128)(2,1)S(1)}, bf16[384,1024]{1,0:T(8,128)(2,1)}, u32[]{:S(2)}) copy-start(bf16[384,1024]{1,0:T(8,128)(2,1)} %q_ref.3) | copy-start | bytes 2359300
  2.0 11.9 %collective-permute-start = (bf16[384,512]{1,0:T(8,128)(2,1)S(1)}, bf16[384,512]{1,0:T(8,128)(2,1)S(1)}, u32[]{:S(2)}, u32[]{:S(2)}) collective-permute-start(bf16[384,512]{1,0:T(8,128)(2,1)S(1)} %constant_dynamic-update-slice_fusion.refs_0_.refs_3_), channel_id=1, source_target_pairs={{0,8},{1,9},{2,10},{3,11},{4,12},{5,13},{6,14},{7,15},{8,16},{9,17... | collective-permute-start | bytes 1179656 | tf_op jit(solution)/shard_map/ppermute | solution.py:127
  13.8 11.0 %collective-permute-start.1 = (bf16[384,512]{1,0:T(8,128)(2,1)S(1)}, bf16[384,512]{1,0:T(8,128)(2,1)S(1)}, u32[]{:S(2)}, u32[]{:S(2)}) collective-permute-start(bf16[384,512]{1,0:T(8,128)(2,1)S(1)} %collective-permute-done.refs_1_.refs_4_), channel_id=1, source_target_pairs={{0,8},{1,9},{2,10},{3,11},{4,12},{5,13},{6,14},{7,15},{8,16},{9,17... | collective-permute-start | bytes 1179656 | tf_op jit(solution)/shard_map/ppermute | solution.py:127
  17.0 44.8 %collective-permute-start.8 = (bf16[1024,512]{1,0:T(8,128)(2,1)}, bf16[1024,512]{1,0:T(8,128)(2,1)}, u32[]{:S(2)}, u32[]{:S(2)}) collective-permute-start(bf16[1024,512]{1,0:T(8,128)(2,1)} %param.9), channel_id=1, source_target_pairs={{0,16},{1,17},{2,18},{3,19},{4,20},{5,21},{6,22},{7,23},{8,24},{9,... | collective-permute-start | bytes 3145736 | tf_op jit(solution)/shard_map/ppermute | solution.py:127
  18.0 9.1 %collective-permute-start.3 = (bf16[384,512]{1,0:T(8,128)(2,1)S(1)}, bf16[384,512]{1,0:T(8,128)(2,1)S(1)}, u32[]{:S(2)}, u32[]{:S(2)}) collective-permute-start(bf16[384,512]{1,0:T(8,128)(2,1)S(1)} %collective-permute-done.refs_1_.refs_4_), channel_id=1, source_target_pairs={{0,4},{1,5},{2,6},{3,7},{4,0},{5,1},{6,2},{7,3},{8,12},{9,13},{10,... | collective-permute-start | bytes 1179656 | tf_op jit(solution)/shard_map/ppermute | solution.py:127
  25.7 13.2 %collective-permute-start.2 = (bf16[384,512]{1,0:T(8,128)(2,1)}, bf16[384,512]{1,0:T(8,128)(2,1)S(1)}, u32[]{:S(2)}, u32[]{:S(2)}) collective-permute-start(bf16[384,512]{1,0:T(8,128)(2,1)} %broadcast_select_fusion.2), channel_id=1, source_target_pairs={{0,4},{1,5},{2,6},{3,7},{4,0},{5,1},{6,2},{7,3},{8,12},{9,13},{10,... | collective-permute-start | bytes 1179656 | tf_op jit(solution)/shard_map/ppermute | solution.py:127
  50.3 29.9 %collective-permute-start.4 = (bf16[384,1024]{1,0:T(8,128)(2,1)S(1)}, bf16[384,1024]{1,0:T(8,128)(2,1)S(1)}, u32[]{:S(2)}, u32[]{:S(2)}) collective-permute-start(bf16[384,1024]{1,0:T(8,128)(2,1)S(1)} %shard_map.56), channel_id=1, source_target_pairs={{0,8},{1,9},{2,10},{3,11},{4,12},{5,13},{6,14},{7,15},{8,0},{9,1},... | collective-permute-start | bytes 2359304 | tf_op jit(solution)/shard_map/ppermute | solution.py:127
  51.5 41.9 %collective-permute-start.12 = (bf16[1024,512]{1,0:T(8,128)(2,1)}, bf16[1024,512]{1,0:T(8,128)(2,1)S(1)}, u32[]{:S(2)}, u32[]{:S(2)}) collective-permute-start(bf16[1024,512]{1,0:T(8,128)(2,1)} %param.9), channel_id=1, source_target_pairs={{0,4},{1,5},{2,6},{3,7},{4,0},{5,1},{6,2},{7,3},{8,12},{9,13},{10,... | collective-permute-start | bytes 3145736 | tf_op jit(solution)/shard_map/ppermute | solution.py:127
  61.8 32.7 %collective-permute-start.16 = (bf16[1024,512]{1,0:T(8,128)(2,1)}, bf16[1024,512]{1,0:T(8,128)(2,1)S(1)}, u32[]{:S(2)}, u32[]{:S(2)}) collective-permute-start(bf16[1024,512]{1,0:T(8,128)(2,1)} %collective-permute-done.8), channel_id=1, source_target_pairs={{0,4},{1,5},{2,6},{3,7},{4,0},{5,1},{6,2},{7,3},{8,12},{9,13},{10,... | collective-permute-start | bytes 3145736 | tf_op jit(solution)/shard_map/ppermute | solution.py:127
  82.0 22.6 %collective-permute-start.5 = (bf16[384,512]{1,0:T(8,128)(2,1)S(1)}, bf16[384,512]{1,0:T(8,128)(2,1)S(1)}, u32[]{:S(2)}, u32[]{:S(2)}) collective-permute-start(bf16[384,512]{1,0:T(8,128)(2,1)S(1)} %convolution_convert_fusion.3), channel_id=1, source_target_pairs={{0,1},{1,0},{2,3},{3,2},{4,5},{5,4},{6,7},{7,6},{8,9},{9,8},{10,11... | collective-permute-start | bytes 1179656 | tf_op jit(solution)/shard_map/ppermute | solution.py:127
  93.3 16.3 %collective-permute-start.9 = (bf16[384,512]{1,0:T(8,128)(2,1)S(1)}, bf16[384,512]{1,0:T(8,128)(2,1)S(1)}, u32[]{:S(2)}, u32[]{:S(2)}) collective-permute-start(bf16[384,512]{1,0:T(8,128)(2,1)S(1)} %convolution_convert_fusion.2), channel_id=1, source_target_pairs={{0,1},{1,0},{2,3},{3,2},{4,5},{5,4},{6,7},{7,6},{8,9},{9,8},{10,11... | collective-permute-start | bytes 1179656 | tf_op jit(solution)/shard_map/ppermute | solution.py:127
  94.0 18.8 %collective-permute-start.13 = (bf16[384,512]{1,0:T(8,128)(2,1)S(1)}, bf16[384,512]{1,0:T(8,128)(2,1)S(1)}, u32[]{:S(2)}, u32[]{:S(2)}) collective-permute-start(bf16[384,512]{1,0:T(8,128)(2,1)S(1)} %convolution_convert_fusion.1), channel_id=1, source_target_pairs={{0,1},{1,0},{2,3},{3,2},{4,5},{5,4},{6,7},{7,6},{8,9},{9,8},{10,11... | collective-permute-start | bytes 1179656 | tf_op jit(solution)/shard_map/ppermute | solution.py:127
  95.1 22.3 %collective-permute-start.17 = (bf16[384,512]{1,0:T(8,128)(2,1)S(1)}, bf16[384,512]{1,0:T(8,128)(2,1)S(1)}, u32[]{:S(2)}, u32[]{:S(2)}) collective-permute-start(bf16[384,512]{1,0:T(8,128)(2,1)S(1)} %convolution_convert_fusion), channel_id=1, source_target_pairs={{0,1},{1,0},{2,3},{3,2},{4,5},{5,4},{6,7},{7,6},{8,9},{9,8},{10,11... | collective-permute-start | bytes 1179656 | tf_op jit(solution)/shard_map/ppermute | solution.py:127
  106.5 12.8 %collective-permute-start.6 = (bf16[384,512]{1,0:T(8,128)(2,1)S(1)}, bf16[384,512]{1,0:T(8,128)(2,1)S(1)}, u32[]{:S(2)}, u32[]{:S(2)}) collective-permute-start(bf16[384,512]{1,0:T(8,128)(2,1)S(1)} %get-tuple-element.17), channel_id=1, source_target_pairs={{2,0},{3,1},{6,4},{7,5},{10,8},{11,9},{14,12},{15,13},{16,18},{17,... | collective-permute-start | bytes 1179656 | tf_op jit(solution)/shard_map/ppermute | solution.py:127
  111.5 12.3 %collective-permute-start.10 = (bf16[384,512]{1,0:T(8,128)(2,1)S(1)}, bf16[384,512]{1,0:T(8,128)(2,1)S(1)}, u32[]{:S(2)}, u32[]{:S(2)}) collective-permute-start(bf16[384,512]{1,0:T(8,128)(2,1)S(1)} %get-tuple-element.15), channel_id=1, source_target_pairs={{0,2},{1,3},{4,6},{5,7},{8,10},{9,11},{12,14},{13,15},{18,16},{19,... | collective-permute-start | bytes 1179656 | tf_op jit(solution)/shard_map/ppermute | solution.py:127
  113.4 18.3 %collective-permute-start.14 = (bf16[384,512]{1,0:T(8,128)(2,1)S(1)}, bf16[384,512]{1,0:T(8,128)(2,1)S(1)}, u32[]{:S(2)}, u32[]{:S(2)}) collective-permute-start(bf16[384,512]{1,0:T(8,128)(2,1)S(1)} %get-tuple-element.13), channel_id=1, source_target_pairs={{2,0},{3,1},{6,4},{7,5},{10,8},{11,9},{14,12},{15,13},{16,18},{17,... | collective-permute-start | bytes 1179656 | tf_op jit(solution)/shard_map/ppermute | solution.py:127
  118.0 14.5 %collective-permute-start.18 = (bf16[384,512]{1,0:T(8,128)(2,1)S(1)}, bf16[384,512]{1,0:T(8,128)(2,1)S(1)}, u32[]{:S(2)}, u32[]{:S(2)}) collective-permute-start(bf16[384,512]{1,0:T(8,128)(2,1)S(1)} %get-tuple-element.11), channel_id=1, source_target_pairs={{0,2},{1,3},{4,6},{5,7},{8,10},{9,11},{12,14},{13,15},{18,16},{19,... | collective-permute-start | bytes 1179656 | tf_op jit(solution)/shard_map/ppermute | solution.py:127
  119.4 19.9 %collective-permute-start.7 = (bf16[384,512]{1,0:T(8,128)(2,1)S(1)}, bf16[384,512]{1,0:T(8,128)(2,1)S(1)}, u32[]{:S(2)}, u32[]{:S(2)}) collective-permute-start(bf16[384,512]{1,0:T(8,128)(2,1)S(1)} %add_convert_fusion.3), channel_id=1, source_target_pairs={{1,8},{5,12},{8,1},{12,5},{19,26},{23,30},{26,19},{30,23}} | collective-permute-start | bytes 1179656 | tf_op jit(solution)/shard_map/ppermute | solution.py:127
  123.9 15.5 %collective-permute-start.11 = (bf16[384,512]{1,0:T(8,128)(2,1)S(1)}, bf16[384,512]{1,0:T(8,128)(2,1)S(1)}, u32[]{:S(2)}, u32[]{:S(2)}) collective-permute-start(bf16[384,512]{1,0:T(8,128)(2,1)S(1)} %add_convert_fusion.2), channel_id=1, source_target_pairs={{3,10},{7,14},{10,3},{14,7},{17,24},{21,28},{24,17},{28,21}} | collective-permute-start | bytes 1179656 | tf_op jit(solution)/shard_map/ppermute | solution.py:127
  131.8 7.7 %collective-permute-start.15 = (bf16[384,512]{1,0:T(8,128)(2,1)S(1)}, bf16[384,512]{1,0:T(8,128)(2,1)S(1)}, u32[]{:S(2)}, u32[]{:S(2)}) collective-permute-start(bf16[384,512]{1,0:T(8,128)(2,1)S(1)} %add_convert_fusion.1), channel_id=1, source_target_pairs={{1,8},{5,12},{8,1},{12,5},{19,26},{23,30},{26,19},{30,23}} | collective-permute-start | bytes 1179656 | tf_op jit(solution)/shard_map/ppermute | solution.py:127
  132.6 12.2 %collective-permute-start.19 = (bf16[384,512]{1,0:T(8,128)(2,1)S(1)}, bf16[384,512]{1,0:T(8,128)(2,1)S(1)}, u32[]{:S(2)}, u32[]{:S(2)}) collective-permute-start(bf16[384,512]{1,0:T(8,128)(2,1)S(1)} %add_convert_fusion), channel_id=1, source_target_pairs={{3,10},{7,14},{10,3},{14,7},{17,24},{21,28},{24,17},{28,21}} | collective-permute-start | bytes 1179656 | tf_op jit(solution)/shard_map/ppermute | solution.py:127

commit v2 on v1

--- a/solution.py
+++ b/solution.py
@@ -14,6 +14,7 @@
 RATIO = QH // KVH
 SCALE = 1.0 / HD**0.5
 LOW = -1e30
+STACK = 2
 
 
 def doc_ends(lengths):
@@ -27,70 +28,99 @@
 
 
 def attend_kernel(count, own, resume, last, bases, q_ref, start_ref, *refs):
-    keys, vals = refs[:count], refs[count : 2 * count]
-    refs = refs[2 * count :]
+    pieces, refs = refs[:count], refs[count:]
     if resume:
         acc_in, top_in = refs[:2]
         refs = refs[2:]
-    query = q_ref[...]
-    start = start_ref[...]
-    rows = query.shape[0]
+    outs = refs[-1:] if last else refs[-2:]
+    group = pl.program_id(0)
+    groups = pieces[0].shape[1] // (2 * HD)
+    rows = q_ref.shape[0]
+    stack = STACK
     factor = SCALE * math.log2(math.e)
-    scores = []
-    top = top_in[:, :1] if resume else None
-    for i in range(count):
-        s = lax.dot_general(
-            query, keys[i][...], (((1,), (1,)), ((), ())), preferred_element_type=jnp.float32
-        )
-        column = lax.broadcasted_iota(jnp.int32, s.shape, 1)
-        allowed = column >= start - bases[i]
-        if own and i == 0:
-            allowed = allowed & (column <= lax.broadcasted_iota(jnp.int32, s.shape, 0))
-        s = jnp.where(allowed, s, LOW)
-        high = jnp.max(s, axis=1, keepdims=True)
-        top = high if top is None else jnp.maximum(top, high)
-        scores.append(s)
-    acc = None
-    for i in range(count):
-        weights = jnp.exp2((scores[i] - top) * factor).astype(jnp.bfloat16)
-        value = vals[i][...]
-        wide = jnp.concatenate([value, jnp.ones_like(value)], axis=1)
-        part = jnp.dot(weights, wide, preferred_element_type=jnp.float32)
-        acc = part if acc is None else acc + part
-    if resume:
-        acc = acc + acc_in[...] * jnp.exp2((top_in[:, :1] - top) * factor)
-    if last:
-        out_ref = refs[0]
-        out_ref[...] = (acc[:, :HD] / acc[:, HD:]).astype(out_ref.dtype)
-    else:
-        acc_out, top_out = refs
-        acc_out[...] = acc
-        top_out[...] = jnp.broadcast_to(top, (rows, HD))
-
-
-def attend(queries, start, pieces, bases, own, state, last):
+    start = jnp.concatenate([start_ref[...]] * stack, axis=0)
+
+    def part(i, index):
+        return pieces[i][:, pl.ds(pl.multiple_of(index * HD, HD), HD)]
+
+    key = jnp.concatenate([part(i, group) for i in range(count)], axis=0)
+    value = jnp.concatenate([part(i, groups + group) for i in range(count)], axis=0)
+    value = jnp.concatenate([value, jnp.ones_like(value)], axis=1)
+
+    def score(c):
+        heads = range(c * stack, (c + 1) * stack)
+        query = jnp.concatenate([q_ref[:, j * HD : (j + 1) * HD] for j in heads], axis=0)
+        full = lax.dot_general(
+            query, key, (((1,), (1,)), ((), ())), preferred_element_type=jnp.float32
+        )
+        scores = []
+        at = 0
+        for i in range(count):
+            size = pieces[i].shape[0]
+            s = full[:, at : at + size]
+            at += size
+            column = lax.broadcasted_iota(jnp.int32, s.shape, 1)
+            allowed = column >= start - bases[i]
+            if own and i == 0:
+                row = lax.broadcasted_iota(jnp.int32, (rows, size), 0)
+                allowed = allowed & (column <= jnp.concatenate([row] * stack, axis=0))
+            scores.append(jnp.where(allowed, s, LOW))
+        return scores
+
+    def finish(c, scores):
+        heads = range(c * stack, (c + 1) * stack)
+        top = functools.reduce(jnp.maximum, [jnp.max(s, axis=1, keepdims=True) for s in scores])
+        if resume:
+            before = jnp.concatenate([top_in[:, j * HD : j * HD + 1] for j in heads], axis=0)
+            top = jnp.maximum(top, before)
+        weights = [jnp.exp2((s - top) * factor).astype(jnp.bfloat16) for s in scores]
+        acc = jnp.dot(
+            jnp.concatenate(weights, axis=1), value, preferred_element_type=jnp.float32
+        )
+        if resume:
+            old = [acc_in[:, 2 * j * HD : 2 * (j + 1) * HD] for j in heads]
+            acc = acc + jnp.concatenate(old, axis=0) * jnp.exp2((before - top) * factor)
+        for n, j in enumerate(heads):
+            mine = acc[n * rows : (n + 1) * rows]
+            if last:
+                ratio = mine[:, :HD] / mine[:, HD:]
+                outs[0][:, j * HD : (j + 1) * HD] = ratio.astype(outs[0].dtype)
+            else:
+                outs[0][:, 2 * j * HD : 2 * (j + 1) * HD] = mine
+                outs[1][:, j * HD : (j + 1) * HD] = jnp.broadcast_to(
+                    top[n * rows : (n + 1) * rows], (rows, HD)
+                )
+
+    held = None
+    for c in range(RATIO // stack):
+        scores = score(c)
+        if held is not None:
+            finish(*held)
+        held = (c, scores)
+    finish(*held)
+
+
+def attend(queries, start, pieces, bases, own, state, last, after=()):
     rows, width = queries.shape
     heads = width // HD
     groups = heads // RATIO
     count = len(pieces)
     resume = state is not None
     specs = [
-        pl.BlockSpec((rows, HD), lambda h, b: (0, h)),
-        pl.BlockSpec((rows, 1), lambda h, b: (0, 0)),
+        pl.BlockSpec((rows, RATIO * HD), lambda g, b: (0, g)),
+        pl.BlockSpec((rows, 1), lambda g, b: (0, 0)),
     ]
-    specs += [pl.BlockSpec((p.shape[0], HD), lambda h, b: (0, h // RATIO)) for p in pieces]
-    specs += [
-        pl.BlockSpec((p.shape[0], HD), lambda h, b, g=groups: (0, g + h // RATIO)) for p in pieces
-    ]
+    specs += [pl.BlockSpec(p.shape, lambda g, b: (0, 0)) for p in pieces]
     state_specs = [
-        pl.BlockSpec((rows, 2 * HD), lambda h, b: (0, h)),
-        pl.BlockSpec((rows, HD), lambda h, b: (0, h)),
+        pl.BlockSpec((rows, 2 * RATIO * HD), lambda g, b: (0, g)),
+        pl.BlockSpec((rows, RATIO * HD), lambda g, b: (0, g)),
     ]
     if resume:
         specs += state_specs
+    specs += [pl.BlockSpec(memory_space=pl.ANY)] * len(after)
     if last:
         out_shape = jax.ShapeDtypeStruct((rows, width), jnp.bfloat16)
-        out_specs = pl.BlockSpec((rows, HD), lambda h, b: (0, h))
+        out_specs = pl.BlockSpec((rows, RATIO * HD), lambda g, b: (0, g))
     else:
         out_shape = (
             jax.ShapeDtypeStruct((rows, 2 * width), jnp.float32),
@@ -102,7 +132,7 @@
         functools.partial(attend_kernel, count, own, resume, last),
         grid_spec=pltpu.PrefetchScalarGridSpec(
             num_scalar_prefetch=1,
-            grid=(heads,),
+            grid=(groups,),
             in_specs=specs,
             out_specs=out_specs,
         ),
@@ -113,7 +143,7 @@
             bytes_accessed=4 * rows * width,
             transcendentals=rows * seen * heads,
         ),
-    )(bases, queries, start, *pieces, *pieces, *(state or ()))
+    )(bases, queries, start, *pieces, *(state or ()), *after)
 
 
 def moved(value, axes, sizes, where):
@@ -139,20 +169,25 @@
     own = jnp.concatenate([keys, values], axis=1)
     back2 = send(own, where=lambda t, h: (t + 2, h) if t + 2 < count else None)
     weight_side = send(out_weight, where=lambda t, h: (t ^ 1, h))
-    back4 = send(back2, where=lambda t, h: (t + 2, h) if t + 2 < count else None)
-    back2_side = send(back2, where=lambda t, h: (t ^ 1, h))
+    weight_down = send(out_weight, where=lambda t, h: (t - 4, h) if t >= 4 else None)
+    back4 = send(back2, where=lambda t, h: (t + 2, h) if 2 <= t < count - 2 else None)
+    back2_side = send(back2, where=lambda t, h: (t ^ 1, h) if t >= 2 else None)
     rest = jnp.where(side == 0, own, back4)
-    rest = send(rest, where=lambda t, h: (t ^ 1, h))
-    weight_far = send(out_weight, where=lambda t, h: (t ^ 4, h))
+    rest = send(rest, where=lambda t, h: (t ^ 1, h) if t % 2 == 0 or t >= 4 else None)
+    late, _ = lax.optimization_barrier((out_weight, back4))
+    weight_up = send(late, where=lambda t, h: (t + 4, h) if t < 4 else None)
+    weight_far = jnp.where(level < 2, weight_down, weight_up)
     weight_far_side = send(weight_far, where=lambda t, h: (t ^ 1, h))
 
     qpos = tok * rows + jnp.arange(rows, dtype=jnp.int32)
     start = doc_starts(lengths, qpos)[:, None]
     shift = lambda k: (tok - k) * rows
-    near = jnp.stack([shift(0), shift(2), shift(2) + rows * (1 - 2 * side)])
-    far = jnp.stack([shift(4), jnp.where(side == 0, shift(3), shift(1))])
-    state = attend(queries, start, [own, back2, back2_side], near, True, None, False)
-    attn = attend(queries, start, [back4, rest], far, False, state, True)
+    first = jnp.stack([shift(0), shift(2)])
+    second = jnp.stack([shift(2) + rows * (1 - 2 * side), shift(4)])
+    third = jnp.where(side == 0, shift(3), shift(1))[None]
+    state = attend(queries, start, [own, back2], first, True, None, False)
+    state = attend(queries, start, [back2_side, back4], second, False, state, False)
+    attn = attend(queries, start, [rest], third, False, state, True, (weight_side,))
     attn_pair = send(attn, where=lambda t, h: (t ^ 2, h))
 
     mine = core == parity

time: 146 us -> 133 us (0.911)
  starting transfers between devices: 57.5 us -> 41.8 us
  waiting for transfers between devices: 49.8 us -> 62.2 us
  Pallas kernels: 23.1 us -> 15.9 us
  matrix products: 9.51 us -> 4.56 us
    ppermute x20 -> x21, starting transfers between devices: 57.5 us -> 41.8 us  [moved(): return lax.ppermute(value, axes, pairs)]
    ppermute x20 -> x21, waiting for transfers between devices: 49.8 us -> 62.2 us  [moved(): return lax.ppermute(value, axes, pairs)]
    pallas_call x2 -> x3, Pallas kernels: 23.1 us -> 15.9 us  [attend(): pl.pallas_call(functools.partial(attend_kernel, count, own, resume, last)...]
    dot_general x4, matrix products: 4.77 us -> 2.29 us  [unit(): keep = jnp.dot(keep_rows, weight, preferred_element_type=jnp.float32)]
    dot_general x4, matrix products: 4.74 us -> 2.27 us  [unit(): jnp.dot(send_rows, weight, preferred_element_type=jnp.float32)]
  transfers between devices with their start and end apart: 20 -> 21, of which waited for: 6 -> 10; matrix products, arithmetic and copies ran while one was open for 8% -> 6% of each run, Pallas kernels for 16% -> 12%
where the time goes in v2:
time: 133 us; the launch traced here: 132 us
  waiting for transfers between devices  62.2 us (47%)
  starting transfers between devices  41.8 us (31%)
  Pallas kernels  15.9 us (12%)
  other arithmetic  5 us (4%)
  matrix products  4.56 us (3%)
  local copies, waits for them, and re-layouts  2.07 us (2%)
    ppermute x21, waiting for transfers between devices, moved(): return lax.ppermute(value, axes, pairs)  62.2 us
    ppermute x21, starting transfers between devices, moved(): return lax.ppermute(value, axes, pairs)  41.8 us
    pallas_call x3, Pallas kernels, attend(): pl.pallas_call(functools.partial(attend_kernel, count, own, resume, last)...  15.9 us
  transfers between devices with their start and end apart: 21, of which 10 were waited for; matrix products, arithmetic and copies ran while one was open for 6% of the time, Pallas kernels for 12%

profile of v2, /device:TPU:17, one launch (start us, length us, event | category | flops | bytes accessed | tf_op | source)
XLA Modules:
  0.0 132.0 jit_solution(316559033302558682)
XLA Ops:
  2.0 3.2 %collective-permute-start = (bf16[384,512]{1,0:T(8,128)(2,1)S(1)}, bf16[384,512]{1,0:T(8,128)(2,1)}, u32[]{:S(2)}, u32[]{:S(2)}) collective-permute-start(bf16[384,512]{1,0:T(8,128)(2,1)S(1)} %constant_dynamic-update-slice_fusion.refs_0_), channel_id=1, source_target_pairs={{0,8},{1,9},{2,10},{3,11},{4,12},{5,13},{6,14},{7,15},{8,16},{9,17... | collective-permute-start | bytes 1179656 | tf_op jit(solution)/shard_map/ppermute | solution.py:157
  6.5 3.6 %collective-permute-start.9 = (bf16[1024,512]{1,0:T(8,128)(2,1)}, bf16[1024,512]{1,0:T(8,128)(2,1)}, u32[]{:S(2)}, u32[]{:S(2)}) collective-permute-start(bf16[1024,512]{1,0:T(8,128)(2,1)} %param.9), channel_id=1, source_target_pairs={{16,0},{17,1},{18,2},{19,3},{20,4},{21,5},{22,6},{23,7},{24,8},{25... | collective-permute-start | bytes 3145736 | tf_op jit(solution)/shard_map/ppermute | solution.py:157
  10.1 3.9 %collective-permute-done.refs_1_ = bf16[384,512]{1,0:T(8,128)(2,1)} collective-permute-done((bf16[384,512]{1,0:T(8,128)(2,1)S(1)}, bf16[384,512]{1,0:T(8,128)(2,1)}, u32[]{:S(2)}, u32[]{:S(2)}) %collective-permute-start) | collective-permute-done | bytes 393248 | tf_op jit(solution)/shard_map/ppermute | solution.py:157
  13.9 3.2 %collective-permute-start.1 = (bf16[384,512]{1,0:T(8,128)(2,1)}, bf16[384,512]{1,0:T(8,128)(2,1)S(1)}, u32[]{:S(2)}, u32[]{:S(2)}) collective-permute-start(bf16[384,512]{1,0:T(8,128)(2,1)} %collective-permute-done.refs_1_), channel_id=1, source_target_pairs={{8,16},{9,17},{10,18},{11,19},{12,20},{13,21},{14,22},{15,23},{16,... | collective-permute-start | bytes 1179656 | tf_op jit(solution)/shard_map/ppermute | solution.py:157
  18.1 3.1 %collective-permute-start.3 = (bf16[384,512]{1,0:T(8,128)(2,1)}, bf16[384,512]{1,0:T(8,128)(2,1)}, u32[]{:S(2)}, u32[]{:S(2)}) collective-permute-start(bf16[384,512]{1,0:T(8,128)(2,1)} %collective-permute-done.refs_1_), channel_id=1, source_target_pairs={{8,12},{9,13},{10,14},{11,15},{12,8},{13,9},{14,10},{15,11},{16,20... | collective-permute-start | bytes 1179656 | tf_op jit(solution)/shard_map/ppermute | solution.py:157
  21.2 3.9 %collective-permute-done.1.refs_1_ = bf16[384,512]{1,0:T(8,128)(2,1)S(1)} collective-permute-done((bf16[384,512]{1,0:T(8,128)(2,1)}, bf16[384,512]{1,0:T(8,128)(2,1)S(1)}, u32[]{:S(2)}, u32[]{:S(2)}) %collective-permute-start.1) | collective-permute-done | bytes 393248 | tf_op jit(solution)/shard_map/ppermute | solution.py:157
  27.2 3.1 %collective-permute-start.2 = (bf16[384,512]{1,0:T(8,128)(2,1)}, bf16[384,512]{1,0:T(8,128)(2,1)S(1)}, u32[]{:S(2)}, u32[]{:S(2)}) collective-permute-start(bf16[384,512]{1,0:T(8,128)(2,1)} %broadcast_select_fusion.3), channel_id=1, source_target_pairs={{0,4},{1,5},{2,6},{3,7},{8,12},{9,13},{10,14},{11,15},{16,20},{17,... | collective-permute-start | bytes 1179656 | tf_op jit(solution)/shard_map/ppermute | solution.py:157
  30.5 5.4 %shard_map.55 = (f32[384,2048]{1,0:T(8,128)S(1)}, f32[384,1024]{1,0:T(8,128)S(1)}) custom-call(s32[2]{0:T(128)S(1)} %pad_add_fusion.1.bases, bf16[384,1024]{1,0:T(8,128)(2,1)S(1)} %copy-done, s32[384,1]{1,0:T(8,128)S(1)} %broadcast_in_dim.38.start_ref, bf16[384,512]{1,0:T(8,128)(2,1)S(1)} %constant_dynamic-update-slice_fusion.refs_0_, ...), custom_call_target="tpu_custom_call" | custom-call | flops 1811939328 | bytes 1572864 | tf_op jit(solution)/shard_map/pallas_call | solution.py:131
  35.9 1.8 %collective-permute-done.3.refs_0_ = bf16[384,512]{1,0:T(8,128)(2,1)} collective-permute-done((bf16[384,512]{1,0:T(8,128)(2,1)}, bf16[384,512]{1,0:T(8,128)(2,1)}, u32[]{:S(2)}, u32[]{:S(2)}) %collective-permute-start.3) | collective-permute-done | bytes 393248 | tf_op jit(solution)/shard_map/ppermute | solution.py:157
  37.7 5.9 %shard_map.56 = (f32[384,2048]{1,0:T(8,128)S(1)}, f32[384,1024]{1,0:T(8,128)S(1)}) custom-call(s32[2]{0:T(128)S(1)} %pad_add_fusion.bases, bf16[384,1024]{1,0:T(8,128)(2,1)S(1)} %copy-done, s32[384,1]{1,0:T(8,128)S(1)} %broadcast_in_dim.38.start_ref, bf16[384,512]{1,0:T(8,128)(2,1)} %collective-permute-done.3.refs_0_, ...), custom_call_target="tpu_custom_call" | custom-call | flops 1811939328 | bytes 1572864 | tf_op jit(solution)/shard_map/pallas_call | solution.py:131
  43.6 2.5 %collective-permute-done.2.refs_0_ = bf16[384,512]{1,0:T(8,128)(2,1)S(1)} collective-permute-done((bf16[384,512]{1,0:T(8,128)(2,1)}, bf16[384,512]{1,0:T(8,128)(2,1)S(1)}, u32[]{:S(2)}, u32[]{:S(2)}) %collective-permute-start.2) | collective-permute-done | bytes 393248 | tf_op jit(solution)/shard_map/ppermute | solution.py:157
  46.1 4.7 %shard_map.57 = bf16[384,1024]{1,0:T(8,128)(2,1)S(1)} custom-call(s32[1]{0:T(128)} %bitcast.bases, bf16[384,1024]{1,0:T(8,128)(2,1)S(1)} %copy-done, s32[384,1]{1,0:T(8,128)S(1)} %broadcast_in_dim.38.start_ref, bf16[384,512]{1,0:T(8,128)(2,1)S(1)} %collective-permute-done.2.refs_0_, f32[384,2048]{1,0:T(8,128)S(1)} %get-tuple-element.12.refs_1_, ...), custom_call_target="tpu_custom_call" | custom-call | flops 905969664 | bytes 1572864 | tf_op jit(solution)/shard_map/pallas_call | solution.py:131
  50.9 3.5 %collective-permute-done.9 = bf16[1024,512]{1,0:T(8,128)(2,1)} collective-permute-done((bf16[1024,512]{1,0:T(8,128)(2,1)}, bf16[1024,512]{1,0:T(8,128)(2,1)}, u32[]{:S(2)}, u32[]{:S(2)}) %collective-permute-start.9) | collective-permute-done | bytes 1048608 | tf_op jit(solution)/shard_map/ppermute | solution.py:157
  54.4 1.3 %broadcast_select_fusion = bf16[1024,512]{1,0:T(8,128)(2,1)S(1)} fusion(bf16[1024,512]{1,0:T(8,128)(2,1)} %collective-permute-done.9, bf16[1024,512]{1,0:T(8,128)(2,1)} %collective-permute-done.10, pred[]{:T(512)S(6)} %lt.20), kind=kLoop, calls=%fused_computation.8 | loop fusion | flops 524288 | bytes 3145729 | tf_op jit(solution)/shard_map/jit(_where)/select_n | solution.py:179
  56.1 33.4 %collective-permute-done.5 = bf16[384,1024]{1,0:T(8,128)(2,1)S(1)} collective-permute-done((bf16[384,1024]{1,0:T(8,128)(2,1)S(1)}, bf16[384,1024]{1,0:T(8,128)(2,1)S(1)}, u32[]{:S(2)}, u32[]{:S(2)}) %collective-permute-start.5) | collective-permute-done | bytes 786464 | tf_op jit(solution)/shard_map/ppermute | solution.py:157
  90.2 1.6 %collective-permute-start.6 = (bf16[384,512]{1,0:T(8,128)(2,1)S(1)}, bf16[384,512]{1,0:T(8,128)(2,1)S(1)}, u32[]{:S(2)}, u32[]{:S(2)}) collective-permute-start(bf16[384,512]{1,0:T(8,128)(2,1)S(1)} %convolution_convert_fusion.3), channel_id=1, source_target_pairs={{0,1},{1,0},{2,3},{3,2},{4,5},{5,4},{6,7},{7,6},{8,9},{9,8},{10,11... | collective-permute-start | bytes 1179656 | tf_op jit(solution)/shard_map/ppermute | solution.py:157
  94.1 3.2 %collective-permute-start.7 = (bf16[384,512]{1,0:T(8,128)(2,1)S(1)}, bf16[384,512]{1,0:T(8,128)(2,1)S(1)}, u32[]{:S(2)}, u32[]{:S(2)}) collective-permute-start(bf16[384,512]{1,0:T(8,128)(2,1)S(1)} %get-tuple-element.23), channel_id=1, source_target_pairs={{2,0},{3,1},{6,4},{7,5},{10,8},{11,9},{14,12},{15,13},{16,18},{17,... | collective-permute-start | bytes 1179656 | tf_op jit(solution)/shard_map/ppermute | solution.py:157
  100.8 4.3 %collective-permute-start.15 = (bf16[384,512]{1,0:T(8,128)(2,1)S(1)}, bf16[384,512]{1,0:T(8,128)(2,1)S(1)}, u32[]{:S(2)}, u32[]{:S(2)}) collective-permute-start(bf16[384,512]{1,0:T(8,128)(2,1)S(1)} %get-tuple-element.19), channel_id=1, source_target_pairs={{2,0},{3,1},{6,4},{7,5},{10,8},{11,9},{14,12},{15,13},{16,18},{17,... | collective-permute-start | bytes 1179656 | tf_op jit(solution)/shard_map/ppermute | solution.py:157
  107.2 1.3 collective-permute-start.19
  108.5 1.7 %collective-permute-done.12 = bf16[384,512]{1,0:T(8,128)(2,1)S(1)} collective-permute-done((bf16[384,512]{1,0:T(8,128)(2,1)S(1)}, bf16[384,512]{1,0:T(8,128)(2,1)S(1)}, u32[]{:S(2)}, u32[]{:S(2)}) %collective-permute-start.12) | collective-permute-done | bytes 393248 | tf_op jit(solution)/shard_map/ppermute | solution.py:157
  110.3 5.1 %collective-permute-start.13 = (bf16[384,512]{1,0:T(8,128)(2,1)S(1)}, bf16[384,512]{1,0:T(8,128)(2,1)S(1)}, u32[]{:S(2)}, u32[]{:S(2)}) collective-permute-start(bf16[384,512]{1,0:T(8,128)(2,1)S(1)} %add_convert_fusion.2), channel_id=1, source_target_pairs={{3,10},{7,14},{10,3},{14,7},{17,24},{21,28},{24,17},{28,21}} | collective-permute-start | bytes 1179656 | tf_op jit(solution)/shard_map/ppermute | solution.py:157
  116.3 5.3 %collective-permute-done.19 = bf16[384,512]{1,0:T(8,128)(2,1)S(1)} collective-permute-done((bf16[384,512]{1,0:T(8,128)(2,1)S(1)}, bf16[384,512]{1,0:T(8,128)(2,1)S(1)}, u32[]{:S(2)}, u32[]{:S(2)}) %collective-permute-start.19) | collective-permute-done | bytes 393248 | tf_op jit(solution)/shard_map/ppermute | solution.py:157
  121.8 3.4 %collective-permute-start.20 = (bf16[384,512]{1,0:T(8,128)(2,1)S(1)}, bf16[384,512]{1,0:T(8,128)(2,1)S(1)}, u32[]{:S(2)}, u32[]{:S(2)}) collective-permute-start(bf16[384,512]{1,0:T(8,128)(2,1)S(1)} %add_convert_fusion), channel_id=1, source_target_pairs={{3,10},{7,14},{10,3},{14,7},{17,24},{21,28},{24,17},{28,21}} | collective-permute-start | bytes 1179656 | tf_op jit(solution)/shard_map/ppermute | solution.py:157
  125.3 5.5 %collective-permute-done.20 = bf16[384,512]{1,0:T(8,128)(2,1)S(1)} collective-permute-done((bf16[384,512]{1,0:T(8,128)(2,1)S(1)}, bf16[384,512]{1,0:T(8,128)(2,1)S(1)}, u32[]{:S(2)}, u32[]{:S(2)}) %collective-permute-start.20) | collective-permute-done | bytes 393248 | tf_op jit(solution)/shard_map/ppermute | solution.py:157
  (51 shorter events, 17.7 us)
Async XLA Ops:
  0.0 30.5 %copy-start = (bf16[384,1024]{1,0:T(8,128)(2,1)S(1)}, bf16[384,1024]{1,0:T(8,128)(2,1)}, u32[]{:S(2)}) copy-start(bf16[384,1024]{1,0:T(8,128)(2,1)} %q_ref.5) | copy-start | bytes 2359300
  2.0 12.0 %collective-permute-start = (bf16[384,512]{1,0:T(8,128)(2,1)S(1)}, bf16[384,512]{1,0:T(8,128)(2,1)}, u32[]{:S(2)}, u32[]{:S(2)}) collective-permute-start(bf16[384,512]{1,0:T(8,128)(2,1)S(1)} %constant_dynamic-update-slice_fusion.refs_0_), channel_id=1, source_target_pairs={{0,8},{1,9},{2,10},{3,11},{4,12},{5,13},{6,14},{7,15},{8,16},{9,17... | collective-permute-start | bytes 1179656 | tf_op jit(solution)/shard_map/ppermute | solution.py:157
  5.2 38.4 %collective-permute-start.4 = (bf16[1024,512]{1,0:T(8,128)(2,1)}, bf16[1024,512]{1,0:T(8,128)(2,1)S(1)}, u32[]{:S(2)}, u32[]{:S(2)}) collective-permute-start(bf16[1024,512]{1,0:T(8,128)(2,1)} %param.9), channel_id=1, source_target_pairs={{0,4},{1,5},{2,6},{3,7},{4,0},{5,1},{6,2},{7,3},{8,12},{9,13},{10,... | collective-permute-start | bytes 3145736 | tf_op jit(solution)/shard_map/ppermute | solution.py:157
  6.5 47.9 %collective-permute-start.9 = (bf16[1024,512]{1,0:T(8,128)(2,1)}, bf16[1024,512]{1,0:T(8,128)(2,1)}, u32[]{:S(2)}, u32[]{:S(2)}) collective-permute-start(bf16[1024,512]{1,0:T(8,128)(2,1)} %param.9), channel_id=1, source_target_pairs={{16,0},{17,1},{18,2},{19,3},{20,4},{21,5},{22,6},{23,7},{24,8},{25... | collective-permute-start | bytes 3145736 | tf_op jit(solution)/shard_map/ppermute | solution.py:157
  13.9 11.2 %collective-permute-start.1 = (bf16[384,512]{1,0:T(8,128)(2,1)}, bf16[384,512]{1,0:T(8,128)(2,1)S(1)}, u32[]{:S(2)}, u32[]{:S(2)}) collective-permute-start(bf16[384,512]{1,0:T(8,128)(2,1)} %collective-permute-done.refs_1_), channel_id=1, source_target_pairs={{8,16},{9,17},{10,18},{11,19},{12,20},{13,21},{14,22},{15,23},{16,... | collective-permute-start | bytes 1179656 | tf_op jit(solution)/shard_map/ppermute | solution.py:157
  18.1 19.6 %collective-permute-start.3 = (bf16[384,512]{1,0:T(8,128)(2,1)}, bf16[384,512]{1,0:T(8,128)(2,1)}, u32[]{:S(2)}, u32[]{:S(2)}) collective-permute-start(bf16[384,512]{1,0:T(8,128)(2,1)} %collective-permute-done.refs_1_), channel_id=1, source_target_pairs={{8,12},{9,13},{10,14},{11,15},{12,8},{13,9},{14,10},{15,11},{16,20... | collective-permute-start | bytes 1179656 | tf_op jit(solution)/shard_map/ppermute | solution.py:157
  25.1 29.3 %collective-permute-start.10 = (bf16[1024,512]{1,0:T(8,128)(2,1)}, bf16[1024,512]{1,0:T(8,128)(2,1)}, u32[]{:S(2)}, u32[]{:S(2)}) collective-permute-start(bf16[1024,512]{1,0:T(8,128)(2,1)} %param.9), channel_id=1, source_target_pairs={{0,16},{1,17},{2,18},{3,19},{4,20},{5,21},{6,22},{7,23},{8,24},{9,... | collective-permute-start | bytes 3145736 | tf_op jit(solution)/shard_map/ppermute | solution.py:157
  27.2 18.9 %collective-permute-start.2 = (bf16[384,512]{1,0:T(8,128)(2,1)}, bf16[384,512]{1,0:T(8,128)(2,1)S(1)}, u32[]{:S(2)}, u32[]{:S(2)}) collective-permute-start(bf16[384,512]{1,0:T(8,128)(2,1)} %broadcast_select_fusion.3), channel_id=1, source_target_pairs={{0,4},{1,5},{2,6},{3,7},{8,12},{9,13},{10,14},{11,15},{16,20},{17,... | collective-permute-start | bytes 1179656 | tf_op jit(solution)/shard_map/ppermute | solution.py:157
  50.8 38.7 %collective-permute-start.5 = (bf16[384,1024]{1,0:T(8,128)(2,1)S(1)}, bf16[384,1024]{1,0:T(8,128)(2,1)S(1)}, u32[]{:S(2)}, u32[]{:S(2)}) collective-permute-start(bf16[384,1024]{1,0:T(8,128)(2,1)S(1)} %shard_map.57), channel_id=1, source_target_pairs={{0,8},{1,9},{2,10},{3,11},{4,12},{5,13},{6,14},{7,15},{8,0},{9,1},... | collective-permute-start | bytes 2359304 | tf_op jit(solution)/shard_map/ppermute | solution.py:157
  55.7 33.8 %copy-start.1 = (bf16[1024,512]{1,0:T(8,128)(2,1)S(1)}, bf16[1024,512]{1,0:T(8,128)(2,1)}, u32[]{:S(2)}) copy-start(bf16[1024,512]{1,0:T(8,128)(2,1)} %param.9) | copy-start | bytes 3145732
  55.8 43.5 %collective-permute-start.17 = (bf16[1024,512]{1,0:T(8,128)(2,1)S(1)}, bf16[1024,512]{1,0:T(8,128)(2,1)S(1)}, u32[]{:S(2)}, u32[]{:S(2)}) collective-permute-start(bf16[1024,512]{1,0:T(8,128)(2,1)S(1)} %broadcast_select_fusion), channel_id=1, source_target_pairs={{0,4},{1,5},{2,6},{3,7},{4,0},{5,1},{6,2},{7,3},{8,12},{9,13},{10,... | collective-permute-start | bytes 3145736 | tf_op jit(solution)/shard_map/ppermute | solution.py:157
  90.2 3.4 %collective-permute-start.6 = (bf16[384,512]{1,0:T(8,128)(2,1)S(1)}, bf16[384,512]{1,0:T(8,128)(2,1)S(1)}, u32[]{:S(2)}, u32[]{:S(2)}) collective-permute-start(bf16[384,512]{1,0:T(8,128)(2,1)S(1)} %convolution_convert_fusion.3), channel_id=1, source_target_pairs={{0,1},{1,0},{2,3},{3,2},{4,5},{5,4},{6,7},{7,6},{8,9},{9,8},{10,11... | collective-permute-start | bytes 1179656 | tf_op jit(solution)/shard_map/ppermute | solution.py:157
  92.3 5.0 %collective-permute-start.11 = (bf16[384,512]{1,0:T(8,128)(2,1)S(1)}, bf16[384,512]{1,0:T(8,128)(2,1)S(1)}, u32[]{:S(2)}, u32[]{:S(2)}) collective-permute-start(bf16[384,512]{1,0:T(8,128)(2,1)S(1)} %convolution_convert_fusion.2), channel_id=1, source_target_pairs={{0,1},{1,0},{2,3},{3,2},{4,5},{5,4},{6,7},{7,6},{8,9},{9,8},{10,11... | collective-permute-start | bytes 1179656 | tf_op jit(solution)/shard_map/ppermute | solution.py:157
  93.0 7.2 %collective-permute-start.14 = (bf16[384,512]{1,0:T(8,128)(2,1)S(1)}, bf16[384,512]{1,0:T(8,128)(2,1)S(1)}, u32[]{:S(2)}, u32[]{:S(2)}) collective-permute-start(bf16[384,512]{1,0:T(8,128)(2,1)S(1)} %convolution_convert_fusion.1), channel_id=1, source_target_pairs={{0,1},{1,0},{2,3},{3,2},{4,5},{5,4},{6,7},{7,6},{8,9},{9,8},{10,11... | collective-permute-start | bytes 1179656 | tf_op jit(solution)/shard_map/ppermute | solution.py:157
  94.1 11.7 %collective-permute-start.7 = (bf16[384,512]{1,0:T(8,128)(2,1)S(1)}, bf16[384,512]{1,0:T(8,128)(2,1)S(1)}, u32[]{:S(2)}, u32[]{:S(2)}) collective-permute-start(bf16[384,512]{1,0:T(8,128)(2,1)S(1)} %get-tuple-element.23), channel_id=1, source_target_pairs={{2,0},{3,1},{6,4},{7,5},{10,8},{11,9},{14,12},{15,13},{16,18},{17,... | collective-permute-start | bytes 1179656 | tf_op jit(solution)/shard_map/ppermute | solution.py:157
  97.9 12.3 %collective-permute-start.12 = (bf16[384,512]{1,0:T(8,128)(2,1)S(1)}, bf16[384,512]{1,0:T(8,128)(2,1)S(1)}, u32[]{:S(2)}, u32[]{:S(2)}) collective-permute-start(bf16[384,512]{1,0:T(8,128)(2,1)S(1)} %get-tuple-element.21), channel_id=1, source_target_pairs={{0,2},{1,3},{4,6},{5,7},{8,10},{9,11},{12,14},{13,15},{18,16},{19,... | collective-permute-start | bytes 1179656 | tf_op jit(solution)/shard_map/ppermute | solution.py:157
  99.8 6.8 %collective-permute-start.18 = (bf16[384,512]{1,0:T(8,128)(2,1)S(1)}, bf16[384,512]{1,0:T(8,128)(2,1)S(1)}, u32[]{:S(2)}, u32[]{:S(2)}) collective-permute-start(bf16[384,512]{1,0:T(8,128)(2,1)S(1)} %convolution_convert_fusion), channel_id=1, source_target_pairs={{0,1},{1,0},{2,3},{3,2},{4,5},{5,4},{6,7},{7,6},{8,9},{9,8},{10,11... | collective-permute-start | bytes 1179656 | tf_op jit(solution)/shard_map/ppermute | solution.py:157
  100.8 14.7 %collective-permute-start.15 = (bf16[384,512]{1,0:T(8,128)(2,1)S(1)}, bf16[384,512]{1,0:T(8,128)(2,1)S(1)}, u32[]{:S(2)}, u32[]{:S(2)}) collective-permute-start(bf16[384,512]{1,0:T(8,128)(2,1)S(1)} %get-tuple-element.19), channel_id=1, source_target_pairs={{2,0},{3,1},{6,4},{7,5},{10,8},{11,9},{14,12},{15,13},{16,18},{17,... | collective-permute-start | bytes 1179656 | tf_op jit(solution)/shard_map/ppermute | solution.py:157
  105.9 19.3 %collective-permute-start.8 = (bf16[384,512]{1,0:T(8,128)(2,1)S(1)}, bf16[384,512]{1,0:T(8,128)(2,1)S(1)}, u32[]{:S(2)}, u32[]{:S(2)}) collective-permute-start(bf16[384,512]{1,0:T(8,128)(2,1)S(1)} %add_convert_fusion.3), channel_id=1, source_target_pairs={{1,8},{5,12},{8,1},{12,5},{19,26},{23,30},{26,19},{30,23}} | collective-permute-start | bytes 1179656 | tf_op jit(solution)/shard_map/ppermute | solution.py:157
  107.2 14.4 %collective-permute-start.19 = (bf16[384,512]{1,0:T(8,128)(2,1)S(1)}, bf16[384,512]{1,0:T(8,128)(2,1)S(1)}, u32[]{:S(2)}, u32[]{:S(2)}) collective-permute-start(bf16[384,512]{1,0:T(8,128)(2,1)S(1)} %get-tuple-element.17), channel_id=1, source_target_pairs={{0,2},{1,3},{4,6},{5,7},{8,10},{9,11},{12,14},{13,15},{18,16},{19,... | collective-permute-start | bytes 1179656 | tf_op jit(solution)/shard_map/ppermute | solution.py:157
  110.3 14.9 %collective-permute-start.13 = (bf16[384,512]{1,0:T(8,128)(2,1)S(1)}, bf16[384,512]{1,0:T(8,128)(2,1)S(1)}, u32[]{:S(2)}, u32[]{:S(2)}) collective-permute-start(bf16[384,512]{1,0:T(8,128)(2,1)S(1)} %add_convert_fusion.2), channel_id=1, source_target_pairs={{3,10},{7,14},{10,3},{14,7},{17,24},{21,28},{24,17},{28,21}} | collective-permute-start | bytes 1179656 | tf_op jit(solution)/shard_map/ppermute | solution.py:157
  115.6 9.7 %collective-permute-start.16 = (bf16[384,512]{1,0:T(8,128)(2,1)S(1)}, bf16[384,512]{1,0:T(8,128)(2,1)S(1)}, u32[]{:S(2)}, u32[]{:S(2)}) collective-permute-start(bf16[384,512]{1,0:T(8,128)(2,1)S(1)} %add_convert_fusion.1), channel_id=1, source_target_pairs={{1,8},{5,12},{8,1},{12,5},{19,26},{23,30},{26,19},{30,23}} | collective-permute-start | bytes 1179656 | tf_op jit(solution)/shard_map/ppermute | solution.py:157
  121.8 9.1 %collective-permute-start.20 = (bf16[384,512]{1,0:T(8,128)(2,1)S(1)}, bf16[384,512]{1,0:T(8,128)(2,1)S(1)}, u32[]{:S(2)}, u32[]{:S(2)}) collective-permute-start(bf16[384,512]{1,0:T(8,128)(2,1)S(1)} %add_convert_fusion), channel_id=1, source_target_pairs={{3,10},{7,14},{10,3},{14,7},{17,24},{21,28},{24,17},{28,21}} | collective-permute-start | bytes 1179656 | tf_op jit(solution)/shard_map/ppermute | solution.py:157

commit v3 on v2

--- a/solution.py
+++ b/solution.py
@@ -157,6 +157,19 @@
     return lax.ppermute(value, axes, pairs)
 
 
+def beside_kernel(left, right, out):
+    width = left.shape[1]
+    out[:, :width] = left[...]
+    out[:, width:] = right[...]
+
+
+def beside(left, right):
+    rows, width = left.shape
+    return pl.pallas_call(
+        beside_kernel, out_shape=jax.ShapeDtypeStruct((rows, 2 * width), left.dtype)
+    )(left, right)
+
+
 def paired_body(queries, keys, values, lengths, out_weight):
     rows, width = queries.shape
     axes = ("tok", "head")
@@ -166,7 +179,7 @@
     parity, core, half = level % 2, head % 2, head // 2
     send = functools.partial(moved, axes=axes, sizes=sizes)
 
-    own = jnp.concatenate([keys, values], axis=1)
+    own = beside(keys, values)
     back2 = send(own, where=lambda t, h: (t + 2, h) if t + 2 < count else None)
     weight_side = send(out_weight, where=lambda t, h: (t ^ 1, h))
     weight_down = send(out_weight, where=lambda t, h: (t - 4, h) if t >= 4 else None)
@@ -174,9 +187,13 @@
     back2_side = send(back2, where=lambda t, h: (t ^ 1, h) if t >= 2 else None)
     rest = jnp.where(side == 0, own, back4)
     rest = send(rest, where=lambda t, h: (t ^ 1, h) if t % 2 == 0 or t >= 4 else None)
-    late, _ = lax.optimization_barrier((out_weight, back4))
-    weight_up = send(late, where=lambda t, h: (t + 4, h) if t < 4 else None)
-    weight_far = jnp.where(level < 2, weight_down, weight_up)
+    late, _ = lax.optimization_barrier((out_weight, back2))
+    weight_up = send(late, where=lambda t, h: (t + 4, h) if t in (2, 3) else None)
+    later, _ = lax.optimization_barrier((out_weight, back2_side))
+    weight_up2 = send(later, where=lambda t, h: (t + 4, h) if t < 2 else None)
+    weight_far = jnp.where(
+        level < 2, weight_down, jnp.where(level == 2, weight_up2, weight_up)
+    )
     weight_far_side = send(weight_far, where=lambda t, h: (t ^ 1, h))
 
     qpos = tok * rows + jnp.arange(rows, dtype=jnp.int32)

time: 133 us -> 127 us (0.955)
  waiting for transfers between devices: 62.2 us -> 46 us
  starting transfers between devices: 41.8 us -> 51.4 us
    ppermute x21 -> x22, waiting for transfers between devices: 62.2 us -> 46 us  [moved(): return lax.ppermute(value, axes, pairs)]
    ppermute x21 -> x22, starting transfers between devices: 41.8 us -> 51.4 us  [moved(): return lax.ppermute(value, axes, pairs)]
    pallas_call x0 -> x1, Pallas kernels: none -> 1.87 us  [beside(): pl.pallas_call(beside_kernel, out_shape=jax.ShapeDtypeStruct((rows, 2 * w...]
    pallas_call x3, Pallas kernels: 15.9 us -> 14.2 us  [attend(): pl.pallas_call(functools.partial(attend_kernel, count, own, resume, last)...]
  transfers between devices with their start and end apart: 21 -> 22, of which waited for: 10 -> 8; matrix products, arithmetic and copies ran while one was open for 6% -> 8% of each run, Pallas kernels for 12% -> 11%
where the time goes in v3:
time: 127 us; the launch traced here: 126 us
  starting transfers between devices  51.4 us (40%)
  waiting for transfers between devices  46 us (36%)
  Pallas kernels  16.1 us (13%)
  other arithmetic  6.03 us (5%)
  matrix products  4.62 us (4%)
  local copies, waits for them, and re-layouts  1.84 us (1%)
    ppermute x22, starting transfers between devices, moved(): return lax.ppermute(value, axes, pairs)  51.4 us
    ppermute x22, waiting for transfers between devices, moved(): return lax.ppermute(value, axes, pairs)  46 us
    pallas_call x3, Pallas kernels, attend(): pl.pallas_call(functools.partial(attend_kernel, count, own, resume, last)...  14.2 us
  transfers between devices with their start and end apart: 22, of which 8 were waited for; matrix products, arithmetic and copies ran while one was open for 8% of the time, Pallas kernels for 11%

profile of v3, /device:TPU:17, one launch (start us, length us, event | category | flops | bytes accessed | tf_op | source)
XLA Modules:
  0.0 126.4 jit_solution(11028260256795942497)
XLA Ops:
  0.0 1.9 %shard_map.55.refs_0_ = bf16[384,512]{1,0:T(8,128)(2,1)} custom-call(bf16[384,256]{1,0:T(8,128)(2,1)} %left.1, bf16[384,256]{1,0:T(8,128)(2,1)} %right.1), custom_call_target="tpu_custom_call" | custom-call | tf_op jit(solution)/shard_map/pallas_call | solution.py:168
  1.9 3.2 %collective-permute-start = (bf16[384,512]{1,0:T(8,128)(2,1)}, bf16[384,512]{1,0:T(8,128)(2,1)S(1)}, u32[]{:S(2)}, u32[]{:S(2)}) collective-permute-start(bf16[384,512]{1,0:T(8,128)(2,1)} %shard_map.55.refs_0_), channel_id=1, source_target_pairs={{0,8},{1,9},{2,10},{3,11},{4,12},{5,13},{6,14},{7,15},{8,16},{9,17... | collective-permute-start | bytes 1179656 | tf_op jit(solution)/shard_map/ppermute | solution.py:157
  6.3 3.0 %collective-permute-start.9 = (bf16[1024,512]{1,0:T(8,128)(2,1)}, bf16[1024,512]{1,0:T(8,128)(2,1)}, u32[]{:S(2)}, u32[]{:S(2)}) collective-permute-start(bf16[1024,512]{1,0:T(8,128)(2,1)} %param.9), channel_id=1, source_target_pairs={{16,0},{17,1},{18,2},{19,3},{20,4},{21,5},{22,6},{23,7},{24,8},{25... | collective-permute-start | bytes 3145736 | tf_op jit(solution)/shard_map/ppermute | solution.py:157
  9.3 4.6 %collective-permute-done.refs_1_ = bf16[384,512]{1,0:T(8,128)(2,1)S(1)} collective-permute-done((bf16[384,512]{1,0:T(8,128)(2,1)}, bf16[384,512]{1,0:T(8,128)(2,1)S(1)}, u32[]{:S(2)}, u32[]{:S(2)}) %collective-permute-start) | collective-permute-done | bytes 393248 | tf_op jit(solution)/shard_map/ppermute | solution.py:157
  13.9 3.2 %collective-permute-start.1 = (bf16[384,512]{1,0:T(8,128)(2,1)S(1)}, bf16[384,512]{1,0:T(8,128)(2,1)S(1)}, u32[]{:S(2)}, u32[]{:S(2)}) collective-permute-start(bf16[384,512]{1,0:T(8,128)(2,1)S(1)} %collective-permute-done.refs_1_), channel_id=1, source_target_pairs={{8,16},{9,17},{10,18},{11,19},{12,20},{13,21},{14,22},{15,23},{16,... | collective-permute-start | bytes 1179656 | tf_op jit(solution)/shard_map/ppermute | solution.py:157
  17.1 3.1 %collective-permute-start.3 = (bf16[384,512]{1,0:T(8,128)(2,1)S(1)}, bf16[384,512]{1,0:T(8,128)(2,1)S(1)}, u32[]{:S(2)}, u32[]{:S(2)}) collective-permute-start(bf16[384,512]{1,0:T(8,128)(2,1)S(1)} %collective-permute-done.refs_1_), channel_id=1, source_target_pairs={{8,12},{9,13},{10,14},{11,15},{12,8},{13,9},{14,10},{15,11},{16,20... | collective-permute-start | bytes 1179656 | tf_op jit(solution)/shard_map/ppermute | solution.py:157
  21.2 1.6 %collective-permute-start.11 = (bf16[1024,512]{1,0:T(8,128)(2,1)}, bf16[1024,512]{1,0:T(8,128)(2,1)}, u32[]{:S(2)}, u32[]{:S(2)}) collective-permute-start(bf16[1024,512]{1,0:T(8,128)(2,1)} %param.9), channel_id=1, source_target_pairs={{8,24},{9,25},{10,26},{11,27},{12,28},{13,29},{14,30},{15,31}} | collective-permute-start | bytes 3145736 | tf_op jit(solution)/shard_map/ppermute | solution.py:157
  22.8 14.6 %collective-permute-done.3.refs_0_ = bf16[384,512]{1,0:T(8,128)(2,1)S(1)} collective-permute-done((bf16[384,512]{1,0:T(8,128)(2,1)S(1)}, bf16[384,512]{1,0:T(8,128)(2,1)S(1)}, u32[]{:S(2)}, u32[]{:S(2)}) %collective-permute-start.3) | collective-permute-done | bytes 393248 | tf_op jit(solution)/shard_map/ppermute | solution.py:157
  39.5 1.8 %broadcast_select_fusion.2 = bf16[384,512]{1,0:T(8,128)(2,1)} fusion(bf16[384,512]{1,0:T(8,128)(2,1)} %shard_map.55.refs_0_, bf16[384,512]{1,0:T(8,128)(2,1)S(1)} %collective-permute-done.1.refs_1_, pred[]{:T(512)S(6)} %eq.18), kind=kLoop, calls=%fused_computation.18 | loop fusion | flops 196608 | bytes 1179649 | tf_op jit(solution)/shard_map/jit(_where)/select_n | solution.py:188
  41.3 2.1 %collective-permute-start.2 = (bf16[384,512]{1,0:T(8,128)(2,1)}, bf16[384,512]{1,0:T(8,128)(2,1)S(1)}, u32[]{:S(2)}, u32[]{:S(2)}) collective-permute-start(bf16[384,512]{1,0:T(8,128)(2,1)} %broadcast_select_fusion.2), channel_id=1, source_target_pairs={{0,4},{1,5},{2,6},{3,7},{8,12},{9,13},{10,14},{11,15},{16,20},{17,... | collective-permute-start | bytes 1179656 | tf_op jit(solution)/shard_map/ppermute | solution.py:157
  44.6 4.4 %shard_map.56 = (f32[384,2048]{1,0:T(8,128)S(1)}, f32[384,1024]{1,0:T(8,128)S(1)}) custom-call(s32[2]{0:T(128)S(1)} %pad_add_fusion.1.bases, bf16[384,1024]{1,0:T(8,128)(2,1)S(1)} %copy-done.1, s32[384,1]{1,0:T(8,128)S(1)} %broadcast_in_dim.38.start_ref, bf16[384,512]{1,0:T(8,128)(2,1)S(1)} %copy-done, bf16[384,512]{1,0:T(8,128)(2,1)S(1)} %collective-permute-done.refs_1_), custom_call_target="tpu_custom_call" | custom-call | flops 1811939328 | bytes 1572864 | tf_op jit(solution)/shard_map/pallas_call | solution.py:131
  49.1 5.1 %shard_map.57 = (f32[384,2048]{1,0:T(8,128)S(1)}, f32[384,1024]{1,0:T(8,128)S(1)}) custom-call(s32[2]{0:T(128)S(1)} %pad_add_fusion.bases, bf16[384,1024]{1,0:T(8,128)(2,1)S(1)} %copy-done.1, s32[384,1]{1,0:T(8,128)S(1)} %broadcast_in_dim.38.start_ref, bf16[384,512]{1,0:T(8,128)(2,1)S(1)} %copy-done.3, bf16[384,512]{1,0:T(8,128)(2,1)S(1)} %collective-permute-done.1.refs_1_, ...), custom_call_target="tpu_custom_call" | custom-call | flops 1811939328 | bytes 1572864 | tf_op jit(solution)/shard_map/pallas_call | solution.py:131
  54.2 4.7 %shard_map.58 = bf16[384,1024]{1,0:T(8,128)(2,1)S(1)} custom-call(s32[1]{0:T(128)} %bitcast.bases, bf16[384,1024]{1,0:T(8,128)(2,1)S(1)} %copy-done.1, s32[384,1]{1,0:T(8,128)S(1)} %broadcast_in_dim.38.start_ref, bf16[384,512]{1,0:T(8,128)(2,1)S(1)} %collective-permute-done.2.refs_0_, f32[384,2048]{1,0:T(8,128)S(1)} %get-tuple-element.13.refs_1_, ...), custom_call_target="tpu_custom_call" | custom-call | flops 905969664 | bytes 1572864 | tf_op jit(solution)/shard_map/pallas_call | solution.py:131
  59.1 5.1 %collective-permute-done.10 = bf16[1024,512]{1,0:T(8,128)(2,1)} collective-permute-done((bf16[1024,512]{1,0:T(8,128)(2,1)}, bf16[1024,512]{1,0:T(8,128)(2,1)}, u32[]{:S(2)}, u32[]{:S(2)}) %collective-permute-start.10) | collective-permute-done | bytes 1048608 | tf_op jit(solution)/shard_map/ppermute | solution.py:157
  64.2 1.4 %select_select_fusion = bf16[1024,512]{1,0:T(8,128)(2,1)S(1)} fusion(bf16[1024,512]{1,0:T(8,128)(2,1)} %collective-permute-done.9, bf16[1024,512]{1,0:T(8,128)(2,1)} %collective-permute-done.10, bf16[1024,512]{1,0:T(8,128)(2,1)} %collective-permute-done.11, pred[]{:T(512)S(6)} %eq.21, pred[]{:T(512)S(6)} %lt.20), kind=kLoop, calls=%fused_computation.8 | loop fusion | flops 1048576 | bytes 4194306 | tf_op jit(solution)/shard_map/jit(_where)/select_n | solution.py:194
  66.9 9.8 %collective-permute-done.5 = bf16[384,1024]{1,0:T(8,128)(2,1)S(1)} collective-permute-done((bf16[384,1024]{1,0:T(8,128)(2,1)S(1)}, bf16[384,1024]{1,0:T(8,128)(2,1)S(1)}, u32[]{:S(2)}, u32[]{:S(2)}) %collective-permute-start.5) | collective-permute-done | bytes 786464 | tf_op jit(solution)/shard_map/ppermute | solution.py:157
  77.4 5.7 %collective-permute-start.6 = (bf16[384,512]{1,0:T(8,128)(2,1)S(1)}, bf16[384,512]{1,0:T(8,128)(2,1)S(1)}, u32[]{:S(2)}, u32[]{:S(2)}) collective-permute-start(bf16[384,512]{1,0:T(8,128)(2,1)S(1)} %convolution_convert_fusion.3), channel_id=1, source_target_pairs={{0,1},{1,0},{2,3},{3,2},{4,5},{5,4},{6,7},{7,6},{8,9},{9,8},{10,11... | collective-permute-start | bytes 1179656 | tf_op jit(solution)/shard_map/ppermute | solution.py:157
  85.5 3.2 %collective-permute-start.7 = (bf16[384,512]{1,0:T(8,128)(2,1)S(1)}, bf16[384,512]{1,0:T(8,128)(2,1)S(1)}, u32[]{:S(2)}, u32[]{:S(2)}) collective-permute-start(bf16[384,512]{1,0:T(8,128)(2,1)S(1)} %get-tuple-element.25), channel_id=1, source_target_pairs={{2,0},{3,1},{6,4},{7,5},{10,8},{11,9},{14,12},{15,13},{16,18},{17,... | collective-permute-start | bytes 1179656 | tf_op jit(solution)/shard_map/ppermute | solution.py:157
  92.5 4.0 %collective-permute-start.16 = (bf16[384,512]{1,0:T(8,128)(2,1)S(1)}, bf16[384,512]{1,0:T(8,128)(2,1)S(1)}, u32[]{:S(2)}, u32[]{:S(2)}) collective-permute-start(bf16[384,512]{1,0:T(8,128)(2,1)S(1)} %get-tuple-element.21), channel_id=1, source_target_pairs={{2,0},{3,1},{6,4},{7,5},{10,8},{11,9},{14,12},{15,13},{16,18},{17,... | collective-permute-start | bytes 1179656 | tf_op jit(solution)/shard_map/ppermute | solution.py:157
  99.9 1.7 %collective-permute-done.13 = bf16[384,512]{1,0:T(8,128)(2,1)S(1)} collective-permute-done((bf16[384,512]{1,0:T(8,128)(2,1)S(1)}, bf16[384,512]{1,0:T(8,128)(2,1)S(1)}, u32[]{:S(2)}, u32[]{:S(2)}) %collective-permute-start.13) | collective-permute-done | bytes 393248 | tf_op jit(solution)/shard_map/ppermute | solution.py:157
  101.7 6.2 %collective-permute-start.14 = (bf16[384,512]{1,0:T(8,128)(2,1)S(1)}, bf16[384,512]{1,0:T(8,128)(2,1)S(1)}, u32[]{:S(2)}, u32[]{:S(2)}) collective-permute-start(bf16[384,512]{1,0:T(8,128)(2,1)S(1)} %add_convert_fusion.2), channel_id=1, source_target_pairs={{3,10},{7,14},{10,3},{14,7},{17,24},{21,28},{24,17},{28,21}} | collective-permute-start | bytes 1179656 | tf_op jit(solution)/shard_map/ppermute | solution.py:157
  108.8 4.2 %collective-permute-done.20 = bf16[384,512]{1,0:T(8,128)(2,1)S(1)} collective-permute-done((bf16[384,512]{1,0:T(8,128)(2,1)S(1)}, bf16[384,512]{1,0:T(8,128)(2,1)S(1)}, u32[]{:S(2)}, u32[]{:S(2)}) %collective-permute-start.20) | collective-permute-done | bytes 393248 | tf_op jit(solution)/shard_map/ppermute | solution.py:157
  113.1 6.6 %collective-permute-start.21 = (bf16[384,512]{1,0:T(8,128)(2,1)S(1)}, bf16[384,512]{1,0:T(8,128)(2,1)S(1)}, u32[]{:S(2)}, u32[]{:S(2)}) collective-permute-start(bf16[384,512]{1,0:T(8,128)(2,1)S(1)} %add_convert_fusion), channel_id=1, source_target_pairs={{3,10},{7,14},{10,3},{14,7},{17,24},{21,28},{24,17},{28,21}} | collective-permute-start | bytes 1179656 | tf_op jit(solution)/shard_map/ppermute | solution.py:157
  119.9 5.3 %collective-permute-done.21 = bf16[384,512]{1,0:T(8,128)(2,1)S(1)} collective-permute-done((bf16[384,512]{1,0:T(8,128)(2,1)S(1)}, bf16[384,512]{1,0:T(8,128)(2,1)S(1)}, u32[]{:S(2)}, u32[]{:S(2)}) %collective-permute-start.21) | collective-permute-done | bytes 393248 | tf_op jit(solution)/shard_map/ppermute | solution.py:157
  (58 shorter events, 19.4 us)
Async XLA Ops:
  0.0 43.6 %copy-start.1 = (bf16[384,1024]{1,0:T(8,128)(2,1)S(1)}, bf16[384,1024]{1,0:T(8,128)(2,1)}, u32[]{:S(2)}) copy-start(bf16[384,1024]{1,0:T(8,128)(2,1)} %q_ref.5) | copy-start | bytes 2359300
  1.9 12.1 %collective-permute-start = (bf16[384,512]{1,0:T(8,128)(2,1)}, bf16[384,512]{1,0:T(8,128)(2,1)S(1)}, u32[]{:S(2)}, u32[]{:S(2)}) collective-permute-start(bf16[384,512]{1,0:T(8,128)(2,1)} %shard_map.55.refs_0_), channel_id=1, source_target_pairs={{0,8},{1,9},{2,10},{3,11},{4,12},{5,13},{6,14},{7,15},{8,16},{9,17... | collective-permute-start | bytes 1179656 | tf_op jit(solution)/shard_map/ppermute | solution.py:157
  5.1 49.1 %collective-permute-start.4 = (bf16[1024,512]{1,0:T(8,128)(2,1)}, bf16[1024,512]{1,0:T(8,128)(2,1)S(1)}, u32[]{:S(2)}, u32[]{:S(2)}) collective-permute-start(bf16[1024,512]{1,0:T(8,128)(2,1)} %param.9), channel_id=1, source_target_pairs={{0,4},{1,5},{2,6},{3,7},{4,0},{5,1},{6,2},{7,3},{8,12},{9,13},{10,... | collective-permute-start | bytes 3145736 | tf_op jit(solution)/shard_map/ppermute | solution.py:157
  6.3 52.8 %collective-permute-start.9 = (bf16[1024,512]{1,0:T(8,128)(2,1)}, bf16[1024,512]{1,0:T(8,128)(2,1)}, u32[]{:S(2)}, u32[]{:S(2)}) collective-permute-start(bf16[1024,512]{1,0:T(8,128)(2,1)} %param.9), channel_id=1, source_target_pairs={{16,0},{17,1},{18,2},{19,3},{20,4},{21,5},{22,6},{23,7},{24,8},{25... | collective-permute-start | bytes 3145736 | tf_op jit(solution)/shard_map/ppermute | solution.py:157
  13.9 25.6 %collective-permute-start.1 = (bf16[384,512]{1,0:T(8,128)(2,1)S(1)}, bf16[384,512]{1,0:T(8,128)(2,1)S(1)}, u32[]{:S(2)}, u32[]{:S(2)}) collective-permute-start(bf16[384,512]{1,0:T(8,128)(2,1)S(1)} %collective-permute-done.refs_1_), channel_id=1, source_target_pairs={{8,16},{9,17},{10,18},{11,19},{12,20},{13,21},{14,22},{15,23},{16,... | collective-permute-start | bytes 1179656 | tf_op jit(solution)/shard_map/ppermute | solution.py:157
  17.1 20.3 %collective-permute-start.3 = (bf16[384,512]{1,0:T(8,128)(2,1)S(1)}, bf16[384,512]{1,0:T(8,128)(2,1)S(1)}, u32[]{:S(2)}, u32[]{:S(2)}) collective-permute-start(bf16[384,512]{1,0:T(8,128)(2,1)S(1)} %collective-permute-done.refs_1_), channel_id=1, source_target_pairs={{8,12},{9,13},{10,14},{11,15},{12,8},{13,9},{14,10},{15,11},{16,20... | collective-permute-start | bytes 1179656 | tf_op jit(solution)/shard_map/ppermute | solution.py:157
  21.2 37.9 %collective-permute-start.11 = (bf16[1024,512]{1,0:T(8,128)(2,1)}, bf16[1024,512]{1,0:T(8,128)(2,1)}, u32[]{:S(2)}, u32[]{:S(2)}) collective-permute-start(bf16[1024,512]{1,0:T(8,128)(2,1)} %param.9), channel_id=1, source_target_pairs={{8,24},{9,25},{10,26},{11,27},{12,28},{13,29},{14,30},{15,31}} | collective-permute-start | bytes 3145736 | tf_op jit(solution)/shard_map/ppermute | solution.py:157
  38.2 26.0 %collective-permute-start.10 = (bf16[1024,512]{1,0:T(8,128)(2,1)}, bf16[1024,512]{1,0:T(8,128)(2,1)}, u32[]{:S(2)}, u32[]{:S(2)}) collective-permute-start(bf16[1024,512]{1,0:T(8,128)(2,1)} %param.9), channel_id=1, source_target_pairs={{0,16},{1,17},{2,18},{3,19},{4,20},{5,21},{6,22},{7,23}} | collective-permute-start | bytes 3145736 | tf_op jit(solution)/shard_map/ppermute | solution.py:157
  41.3 12.9 %collective-permute-start.2 = (bf16[384,512]{1,0:T(8,128)(2,1)}, bf16[384,512]{1,0:T(8,128)(2,1)S(1)}, u32[]{:S(2)}, u32[]{:S(2)}) collective-permute-start(bf16[384,512]{1,0:T(8,128)(2,1)} %broadcast_select_fusion.2), channel_id=1, source_target_pairs={{0,4},{1,5},{2,6},{3,7},{8,12},{9,13},{10,14},{11,15},{16,20},{17,... | collective-permute-start | bytes 1179656 | tf_op jit(solution)/shard_map/ppermute | solution.py:157
  58.9 17.8 %collective-permute-start.5 = (bf16[384,1024]{1,0:T(8,128)(2,1)S(1)}, bf16[384,1024]{1,0:T(8,128)(2,1)S(1)}, u32[]{:S(2)}, u32[]{:S(2)}) collective-permute-start(bf16[384,1024]{1,0:T(8,128)(2,1)S(1)} %shard_map.58), channel_id=1, source_target_pairs={{0,8},{1,9},{2,10},{3,11},{4,12},{5,13},{6,14},{7,15},{8,0},{9,1},... | collective-permute-start | bytes 2359304 | tf_op jit(solution)/shard_map/ppermute | solution.py:157
  65.6 11.2 %copy-start.4 = (bf16[1024,512]{1,0:T(8,128)(2,1)S(1)}, bf16[1024,512]{1,0:T(8,128)(2,1)}, u32[]{:S(2)}) copy-start(bf16[1024,512]{1,0:T(8,128)(2,1)} %param.9) | copy-start | bytes 3145732
  65.6 25.0 %collective-permute-start.18 = (bf16[1024,512]{1,0:T(8,128)(2,1)S(1)}, bf16[1024,512]{1,0:T(8,128)(2,1)S(1)}, u32[]{:S(2)}, u32[]{:S(2)}) collective-permute-start(bf16[1024,512]{1,0:T(8,128)(2,1)S(1)} %select_select_fusion), channel_id=1, source_target_pairs={{0,4},{1,5},{2,6},{3,7},{4,0},{5,1},{6,2},{7,3},{8,12},{9,13},{10,... | collective-permute-start | bytes 3145736 | tf_op jit(solution)/shard_map/ppermute | solution.py:157
  77.4 7.6 %collective-permute-start.6 = (bf16[384,512]{1,0:T(8,128)(2,1)S(1)}, bf16[384,512]{1,0:T(8,128)(2,1)S(1)}, u32[]{:S(2)}, u32[]{:S(2)}) collective-permute-start(bf16[384,512]{1,0:T(8,128)(2,1)S(1)} %convolution_convert_fusion.3), channel_id=1, source_target_pairs={{0,1},{1,0},{2,3},{3,2},{4,5},{5,4},{6,7},{7,6},{8,9},{9,8},{10,11... | collective-permute-start | bytes 1179656 | tf_op jit(solution)/shard_map/ppermute | solution.py:157
  83.7 5.0 %collective-permute-start.12 = (bf16[384,512]{1,0:T(8,128)(2,1)S(1)}, bf16[384,512]{1,0:T(8,128)(2,1)S(1)}, u32[]{:S(2)}, u32[]{:S(2)}) collective-permute-start(bf16[384,512]{1,0:T(8,128)(2,1)S(1)} %convolution_convert_fusion.2), channel_id=1, source_target_pairs={{0,1},{1,0},{2,3},{3,2},{4,5},{5,4},{6,7},{7,6},{8,9},{9,8},{10,11... | collective-permute-start | bytes 1179656 | tf_op jit(solution)/shard_map/ppermute | solution.py:157
  84.3 7.5 %collective-permute-start.15 = (bf16[384,512]{1,0:T(8,128)(2,1)S(1)}, bf16[384,512]{1,0:T(8,128)(2,1)S(1)}, u32[]{:S(2)}, u32[]{:S(2)}) collective-permute-start(bf16[384,512]{1,0:T(8,128)(2,1)S(1)} %convolution_convert_fusion.1), channel_id=1, source_target_pairs={{0,1},{1,0},{2,3},{3,2},{4,5},{5,4},{6,7},{7,6},{8,9},{9,8},{10,11... | collective-permute-start | bytes 1179656 | tf_op jit(solution)/shard_map/ppermute | solution.py:157
  85.5 11.7 %collective-permute-start.7 = (bf16[384,512]{1,0:T(8,128)(2,1)S(1)}, bf16[384,512]{1,0:T(8,128)(2,1)S(1)}, u32[]{:S(2)}, u32[]{:S(2)}) collective-permute-start(bf16[384,512]{1,0:T(8,128)(2,1)S(1)} %get-tuple-element.25), channel_id=1, source_target_pairs={{2,0},{3,1},{6,4},{7,5},{10,8},{11,9},{14,12},{15,13},{16,18},{17,... | collective-permute-start | bytes 1179656 | tf_op jit(solution)/shard_map/ppermute | solution.py:157
  89.3 12.3 %collective-permute-start.13 = (bf16[384,512]{1,0:T(8,128)(2,1)S(1)}, bf16[384,512]{1,0:T(8,128)(2,1)S(1)}, u32[]{:S(2)}, u32[]{:S(2)}) collective-permute-start(bf16[384,512]{1,0:T(8,128)(2,1)S(1)} %get-tuple-element.23), channel_id=1, source_target_pairs={{0,2},{1,3},{4,6},{5,7},{8,10},{9,11},{12,14},{13,15},{18,16},{19,... | collective-permute-start | bytes 1179656 | tf_op jit(solution)/shard_map/ppermute | solution.py:157
  91.2 6.8 %collective-permute-start.19 = (bf16[384,512]{1,0:T(8,128)(2,1)S(1)}, bf16[384,512]{1,0:T(8,128)(2,1)S(1)}, u32[]{:S(2)}, u32[]{:S(2)}) collective-permute-start(bf16[384,512]{1,0:T(8,128)(2,1)S(1)} %convolution_convert_fusion), channel_id=1, source_target_pairs={{0,1},{1,0},{2,3},{3,2},{4,5},{5,4},{6,7},{7,6},{8,9},{9,8},{10,11... | collective-permute-start | bytes 1179656 | tf_op jit(solution)/shard_map/ppermute | solution.py:157
  92.5 15.5 %collective-permute-start.16 = (bf16[384,512]{1,0:T(8,128)(2,1)S(1)}, bf16[384,512]{1,0:T(8,128)(2,1)S(1)}, u32[]{:S(2)}, u32[]{:S(2)}) collective-permute-start(bf16[384,512]{1,0:T(8,128)(2,1)S(1)} %get-tuple-element.21), channel_id=1, source_target_pairs={{2,0},{3,1},{6,4},{7,5},{10,8},{11,9},{14,12},{15,13},{16,18},{17,... | collective-permute-start | bytes 1179656 | tf_op jit(solution)/shard_map/ppermute | solution.py:157
  97.3 22.5 %collective-permute-start.8 = (bf16[384,512]{1,0:T(8,128)(2,1)S(1)}, bf16[384,512]{1,0:T(8,128)(2,1)S(1)}, u32[]{:S(2)}, u32[]{:S(2)}) collective-permute-start(bf16[384,512]{1,0:T(8,128)(2,1)S(1)} %add_convert_fusion.3), channel_id=1, source_target_pairs={{1,8},{5,12},{8,1},{12,5},{19,26},{23,30},{26,19},{30,23}} | collective-permute-start | bytes 1179656 | tf_op jit(solution)/shard_map/ppermute | solution.py:157
  98.6 14.4 %collective-permute-start.20 = (bf16[384,512]{1,0:T(8,128)(2,1)S(1)}, bf16[384,512]{1,0:T(8,128)(2,1)S(1)}, u32[]{:S(2)}, u32[]{:S(2)}) collective-permute-start(bf16[384,512]{1,0:T(8,128)(2,1)S(1)} %get-tuple-element.19), channel_id=1, source_target_pairs={{0,2},{1,3},{4,6},{5,7},{8,10},{9,11},{12,14},{13,15},{18,16},{19,... | collective-permute-start | bytes 1179656 | tf_op jit(solution)/shard_map/ppermute | solution.py:157
  101.7 18.1 %collective-permute-start.14 = (bf16[384,512]{1,0:T(8,128)(2,1)S(1)}, bf16[384,512]{1,0:T(8,128)(2,1)S(1)}, u32[]{:S(2)}, u32[]{:S(2)}) collective-permute-start(bf16[384,512]{1,0:T(8,128)(2,1)S(1)} %add_convert_fusion.2), channel_id=1, source_target_pairs={{3,10},{7,14},{10,3},{14,7},{17,24},{21,28},{24,17},{28,21}} | collective-permute-start | bytes 1179656 | tf_op jit(solution)/shard_map/ppermute | solution.py:157
  108.1 11.8 %collective-permute-start.17 = (bf16[384,512]{1,0:T(8,128)(2,1)S(1)}, bf16[384,512]{1,0:T(8,128)(2,1)S(1)}, u32[]{:S(2)}, u32[]{:S(2)}) collective-permute-start(bf16[384,512]{1,0:T(8,128)(2,1)S(1)} %add_convert_fusion.1), channel_id=1, source_target_pairs={{1,8},{5,12},{8,1},{12,5},{19,26},{23,30},{26,19},{30,23}} | collective-permute-start | bytes 1179656 | tf_op jit(solution)/shard_map/ppermute | solution.py:157
  113.1 12.1 %collective-permute-start.21 = (bf16[384,512]{1,0:T(8,128)(2,1)S(1)}, bf16[384,512]{1,0:T(8,128)(2,1)S(1)}, u32[]{:S(2)}, u32[]{:S(2)}) collective-permute-start(bf16[384,512]{1,0:T(8,128)(2,1)S(1)} %add_convert_fusion), channel_id=1, source_target_pairs={{3,10},{7,14},{10,3},{14,7},{17,24},{21,28},{24,17},{28,21}} | collective-permute-start | bytes 1179656 | tf_op jit(solution)/shard_map/ppermute | solution.py:157
  (3 other events, 6.2 us)

commit v4 on v3

--- a/solution.py
+++ b/solution.py
@@ -191,10 +191,14 @@
     weight_up = send(late, where=lambda t, h: (t + 4, h) if t in (2, 3) else None)
     later, _ = lax.optimization_barrier((out_weight, back2_side))
     weight_up2 = send(later, where=lambda t, h: (t + 4, h) if t < 2 else None)
-    weight_far = jnp.where(
-        level < 2, weight_down, jnp.where(level == 2, weight_up2, weight_up)
-    )
-    weight_far_side = send(weight_far, where=lambda t, h: (t ^ 1, h))
+    wide = out_weight.shape[1] // 2
+    weight_far, weight_far_side = [], []
+    for c in (slice(0, wide), slice(wide, None)):
+        part = jnp.where(
+            level < 2, weight_down[:, c], jnp.where(level == 2, weight_up2[:, c], weight_up[:, c])
+        )
+        weight_far.append(part)
+        weight_far_side.append(send(part, where=lambda t, h: (t ^ 1, h)))
 
     qpos = tok * rows + jnp.arange(rows, dtype=jnp.int32)
     start = doc_starts(lengths, qpos)[:, None]
@@ -213,8 +217,12 @@
 
     def unit(weight, far_off):
         keeper = lambda t: (t // 4) ^ (1 if far_off else 0)
-        keep = jnp.dot(keep_rows, weight, preferred_element_type=jnp.float32)
-        away = jnp.dot(send_rows, weight, preferred_element_type=jnp.float32).astype(jnp.bfloat16)
+        def product(lines):
+            parts = [jnp.dot(lines, w, preferred_element_type=jnp.float32) for w in weight]
+            return parts[0] if len(parts) == 1 else jnp.concatenate(parts, axis=1)
+
+        keep = product(keep_rows)
+        away = product(send_rows).astype(jnp.bfloat16)
         summed = keep + send(away, where=lambda t, h: (t, h ^ 1))
         low = summed.astype(jnp.bfloat16)
         got = send(low, where=lambda t, h: (t, h ^ 2) if (h // 2) != keeper(t) else None)
@@ -227,10 +235,11 @@
         )
         return jnp.where(mine, total, over)
 
-    near_same = unit(out_weight, False)
-    near_side = unit(weight_side, False)
+    near_same = unit([out_weight], False)
+    near_side = unit([weight_side], False)
     far_same = unit(weight_far, True)
-    far_side = unit(weight_far_side, True)
+    far_side = [unit([w], True) for w in weight_far_side]
+    far_side = jnp.concatenate(far_side, axis=1)
     is_near = half == level // 2
     same = jnp.where(is_near, near_same, far_same)
     other = jnp.where(is_near, near_side, far_side)

time: 127 us -> 122 us (0.961)
  waiting for transfers between devices: 46 us -> 37.5 us
  starting transfers between devices: 51.4 us -> 53.1 us
    ppermute x22 -> x26, waiting for transfers between devices: 46 us -> 37.5 us  [moved(): return lax.ppermute(value, axes, pairs)]
    ppermute x22 -> x26, starting transfers between devices: 51.4 us -> 53.1 us  [moved(): return lax.ppermute(value, axes, pairs)]
    dot_general x8 -> x12, matrix products: 4.62 us -> 5.26 us  [product(): jnp.dot(lines, w, preferred_element_type=jnp.float32)]
  transfers between devices with their start and end apart: 22 -> 26, of which waited for: 8 -> 6; matrix products, arithmetic and copies ran while one was open for 8% -> 9% of each run, Pallas kernels for 11% -> 12%
where the time goes in v4:
time: 122 us; the launch traced here: 121 us
  starting transfers between devices  53.1 us (44%)
  waiting for transfers between devices  37.5 us (31%)
  Pallas kernels  16.1 us (13%)
  other arithmetic  6.85 us (6%)
  matrix products  5.26 us (4%)
  local copies, waits for them, and re-layouts  1.85 us (2%)
    ppermute x26, starting transfers between devices, moved(): return lax.ppermute(value, axes, pairs)  53.1 us
    ppermute x26, waiting for transfers between devices, moved(): return lax.ppermute(value, axes, pairs)  37.5 us
    pallas_call x3, Pallas kernels, attend(): pl.pallas_call(functools.partial(attend_kernel, count, own, resume, last)...  14.2 us
    dot_general x12, matrix products, product(): jnp.dot(lines, w, preferred_element_type=jnp.float32)  5.26 us
  transfers between devices with their start and end apart: 26, of which 6 were waited for; matrix products, arithmetic and copies ran while one was open for 9% of the time, Pallas kernels for 12%

profile of v4, /device:TPU:17, one launch (start us, length us, event | category | flops | bytes accessed | tf_op | source)
XLA Modules:
  0.0 121.1 jit_solution(9291566573982257696)
XLA Ops:
  0.0 1.9 %shard_map.55.refs_0_ = bf16[384,512]{1,0:T(8,128)(2,1)} custom-call(bf16[384,256]{1,0:T(8,128)(2,1)} %left.1, bf16[384,256]{1,0:T(8,128)(2,1)} %right.1), custom_call_target="tpu_custom_call" | custom-call | tf_op jit(solution)/shard_map/pallas_call | solution.py:168
  1.9 3.2 %collective-permute-start = (bf16[384,512]{1,0:T(8,128)(2,1)}, bf16[384,512]{1,0:T(8,128)(2,1)S(1)}, u32[]{:S(2)}, u32[]{:S(2)}) collective-permute-start(bf16[384,512]{1,0:T(8,128)(2,1)} %shard_map.55.refs_0_), channel_id=1, source_target_pairs={{0,8},{1,9},{2,10},{3,11},{4,12},{5,13},{6,14},{7,15},{8,16},{9,17... | collective-permute-start | bytes 1179656 | tf_op jit(solution)/shard_map/ppermute | solution.py:157
  6.3 3.0 %collective-permute-start.9 = (bf16[1024,512]{1,0:T(8,128)(2,1)}, bf16[1024,512]{1,0:T(8,128)(2,1)}, u32[]{:S(2)}, u32[]{:S(2)}) collective-permute-start(bf16[1024,512]{1,0:T(8,128)(2,1)} %param.9), channel_id=1, source_target_pairs={{16,0},{17,1},{18,2},{19,3},{20,4},{21,5},{22,6},{23,7},{24,8},{25... | collective-permute-start | bytes 3145736 | tf_op jit(solution)/shard_map/ppermute | solution.py:157
  9.3 4.6 %collective-permute-done.refs_1_ = bf16[384,512]{1,0:T(8,128)(2,1)S(1)} collective-permute-done((bf16[384,512]{1,0:T(8,128)(2,1)}, bf16[384,512]{1,0:T(8,128)(2,1)S(1)}, u32[]{:S(2)}, u32[]{:S(2)}) %collective-permute-start) | collective-permute-done | bytes 393248 | tf_op jit(solution)/shard_map/ppermute | solution.py:157
  13.9 3.2 %collective-permute-start.1 = (bf16[384,512]{1,0:T(8,128)(2,1)S(1)}, bf16[384,512]{1,0:T(8,128)(2,1)S(1)}, u32[]{:S(2)}, u32[]{:S(2)}) collective-permute-start(bf16[384,512]{1,0:T(8,128)(2,1)S(1)} %collective-permute-done.refs_1_), channel_id=1, source_target_pairs={{8,16},{9,17},{10,18},{11,19},{12,20},{13,21},{14,22},{15,23},{16,... | collective-permute-start | bytes 1179656 | tf_op jit(solution)/shard_map/ppermute | solution.py:157
  17.1 3.1 %collective-permute-start.3 = (bf16[384,512]{1,0:T(8,128)(2,1)S(1)}, bf16[384,512]{1,0:T(8,128)(2,1)S(1)}, u32[]{:S(2)}, u32[]{:S(2)}) collective-permute-start(bf16[384,512]{1,0:T(8,128)(2,1)S(1)} %collective-permute-done.refs_1_), channel_id=1, source_target_pairs={{8,12},{9,13},{10,14},{11,15},{12,8},{13,9},{14,10},{15,11},{16,20... | collective-permute-start | bytes 1179656 | tf_op jit(solution)/shard_map/ppermute | solution.py:157
  21.2 1.6 %collective-permute-start.11 = (bf16[1024,512]{1,0:T(8,128)(2,1)}, bf16[1024,512]{1,0:T(8,128)(2,1)}, u32[]{:S(2)}, u32[]{:S(2)}) collective-permute-start(bf16[1024,512]{1,0:T(8,128)(2,1)} %param.9), channel_id=1, source_target_pairs={{8,24},{9,25},{10,26},{11,27},{12,28},{13,29},{14,30},{15,31}} | collective-permute-start | bytes 3145736 | tf_op jit(solution)/shard_map/ppermute | solution.py:157
  22.9 14.6 %collective-permute-done.3.refs_0_ = bf16[384,512]{1,0:T(8,128)(2,1)S(1)} collective-permute-done((bf16[384,512]{1,0:T(8,128)(2,1)S(1)}, bf16[384,512]{1,0:T(8,128)(2,1)S(1)}, u32[]{:S(2)}, u32[]{:S(2)}) %collective-permute-start.3) | collective-permute-done | bytes 393248 | tf_op jit(solution)/shard_map/ppermute | solution.py:157
  39.5 1.8 %broadcast_select_fusion.2 = bf16[384,512]{1,0:T(8,128)(2,1)} fusion(bf16[384,512]{1,0:T(8,128)(2,1)} %shard_map.55.refs_0_, bf16[384,512]{1,0:T(8,128)(2,1)S(1)} %collective-permute-done.1.refs_1_, pred[]{:T(512)S(6)} %eq.19), kind=kLoop, calls=%fused_computation.27 | loop fusion | flops 196608 | bytes 1179649 | tf_op jit(solution)/shard_map/jit(_where)/select_n | solution.py:188
  41.3 2.1 %collective-permute-start.2 = (bf16[384,512]{1,0:T(8,128)(2,1)}, bf16[384,512]{1,0:T(8,128)(2,1)S(1)}, u32[]{:S(2)}, u32[]{:S(2)}) collective-permute-start(bf16[384,512]{1,0:T(8,128)(2,1)} %broadcast_select_fusion.2), channel_id=1, source_target_pairs={{0,4},{1,5},{2,6},{3,7},{8,12},{9,13},{10,14},{11,15},{16,20},{17,... | collective-permute-start | bytes 1179656 | tf_op jit(solution)/shard_map/ppermute | solution.py:157
  44.7 4.4 %shard_map.56 = (f32[384,2048]{1,0:T(8,128)S(1)}, f32[384,1024]{1,0:T(8,128)S(1)}) custom-call(s32[2]{0:T(128)S(1)} %pad_add_fusion.1.bases, bf16[384,1024]{1,0:T(8,128)(2,1)S(1)} %copy-done.1, s32[384,1]{1,0:T(8,128)S(1)} %broadcast_in_dim.38.start_ref, bf16[384,512]{1,0:T(8,128)(2,1)S(1)} %copy-done, bf16[384,512]{1,0:T(8,128)(2,1)S(1)} %collective-permute-done.refs_1_), custom_call_target="tpu_custom_call" | custom-call | flops 1811939328 | bytes 1572864 | tf_op jit(solution)/shard_map/pallas_call | solution.py:131
  49.1 5.1 %shard_map.57 = (f32[384,2048]{1,0:T(8,128)S(1)}, f32[384,1024]{1,0:T(8,128)S(1)}) custom-call(s32[2]{0:T(128)S(1)} %pad_add_fusion.bases, bf16[384,1024]{1,0:T(8,128)(2,1)S(1)} %copy-done.1, s32[384,1]{1,0:T(8,128)S(1)} %broadcast_in_dim.38.start_ref, bf16[384,512]{1,0:T(8,128)(2,1)S(1)} %copy-done.3, bf16[384,512]{1,0:T(8,128)(2,1)S(1)} %collective-permute-done.1.refs_1_, ...), custom_call_target="tpu_custom_call" | custom-call | flops 1811939328 | bytes 1572864 | tf_op jit(solution)/shard_map/pallas_call | solution.py:131
  54.2 4.7 %shard_map.58 = bf16[384,1024]{1,0:T(8,128)(2,1)S(1)} custom-call(s32[1]{0:T(128)} %bitcast.bases, bf16[384,1024]{1,0:T(8,128)(2,1)S(1)} %copy-done.1, s32[384,1]{1,0:T(8,128)S(1)} %broadcast_in_dim.38.start_ref, bf16[384,512]{1,0:T(8,128)(2,1)S(1)} %collective-permute-done.2.refs_0_, f32[384,2048]{1,0:T(8,128)S(1)} %get-tuple-element.13.refs_1_, ...), custom_call_target="tpu_custom_call" | custom-call | flops 905969664 | bytes 1572864 | tf_op jit(solution)/shard_map/pallas_call | solution.py:131
  59.1 5.1 %collective-permute-done.10 = bf16[1024,512]{1,0:T(8,128)(2,1)} collective-permute-done((bf16[1024,512]{1,0:T(8,128)(2,1)}, bf16[1024,512]{1,0:T(8,128)(2,1)}, u32[]{:S(2)}, u32[]{:S(2)}) %collective-permute-start.10) | collective-permute-done | bytes 1048608 | tf_op jit(solution)/shard_map/ppermute | solution.py:157
  64.2 2.0 %fusion.1 = (bf16[1024,256]{1,0:T(8,128)(2,1)S(1)}, bf16[1024,256]{1,0:T(8,128)(2,1)S(1)}) fusion(bf16[1024,512]{1,0:T(8,128)(2,1)} %collective-permute-done.11, bf16[1024,512]{1,0:T(8,128)(2,1)} %collective-permute-done.10, bf16[1024,512]{1,0:T(8,128)(2,1)} %collective-permute-done.9, pred[]{:T(512)S(6)} %eq.22, pred[]{:T(512)S(6)} %lt.21), kind=kLoop, calls=%fused_computation.20 | loop fusion | flops 1048576 | bytes 4194306 | tf_op jit(solution)/shard_map/jit(_where)/select_n | solution.py:197
  67.7 8.9 %collective-permute-done.5 = bf16[384,1024]{1,0:T(8,128)(2,1)S(1)} collective-permute-done((bf16[384,1024]{1,0:T(8,128)(2,1)S(1)}, bf16[384,1024]{1,0:T(8,128)(2,1)S(1)}, u32[]{:S(2)}, u32[]{:S(2)}) %collective-permute-start.5) | collective-permute-done | bytes 786464 | tf_op jit(solution)/shard_map/ppermute | solution.py:157
  78.0 5.8 %collective-permute-start.6 = (bf16[384,512]{1,0:T(8,128)(2,1)S(1)}, bf16[384,512]{1,0:T(8,128)(2,1)S(1)}, u32[]{:S(2)}, u32[]{:S(2)}) collective-permute-start(bf16[384,512]{1,0:T(8,128)(2,1)S(1)} %convolution_convert_fusion.1), channel_id=1, source_target_pairs={{0,1},{1,0},{2,3},{3,2},{4,5},{5,4},{6,7},{7,6},{8,9},{9,8},{10,11... | collective-permute-start | bytes 1179656 | tf_op jit(solution)/shard_map/ppermute | solution.py:157
  86.4 3.2 %collective-permute-start.7 = (bf16[384,512]{1,0:T(8,128)(2,1)S(1)}, bf16[384,512]{1,0:T(8,128)(2,1)S(1)}, u32[]{:S(2)}, u32[]{:S(2)}) collective-permute-start(bf16[384,512]{1,0:T(8,128)(2,1)S(1)} %get-tuple-element.27), channel_id=1, source_target_pairs={{2,0},{3,1},{6,4},{7,5},{10,8},{11,9},{14,12},{15,13},{16,18},{17,... | collective-permute-start | bytes 1179656 | tf_op jit(solution)/shard_map/ppermute | solution.py:157
  91.6 4.2 %collective-permute-start.16 = (bf16[384,512]{1,0:T(8,128)(2,1)S(1)}, bf16[384,512]{1,0:T(8,128)(2,1)S(1)}, u32[]{:S(2)}, u32[]{:S(2)}) collective-permute-start(bf16[384,512]{1,0:T(8,128)(2,1)S(1)} %get-tuple-element.25), channel_id=1, source_target_pairs={{2,0},{3,1},{6,4},{7,5},{10,8},{11,9},{14,12},{15,13},{16,18},{17,... | collective-permute-start | bytes 1179656 | tf_op jit(solution)/shard_map/ppermute | solution.py:157
  98.6 1.3 %collective-permute-start.20 = (bf16[384,256]{1,0:T(8,128)(2,1)S(1)}, bf16[384,256]{1,0:T(8,128)(2,1)S(1)}, u32[]{:S(2)}, u32[]{:S(2)}) collective-permute-start(bf16[384,256]{1,0:T(8,128)(2,1)S(1)} %get-tuple-element.23), channel_id=1, source_target_pairs={{0,2},{1,3},{4,6},{5,7},{8,10},{9,11},{12,14},{13,15},{18,16},{19,... | collective-permute-start | bytes 589832 | tf_op jit(solution)/shard_map/ppermute | solution.py:157
  102.6 4.7 %collective-permute-start.14 = (bf16[384,512]{1,0:T(8,128)(2,1)S(1)}, bf16[384,512]{1,0:T(8,128)(2,1)S(1)}, u32[]{:S(2)}, u32[]{:S(2)}) collective-permute-start(bf16[384,512]{1,0:T(8,128)(2,1)S(1)} %add_convert_fusion.1), channel_id=1, source_target_pairs={{3,10},{7,14},{10,3},{14,7},{17,24},{21,28},{24,17},{28,21}} | collective-permute-start | bytes 1179656 | tf_op jit(solution)/shard_map/ppermute | solution.py:157
  108.2 4.5 %collective-permute-start.21 = (bf16[384,256]{1,0:T(8,128)(2,1)S(1)}, bf16[384,256]{1,0:T(8,128)(2,1)S(1)}, u32[]{:S(2)}, u32[]{:S(2)}) collective-permute-start(bf16[384,256]{1,0:T(8,128)(2,1)S(1)} %add_convert_fusion.4), channel_id=1, source_target_pairs={{3,10},{7,14},{10,3},{14,7},{17,24},{21,28},{24,17},{28,21}} | collective-permute-start | bytes 589832 | tf_op jit(solution)/shard_map/ppermute | solution.py:157
  112.7 3.3 %collective-permute-start.25 = (bf16[384,256]{1,0:T(8,128)(2,1)S(1)}, bf16[384,256]{1,0:T(8,128)(2,1)S(1)}, u32[]{:S(2)}, u32[]{:S(2)}) collective-permute-start(bf16[384,256]{1,0:T(8,128)(2,1)S(1)} %add_convert_fusion.3), channel_id=1, source_target_pairs={{3,10},{7,14},{10,3},{14,7},{17,24},{21,28},{24,17},{28,21}} | collective-permute-start | bytes 589832 | tf_op jit(solution)/shard_map/ppermute | solution.py:157
  116.1 3.6 %collective-permute-done.25 = bf16[384,256]{1,0:T(8,128)(2,1)S(1)} collective-permute-done((bf16[384,256]{1,0:T(8,128)(2,1)S(1)}, bf16[384,256]{1,0:T(8,128)(2,1)S(1)}, u32[]{:S(2)}, u32[]{:S(2)}) %collective-permute-start.25) | collective-permute-done | bytes 196640 | tf_op jit(solution)/shard_map/ppermute | solution.py:157
  (75 shorter events, 20.8 us)
Async XLA Ops:
  1.9 12.1 %collective-permute-start = (bf16[384,512]{1,0:T(8,128)(2,1)}, bf16[384,512]{1,0:T(8,128)(2,1)S(1)}, u32[]{:S(2)}, u32[]{:S(2)}) collective-permute-start(bf16[384,512]{1,0:T(8,128)(2,1)} %shard_map.55.refs_0_), channel_id=1, source_target_pairs={{0,8},{1,9},{2,10},{3,11},{4,12},{5,13},{6,14},{7,15},{8,16},{9,17... | collective-permute-start | bytes 1179656 | tf_op jit(solution)/shard_map/ppermute | solution.py:157
  5.1 49.1 %collective-permute-start.4 = (bf16[1024,512]{1,0:T(8,128)(2,1)}, bf16[1024,512]{1,0:T(8,128)(2,1)S(1)}, u32[]{:S(2)}, u32[]{:S(2)}) collective-permute-start(bf16[1024,512]{1,0:T(8,128)(2,1)} %param.9), channel_id=1, source_target_pairs={{0,4},{1,5},{2,6},{3,7},{4,0},{5,1},{6,2},{7,3},{8,12},{9,13},{10,... | collective-permute-start | bytes 3145736 | tf_op jit(solution)/shard_map/ppermute | solution.py:157
  6.3 52.7 %collective-permute-start.9 = (bf16[1024,512]{1,0:T(8,128)(2,1)}, bf16[1024,512]{1,0:T(8,128)(2,1)}, u32[]{:S(2)}, u32[]{:S(2)}) collective-permute-start(bf16[1024,512]{1,0:T(8,128)(2,1)} %param.9), channel_id=1, source_target_pairs={{16,0},{17,1},{18,2},{19,3},{20,4},{21,5},{22,6},{23,7},{24,8},{25... | collective-permute-start | bytes 3145736 | tf_op jit(solution)/shard_map/ppermute | solution.py:157
  13.9 25.6 %collective-permute-start.1 = (bf16[384,512]{1,0:T(8,128)(2,1)S(1)}, bf16[384,512]{1,0:T(8,128)(2,1)S(1)}, u32[]{:S(2)}, u32[]{:S(2)}) collective-permute-start(bf16[384,512]{1,0:T(8,128)(2,1)S(1)} %collective-permute-done.refs_1_), channel_id=1, source_target_pairs={{8,16},{9,17},{10,18},{11,19},{12,20},{13,21},{14,22},{15,23},{16,... | collective-permute-start | bytes 1179656 | tf_op jit(solution)/shard_map/ppermute | solution.py:157
  17.1 20.3 %collective-permute-start.3 = (bf16[384,512]{1,0:T(8,128)(2,1)S(1)}, bf16[384,512]{1,0:T(8,128)(2,1)S(1)}, u32[]{:S(2)}, u32[]{:S(2)}) collective-permute-start(bf16[384,512]{1,0:T(8,128)(2,1)S(1)} %collective-permute-done.refs_1_), channel_id=1, source_target_pairs={{8,12},{9,13},{10,14},{11,15},{12,8},{13,9},{14,10},{15,11},{16,20... | collective-permute-start | bytes 1179656 | tf_op jit(solution)/shard_map/ppermute | solution.py:157
  21.2 37.9 %collective-permute-start.11 = (bf16[1024,512]{1,0:T(8,128)(2,1)}, bf16[1024,512]{1,0:T(8,128)(2,1)}, u32[]{:S(2)}, u32[]{:S(2)}) collective-permute-start(bf16[1024,512]{1,0:T(8,128)(2,1)} %param.9), channel_id=1, source_target_pairs={{8,24},{9,25},{10,26},{11,27},{12,28},{13,29},{14,30},{15,31}} | collective-permute-start | bytes 3145736 | tf_op jit(solution)/shard_map/ppermute | solution.py:157
  38.2 26.0 %collective-permute-start.10 = (bf16[1024,512]{1,0:T(8,128)(2,1)}, bf16[1024,512]{1,0:T(8,128)(2,1)}, u32[]{:S(2)}, u32[]{:S(2)}) collective-permute-start(bf16[1024,512]{1,0:T(8,128)(2,1)} %param.9), channel_id=1, source_target_pairs={{0,16},{1,17},{2,18},{3,19},{4,20},{5,21},{6,22},{7,23}} | collective-permute-start | bytes 3145736 | tf_op jit(solution)/shard_map/ppermute | solution.py:157
  41.3 12.9 %collective-permute-start.2 = (bf16[384,512]{1,0:T(8,128)(2,1)}, bf16[384,512]{1,0:T(8,128)(2,1)S(1)}, u32[]{:S(2)}, u32[]{:S(2)}) collective-permute-start(bf16[384,512]{1,0:T(8,128)(2,1)} %broadcast_select_fusion.2), channel_id=1, source_target_pairs={{0,4},{1,5},{2,6},{3,7},{8,12},{9,13},{10,14},{11,15},{16,20},{17,... | collective-permute-start | bytes 1179656 | tf_op jit(solution)/shard_map/ppermute | solution.py:157
  58.9 17.7 %collective-permute-start.5 = (bf16[384,1024]{1,0:T(8,128)(2,1)S(1)}, bf16[384,1024]{1,0:T(8,128)(2,1)S(1)}, u32[]{:S(2)}, u32[]{:S(2)}) collective-permute-start(bf16[384,1024]{1,0:T(8,128)(2,1)S(1)} %shard_map.58), channel_id=1, source_target_pairs={{0,8},{1,9},{2,10},{3,11},{4,12},{5,13},{6,14},{7,15},{8,0},{9,1},... | collective-permute-start | bytes 2359304 | tf_op jit(solution)/shard_map/ppermute | solution.py:157
  66.2 29.6 %collective-permute-start.18 = (bf16[1024,256]{1,0:T(8,128)(2,1)S(1)}, bf16[1024,256]{1,0:T(8,128)(2,1)S(1)}, u32[]{:S(2)}, u32[]{:S(2)}) collective-permute-start(bf16[1024,256]{1,0:T(8,128)(2,1)S(1)} %get-tuple-element.17), channel_id=1, source_target_pairs={{0,4},{1,5},{2,6},{3,7},{4,0},{5,1},{6,2},{7,3},{8,12},{9,13},{10,... | collective-permute-start | bytes 1572872 | tf_op jit(solution)/shard_map/ppermute | solution.py:157
  67.5 29.7 %collective-permute-start.22 = (bf16[1024,256]{1,0:T(8,128)(2,1)S(1)}, bf16[1024,256]{1,0:T(8,128)(2,1)S(1)}, u32[]{:S(2)}, u32[]{:S(2)}) collective-permute-start(bf16[1024,256]{1,0:T(8,128)(2,1)S(1)} %get-tuple-element.18), channel_id=1, source_target_pairs={{0,4},{1,5},{2,6},{3,7},{4,0},{5,1},{6,2},{7,3},{8,12},{9,13},{10,... | collective-permute-start | bytes 1572872 | tf_op jit(solution)/shard_map/ppermute | solution.py:157
  78.0 7.8 %collective-permute-start.6 = (bf16[384,512]{1,0:T(8,128)(2,1)S(1)}, bf16[384,512]{1,0:T(8,128)(2,1)S(1)}, u32[]{:S(2)}, u32[]{:S(2)}) collective-permute-start(bf16[384,512]{1,0:T(8,128)(2,1)S(1)} %convolution_convert_fusion.1), channel_id=1, source_target_pairs={{0,1},{1,0},{2,3},{3,2},{4,5},{5,4},{6,7},{7,6},{8,9},{9,8},{10,11... | collective-permute-start | bytes 1179656 | tf_op jit(solution)/shard_map/ppermute | solution.py:157
  83.8 5.8 %collective-permute-start.12 = (bf16[384,512]{1,0:T(8,128)(2,1)S(1)}, bf16[384,512]{1,0:T(8,128)(2,1)S(1)}, u32[]{:S(2)}, u32[]{:S(2)}) collective-permute-start(bf16[384,512]{1,0:T(8,128)(2,1)S(1)} %pad_maximum_fusion), channel_id=1, source_target_pairs={{0,1},{1,0},{2,3},{3,2},{4,5},{5,4},{6,7},{7,6},{8,9},{9,8},{10,11... | collective-permute-start | bytes 1179656 | tf_op jit(solution)/shard_map/ppermute | solution.py:157
  85.3 5.7 %collective-permute-start.15 = (bf16[384,512]{1,0:T(8,128)(2,1)S(1)}, bf16[384,512]{1,0:T(8,128)(2,1)S(1)}, u32[]{:S(2)}, u32[]{:S(2)}) collective-permute-start(bf16[384,512]{1,0:T(8,128)(2,1)S(1)} %convolution_convert_fusion), channel_id=1, source_target_pairs={{0,1},{1,0},{2,3},{3,2},{4,5},{5,4},{6,7},{7,6},{8,9},{9,8},{10,11... | collective-permute-start | bytes 1179656 | tf_op jit(solution)/shard_map/ppermute | solution.py:157
  86.4 15.2 %collective-permute-start.7 = (bf16[384,512]{1,0:T(8,128)(2,1)S(1)}, bf16[384,512]{1,0:T(8,128)(2,1)S(1)}, u32[]{:S(2)}, u32[]{:S(2)}) collective-permute-start(bf16[384,512]{1,0:T(8,128)(2,1)S(1)} %get-tuple-element.27), channel_id=1, source_target_pairs={{2,0},{3,1},{6,4},{7,5},{10,8},{11,9},{14,12},{15,13},{16,18},{17,... | collective-permute-start | bytes 1179656 | tf_op jit(solution)/shard_map/ppermute | solution.py:157
  89.7 12.7 %collective-permute-start.13 = (bf16[384,512]{1,0:T(8,128)(2,1)S(1)}, bf16[384,512]{1,0:T(8,128)(2,1)S(1)}, u32[]{:S(2)}, u32[]{:S(2)}) collective-permute-start(bf16[384,512]{1,0:T(8,128)(2,1)S(1)} %fusion.2), channel_id=1, source_target_pairs={{0,2},{1,3},{4,6},{5,7},{8,10},{9,11},{12,14},{13,15},{18,16},{19,... | collective-permute-start | bytes 1179656 | tf_op jit(solution)/shard_map/ppermute | solution.py:157
  91.6 15.7 %collective-permute-start.16 = (bf16[384,512]{1,0:T(8,128)(2,1)S(1)}, bf16[384,512]{1,0:T(8,128)(2,1)S(1)}, u32[]{:S(2)}, u32[]{:S(2)}) collective-permute-start(bf16[384,512]{1,0:T(8,128)(2,1)S(1)} %get-tuple-element.25), channel_id=1, source_target_pairs={{2,0},{3,1},{6,4},{7,5},{10,8},{11,9},{14,12},{15,13},{16,18},{17,... | collective-permute-start | bytes 1179656 | tf_op jit(solution)/shard_map/ppermute | solution.py:157
  98.6 9.5 %collective-permute-start.20 = (bf16[384,256]{1,0:T(8,128)(2,1)S(1)}, bf16[384,256]{1,0:T(8,128)(2,1)S(1)}, u32[]{:S(2)}, u32[]{:S(2)}) collective-permute-start(bf16[384,256]{1,0:T(8,128)(2,1)S(1)} %get-tuple-element.23), channel_id=1, source_target_pairs={{0,2},{1,3},{4,6},{5,7},{8,10},{9,11},{12,14},{13,15},{18,16},{19,... | collective-permute-start | bytes 589832 | tf_op jit(solution)/shard_map/ppermute | solution.py:157
  100.3 12.4 %collective-permute-start.24 = (bf16[384,256]{1,0:T(8,128)(2,1)S(1)}, bf16[384,256]{1,0:T(8,128)(2,1)S(1)}, u32[]{:S(2)}, u32[]{:S(2)}) collective-permute-start(bf16[384,256]{1,0:T(8,128)(2,1)S(1)} %get-tuple-element.21), channel_id=1, source_target_pairs={{0,2},{1,3},{4,6},{5,7},{8,10},{9,11},{12,14},{13,15},{18,16},{19,... | collective-permute-start | bytes 589832 | tf_op jit(solution)/shard_map/ppermute | solution.py:157
  101.7 18.0 %collective-permute-start.8 = (bf16[384,512]{1,0:T(8,128)(2,1)S(1)}, bf16[384,512]{1,0:T(8,128)(2,1)S(1)}, u32[]{:S(2)}, u32[]{:S(2)}) collective-permute-start(bf16[384,512]{1,0:T(8,128)(2,1)S(1)} %add_convert_fusion.2), channel_id=1, source_target_pairs={{1,8},{5,12},{8,1},{12,5},{19,26},{23,30},{26,19},{30,23}} | collective-permute-start | bytes 1179656 | tf_op jit(solution)/shard_map/ppermute | solution.py:157
  102.6 17.2 %collective-permute-start.14 = (bf16[384,512]{1,0:T(8,128)(2,1)S(1)}, bf16[384,512]{1,0:T(8,128)(2,1)S(1)}, u32[]{:S(2)}, u32[]{:S(2)}) collective-permute-start(bf16[384,512]{1,0:T(8,128)(2,1)S(1)} %add_convert_fusion.1), channel_id=1, source_target_pairs={{3,10},{7,14},{10,3},{14,7},{17,24},{21,28},{24,17},{28,21}} | collective-permute-start | bytes 1179656 | tf_op jit(solution)/shard_map/ppermute | solution.py:157
  107.4 12.4 %collective-permute-start.17 = (bf16[384,512]{1,0:T(8,128)(2,1)S(1)}, bf16[384,512]{1,0:T(8,128)(2,1)S(1)}, u32[]{:S(2)}, u32[]{:S(2)}) collective-permute-start(bf16[384,512]{1,0:T(8,128)(2,1)S(1)} %add_convert_fusion), channel_id=1, source_target_pairs={{1,8},{5,12},{8,1},{12,5},{19,26},{23,30},{26,19},{30,23}} | collective-permute-start | bytes 1179656 | tf_op jit(solution)/shard_map/ppermute | solution.py:157
  108.2 7.9 %collective-permute-start.21 = (bf16[384,256]{1,0:T(8,128)(2,1)S(1)}, bf16[384,256]{1,0:T(8,128)(2,1)S(1)}, u32[]{:S(2)}, u32[]{:S(2)}) collective-permute-start(bf16[384,256]{1,0:T(8,128)(2,1)S(1)} %add_convert_fusion.4), channel_id=1, source_target_pairs={{3,10},{7,14},{10,3},{14,7},{17,24},{21,28},{24,17},{28,21}} | collective-permute-start | bytes 589832 | tf_op jit(solution)/shard_map/ppermute | solution.py:157
  112.7 7.0 %collective-permute-start.25 = (bf16[384,256]{1,0:T(8,128)(2,1)S(1)}, bf16[384,256]{1,0:T(8,128)(2,1)S(1)}, u32[]{:S(2)}, u32[]{:S(2)}) collective-permute-start(bf16[384,256]{1,0:T(8,128)(2,1)S(1)} %add_convert_fusion.3), channel_id=1, source_target_pairs={{3,10},{7,14},{10,3},{14,7},{17,24},{21,28},{24,17},{28,21}} | collective-permute-start | bytes 589832 | tf_op jit(solution)/shard_map/ppermute | solution.py:157
  (7 other events, 63.4 us)

commit v5 on v4

--- a/solution.py
+++ b/solution.py
@@ -139,7 +139,7 @@
         out_shape=out_shape,
         compiler_params=pltpu.CompilerParams(vmem_limit_bytes=40 * 2**20),
         cost_estimate=pl.CostEstimate(
-            flops=6 * rows * seen * width,
+            flops=12 * rows * seen * width,
             bytes_accessed=4 * rows * width,
             transcendentals=rows * seen * heads,
         ),

time: 122 us -> 120 us (0.984)
  waiting for transfers between devices: 37.5 us -> 27.6 us
  starting transfers between devices: 53.1 us -> 62.1 us
    ppermute x26, waiting for transfers between devices: 37.5 us -> 27.6 us  [moved(): return lax.ppermute(value, axes, pairs)]
    ppermute x26, starting transfers between devices: 53.1 us -> 62.1 us  [moved(): return lax.ppermute(value, axes, pairs)]
where the time goes in v5:
time: 120 us
  starting transfers between devices  62.1 us (52%)
  waiting for transfers between devices  27.6 us (23%)
  Pallas kernels  16 us (13%)
  other arithmetic  6.11 us (5%)
  matrix products  5.26 us (4%)
  local copies, waits for them, and re-layouts  1.95 us (2%)
    ppermute x26, starting transfers between devices, moved(): return lax.ppermute(value, axes, pairs)  62.1 us
    ppermute x26, waiting for transfers between devices, moved(): return lax.ppermute(value, axes, pairs)  27.6 us
    pallas_call x3, Pallas kernels, attend(): pl.pallas_call(functools.partial(attend_kernel, count, own, resume, last)...  14.2 us
    dot_general x12, matrix products, product(): jnp.dot(lines, w, preferred_element_type=jnp.float32)  5.26 us
  transfers between devices with their start and end apart: 26, of which 6 were waited for; matrix products, arithmetic and copies ran while one was open for 9% of the time, Pallas kernels for 12%

profile of v5, /device:TPU:17, one launch (start us, length us, event | category | flops | bytes accessed | tf_op | source)
XLA Modules:
  0.0 119.6 jit_solution(6405737562620713660)
XLA Ops:
  0.0 1.9 %shard_map.55.refs_0_ = bf16[384,512]{1,0:T(8,128)(2,1)} custom-call(bf16[384,256]{1,0:T(8,128)(2,1)} %left.1, bf16[384,256]{1,0:T(8,128)(2,1)} %right.1), custom_call_target="tpu_custom_call" | custom-call | tf_op jit(solution)/shard_map/pallas_call | solution.py:168
  1.9 3.2 %collective-permute-start = (bf16[384,512]{1,0:T(8,128)(2,1)}, bf16[384,512]{1,0:T(8,128)(2,1)S(1)}, u32[]{:S(2)}, u32[]{:S(2)}) collective-permute-start(bf16[384,512]{1,0:T(8,128)(2,1)} %shard_map.55.refs_0_), channel_id=1, source_target_pairs={{0,8},{1,9},{2,10},{3,11},{4,12},{5,13},{6,14},{7,15},{8,16},{9,17... | collective-permute-start | bytes 1179656 | tf_op jit(solution)/shard_map/ppermute | solution.py:157
  6.3 3.0 %collective-permute-start.9 = (bf16[1024,512]{1,0:T(8,128)(2,1)}, bf16[1024,512]{1,0:T(8,128)(2,1)}, u32[]{:S(2)}, u32[]{:S(2)}) collective-permute-start(bf16[1024,512]{1,0:T(8,128)(2,1)} %param.9), channel_id=1, source_target_pairs={{16,0},{17,1},{18,2},{19,3},{20,4},{21,5},{22,6},{23,7},{24,8},{25... | collective-permute-start | bytes 3145736 | tf_op jit(solution)/shard_map/ppermute | solution.py:157
  10.1 3.9 %collective-permute-done.refs_1_ = bf16[384,512]{1,0:T(8,128)(2,1)S(1)} collective-permute-done((bf16[384,512]{1,0:T(8,128)(2,1)}, bf16[384,512]{1,0:T(8,128)(2,1)S(1)}, u32[]{:S(2)}, u32[]{:S(2)}) %collective-permute-start) | collective-permute-done | bytes 393248 | tf_op jit(solution)/shard_map/ppermute | solution.py:157
  13.9 3.2 %collective-permute-start.1 = (bf16[384,512]{1,0:T(8,128)(2,1)S(1)}, bf16[384,512]{1,0:T(8,128)(2,1)S(1)}, u32[]{:S(2)}, u32[]{:S(2)}) collective-permute-start(bf16[384,512]{1,0:T(8,128)(2,1)S(1)} %collective-permute-done.refs_1_), channel_id=1, source_target_pairs={{8,16},{9,17},{10,18},{11,19},{12,20},{13,21},{14,22},{15,23},{16,... | collective-permute-start | bytes 1179656 | tf_op jit(solution)/shard_map/ppermute | solution.py:157
  17.3 3.1 %collective-permute-start.3 = (bf16[384,512]{1,0:T(8,128)(2,1)S(1)}, bf16[384,512]{1,0:T(8,128)(2,1)S(1)}, u32[]{:S(2)}, u32[]{:S(2)}) collective-permute-start(bf16[384,512]{1,0:T(8,128)(2,1)S(1)} %collective-permute-done.refs_1_), channel_id=1, source_target_pairs={{8,12},{9,13},{10,14},{11,15},{12,8},{13,9},{14,10},{15,11},{16,20... | collective-permute-start | bytes 1179656 | tf_op jit(solution)/shard_map/ppermute | solution.py:157
  20.7 1.6 %collective-permute-start.11 = (bf16[1024,512]{1,0:T(8,128)(2,1)}, bf16[1024,512]{1,0:T(8,128)(2,1)}, u32[]{:S(2)}, u32[]{:S(2)}) collective-permute-start(bf16[1024,512]{1,0:T(8,128)(2,1)} %param.9), channel_id=1, source_target_pairs={{8,24},{9,25},{10,26},{11,27},{12,28},{13,29},{14,30},{15,31}} | collective-permute-start | bytes 3145736 | tf_op jit(solution)/shard_map/ppermute | solution.py:157
  22.3 2.6 %collective-permute-done.1.refs_1_ = bf16[384,512]{1,0:T(8,128)(2,1)S(1)} collective-permute-done((bf16[384,512]{1,0:T(8,128)(2,1)S(1)}, bf16[384,512]{1,0:T(8,128)(2,1)S(1)}, u32[]{:S(2)}, u32[]{:S(2)}) %collective-permute-start.1) | collective-permute-done | bytes 393248 | tf_op jit(solution)/shard_map/ppermute | solution.py:157
  25.9 2.1 %collective-permute-start.2 = (bf16[384,512]{1,0:T(8,128)(2,1)S(1)}, bf16[384,512]{1,0:T(8,128)(2,1)S(1)}, u32[]{:S(2)}, u32[]{:S(2)}) collective-permute-start(bf16[384,512]{1,0:T(8,128)(2,1)S(1)} %broadcast_select_fusion.2), channel_id=1, source_target_pairs={{0,4},{1,5},{2,6},{3,7},{8,12},{9,13},{10,14},{11,15},{16,20},{17,... | collective-permute-start | bytes 1179656 | tf_op jit(solution)/shard_map/ppermute | solution.py:157
  28.1 9.4 %collective-permute-done.3.refs_0_ = bf16[384,512]{1,0:T(8,128)(2,1)S(1)} collective-permute-done((bf16[384,512]{1,0:T(8,128)(2,1)S(1)}, bf16[384,512]{1,0:T(8,128)(2,1)S(1)}, u32[]{:S(2)}, u32[]{:S(2)}) %collective-permute-start.3) | collective-permute-done | bytes 393248 | tf_op jit(solution)/shard_map/ppermute | solution.py:157
  39.8 4.4 %shard_map.56 = (f32[384,2048]{1,0:T(8,128)S(1)}, f32[384,1024]{1,0:T(8,128)S(1)}) custom-call(s32[2]{0:T(128)S(1)} %pad_add_fusion.1.bases, bf16[384,1024]{1,0:T(8,128)(2,1)S(1)} %copy-done.1, s32[384,1]{1,0:T(8,128)S(1)} %broadcast_in_dim.38.start_ref, bf16[384,512]{1,0:T(8,128)(2,1)S(1)} %copy-done, bf16[384,512]{1,0:T(8,128)(2,1)S(1)} %collective-permute-done.refs_1_), custom_call_target="tpu_custom_call" | custom-call | flops 3623878656 | bytes 1572864 | tf_op jit(solution)/shard_map/pallas_call | solution.py:131
  44.2 5.1 %shard_map.57 = (f32[384,2048]{1,0:T(8,128)S(1)}, f32[384,1024]{1,0:T(8,128)S(1)}) custom-call(s32[2]{0:T(128)S(1)} %pad_add_fusion.bases, bf16[384,1024]{1,0:T(8,128)(2,1)S(1)} %copy-done.1, s32[384,1]{1,0:T(8,128)S(1)} %broadcast_in_dim.38.start_ref, bf16[384,512]{1,0:T(8,128)(2,1)S(1)} %collective-permute-done.3.refs_0_, ...), custom_call_target="tpu_custom_call" | custom-call | flops 3623878656 | bytes 1572864 | tf_op jit(solution)/shard_map/pallas_call | solution.py:131
  49.3 4.7 %shard_map.58 = bf16[384,1024]{1,0:T(8,128)(2,1)S(1)} custom-call(s32[1]{0:T(128)} %bitcast.bases, bf16[384,1024]{1,0:T(8,128)(2,1)S(1)} %copy-done.1, s32[384,1]{1,0:T(8,128)S(1)} %broadcast_in_dim.38.start_ref, bf16[384,512]{1,0:T(8,128)(2,1)S(1)} %collective-permute-done.2.refs_0_, f32[384,2048]{1,0:T(8,128)S(1)} %get-tuple-element.13.refs_1_, ...), custom_call_target="tpu_custom_call" | custom-call | flops 1811939328 | bytes 1572864 | tf_op jit(solution)/shard_map/pallas_call | solution.py:131
  54.2 7.8 %collective-permute-done.10 = bf16[1024,512]{1,0:T(8,128)(2,1)} collective-permute-done((bf16[1024,512]{1,0:T(8,128)(2,1)}, bf16[1024,512]{1,0:T(8,128)(2,1)}, u32[]{:S(2)}, u32[]{:S(2)}) %collective-permute-start.10) | collective-permute-done | bytes 1048608 | tf_op jit(solution)/shard_map/ppermute | solution.py:157
  62.0 2.0 %fusion.1 = (bf16[1024,256]{1,0:T(8,128)(2,1)S(1)}, bf16[1024,256]{1,0:T(8,128)(2,1)S(1)}) fusion(bf16[1024,512]{1,0:T(8,128)(2,1)} %collective-permute-done.11, bf16[1024,512]{1,0:T(8,128)(2,1)} %collective-permute-done.10, bf16[1024,512]{1,0:T(8,128)(2,1)} %collective-permute-done.9, pred[]{:T(512)S(6)} %eq.22, pred[]{:T(512)S(6)} %lt.21), kind=kLoop, calls=%fused_computation.20 | loop fusion | flops 1048576 | bytes 4194306 | tf_op jit(solution)/shard_map/jit(_where)/select_n | solution.py:197
  67.8 12.4 %collective-permute-start.6 = (bf16[384,512]{1,0:T(8,128)(2,1)S(1)}, bf16[384,512]{1,0:T(8,128)(2,1)S(1)}, u32[]{:S(2)}, u32[]{:S(2)}) collective-permute-start(bf16[384,512]{1,0:T(8,128)(2,1)S(1)} %convolution_convert_fusion.1), channel_id=1, source_target_pairs={{0,1},{1,0},{2,3},{3,2},{4,5},{5,4},{6,7},{7,6},{8,9},{9,8},{10,11... | collective-permute-start | bytes 1179656 | tf_op jit(solution)/shard_map/ppermute | solution.py:157
  82.8 3.2 %collective-permute-start.7 = (bf16[384,512]{1,0:T(8,128)(2,1)S(1)}, bf16[384,512]{1,0:T(8,128)(2,1)S(1)}, u32[]{:S(2)}, u32[]{:S(2)}) collective-permute-start(bf16[384,512]{1,0:T(8,128)(2,1)S(1)} %get-tuple-element.27), channel_id=1, source_target_pairs={{2,0},{3,1},{6,4},{7,5},{10,8},{11,9},{14,12},{15,13},{16,18},{17,... | collective-permute-start | bytes 1179656 | tf_op jit(solution)/shard_map/ppermute | solution.py:157
  86.0 1.3 %collective-permute-start.13 = (bf16[384,512]{1,0:T(8,128)(2,1)S(1)}, bf16[384,512]{1,0:T(8,128)(2,1)S(1)}, u32[]{:S(2)}, u32[]{:S(2)}) collective-permute-start(bf16[384,512]{1,0:T(8,128)(2,1)S(1)} %fusion.2), channel_id=1, source_target_pairs={{0,2},{1,3},{4,6},{5,7},{8,10},{9,11},{12,14},{13,15},{18,16},{19,... | collective-permute-start | bytes 1179656 | tf_op jit(solution)/shard_map/ppermute | solution.py:157
  87.9 4.2 %collective-permute-start.16 = (bf16[384,512]{1,0:T(8,128)(2,1)S(1)}, bf16[384,512]{1,0:T(8,128)(2,1)S(1)}, u32[]{:S(2)}, u32[]{:S(2)}) collective-permute-start(bf16[384,512]{1,0:T(8,128)(2,1)S(1)} %get-tuple-element.25), channel_id=1, source_target_pairs={{2,0},{3,1},{6,4},{7,5},{10,8},{11,9},{14,12},{15,13},{16,18},{17,... | collective-permute-start | bytes 1179656 | tf_op jit(solution)/shard_map/ppermute | solution.py:157
  94.9 1.3 %collective-permute-start.20 = (bf16[384,256]{1,0:T(8,128)(2,1)S(1)}, bf16[384,256]{1,0:T(8,128)(2,1)S(1)}, u32[]{:S(2)}, u32[]{:S(2)}) collective-permute-start(bf16[384,256]{1,0:T(8,128)(2,1)S(1)} %get-tuple-element.23), channel_id=1, source_target_pairs={{0,2},{1,3},{4,6},{5,7},{8,10},{9,11},{12,14},{13,15},{18,16},{19,... | collective-permute-start | bytes 589832 | tf_op jit(solution)/shard_map/ppermute | solution.py:157
  98.9 6.5 %collective-permute-start.14 = (bf16[384,512]{1,0:T(8,128)(2,1)S(1)}, bf16[384,512]{1,0:T(8,128)(2,1)S(1)}, u32[]{:S(2)}, u32[]{:S(2)}) collective-permute-start(bf16[384,512]{1,0:T(8,128)(2,1)S(1)} %add_convert_fusion.1), channel_id=1, source_target_pairs={{3,10},{7,14},{10,3},{14,7},{17,24},{21,28},{24,17},{28,21}} | collective-permute-start | bytes 1179656 | tf_op jit(solution)/shard_map/ppermute | solution.py:157
  106.3 4.7 %collective-permute-start.21 = (bf16[384,256]{1,0:T(8,128)(2,1)S(1)}, bf16[384,256]{1,0:T(8,128)(2,1)S(1)}, u32[]{:S(2)}, u32[]{:S(2)}) collective-permute-start(bf16[384,256]{1,0:T(8,128)(2,1)S(1)} %add_convert_fusion.4), channel_id=1, source_target_pairs={{3,10},{7,14},{10,3},{14,7},{17,24},{21,28},{24,17},{28,21}} | collective-permute-start | bytes 589832 | tf_op jit(solution)/shard_map/ppermute | solution.py:157
  111.1 3.7 %collective-permute-start.25 = (bf16[384,256]{1,0:T(8,128)(2,1)S(1)}, bf16[384,256]{1,0:T(8,128)(2,1)S(1)}, u32[]{:S(2)}, u32[]{:S(2)}) collective-permute-start(bf16[384,256]{1,0:T(8,128)(2,1)S(1)} %add_convert_fusion.3), channel_id=1, source_target_pairs={{3,10},{7,14},{10,3},{14,7},{17,24},{21,28},{24,17},{28,21}} | collective-permute-start | bytes 589832 | tf_op jit(solution)/shard_map/ppermute | solution.py:157
  114.9 3.3 %collective-permute-done.25 = bf16[384,256]{1,0:T(8,128)(2,1)S(1)} collective-permute-done((bf16[384,256]{1,0:T(8,128)(2,1)S(1)}, bf16[384,256]{1,0:T(8,128)(2,1)S(1)}, u32[]{:S(2)}, u32[]{:S(2)}) %collective-permute-start.25) | collective-permute-done | bytes 196640 | tf_op jit(solution)/shard_map/ppermute | solution.py:157
  (71 shorter events, 20.6 us)
Async XLA Ops:
  1.9 12.1 %collective-permute-start = (bf16[384,512]{1,0:T(8,128)(2,1)}, bf16[384,512]{1,0:T(8,128)(2,1)S(1)}, u32[]{:S(2)}, u32[]{:S(2)}) collective-permute-start(bf16[384,512]{1,0:T(8,128)(2,1)} %shard_map.55.refs_0_), channel_id=1, source_target_pairs={{0,8},{1,9},{2,10},{3,11},{4,12},{5,13},{6,14},{7,15},{8,16},{9,17... | collective-permute-start | bytes 1179656 | tf_op jit(solution)/shard_map/ppermute | solution.py:157
  5.1 44.2 %collective-permute-start.4 = (bf16[1024,512]{1,0:T(8,128)(2,1)}, bf16[1024,512]{1,0:T(8,128)(2,1)S(1)}, u32[]{:S(2)}, u32[]{:S(2)}) collective-permute-start(bf16[1024,512]{1,0:T(8,128)(2,1)} %param.9), channel_id=1, source_target_pairs={{0,4},{1,5},{2,6},{3,7},{4,0},{5,1},{6,2},{7,3},{8,12},{9,13},{10,... | collective-permute-start | bytes 3145736 | tf_op jit(solution)/shard_map/ppermute | solution.py:157
  6.3 47.9 %collective-permute-start.9 = (bf16[1024,512]{1,0:T(8,128)(2,1)}, bf16[1024,512]{1,0:T(8,128)(2,1)}, u32[]{:S(2)}, u32[]{:S(2)}) collective-permute-start(bf16[1024,512]{1,0:T(8,128)(2,1)} %param.9), channel_id=1, source_target_pairs={{16,0},{17,1},{18,2},{19,3},{20,4},{21,5},{22,6},{23,7},{24,8},{25... | collective-permute-start | bytes 3145736 | tf_op jit(solution)/shard_map/ppermute | solution.py:157
  13.9 10.9 %collective-permute-start.1 = (bf16[384,512]{1,0:T(8,128)(2,1)S(1)}, bf16[384,512]{1,0:T(8,128)(2,1)S(1)}, u32[]{:S(2)}, u32[]{:S(2)}) collective-permute-start(bf16[384,512]{1,0:T(8,128)(2,1)S(1)} %collective-permute-done.refs_1_), channel_id=1, source_target_pairs={{8,16},{9,17},{10,18},{11,19},{12,20},{13,21},{14,22},{15,23},{16,... | collective-permute-start | bytes 1179656 | tf_op jit(solution)/shard_map/ppermute | solution.py:157
  17.3 20.2 %collective-permute-start.3 = (bf16[384,512]{1,0:T(8,128)(2,1)S(1)}, bf16[384,512]{1,0:T(8,128)(2,1)S(1)}, u32[]{:S(2)}, u32[]{:S(2)}) collective-permute-start(bf16[384,512]{1,0:T(8,128)(2,1)S(1)} %collective-permute-done.refs_1_), channel_id=1, source_target_pairs={{8,12},{9,13},{10,14},{11,15},{12,8},{13,9},{14,10},{15,11},{16,20... | collective-permute-start | bytes 1179656 | tf_op jit(solution)/shard_map/ppermute | solution.py:157
  20.7 33.5 %collective-permute-start.11 = (bf16[1024,512]{1,0:T(8,128)(2,1)}, bf16[1024,512]{1,0:T(8,128)(2,1)}, u32[]{:S(2)}, u32[]{:S(2)}) collective-permute-start(bf16[1024,512]{1,0:T(8,128)(2,1)} %param.9), channel_id=1, source_target_pairs={{8,24},{9,25},{10,26},{11,27},{12,28},{13,29},{14,30},{15,31}} | collective-permute-start | bytes 3145736 | tf_op jit(solution)/shard_map/ppermute | solution.py:157
  25.9 23.3 %collective-permute-start.2 = (bf16[384,512]{1,0:T(8,128)(2,1)S(1)}, bf16[384,512]{1,0:T(8,128)(2,1)S(1)}, u32[]{:S(2)}, u32[]{:S(2)}) collective-permute-start(bf16[384,512]{1,0:T(8,128)(2,1)S(1)} %broadcast_select_fusion.2), channel_id=1, source_target_pairs={{0,4},{1,5},{2,6},{3,7},{8,12},{9,13},{10,14},{11,15},{16,20},{17,... | collective-permute-start | bytes 1179656 | tf_op jit(solution)/shard_map/ppermute | solution.py:157
  37.5 24.5 %collective-permute-start.10 = (bf16[1024,512]{1,0:T(8,128)(2,1)}, bf16[1024,512]{1,0:T(8,128)(2,1)}, u32[]{:S(2)}, u32[]{:S(2)}) collective-permute-start(bf16[1024,512]{1,0:T(8,128)(2,1)} %param.9), channel_id=1, source_target_pairs={{0,16},{1,17},{2,18},{3,19},{4,20},{5,21},{6,22},{7,23}} | collective-permute-start | bytes 3145736 | tf_op jit(solution)/shard_map/ppermute | solution.py:157
  54.0 11.5 %collective-permute-start.5 = (bf16[384,1024]{1,0:T(8,128)(2,1)S(1)}, bf16[384,1024]{1,0:T(8,128)(2,1)S(1)}, u32[]{:S(2)}, u32[]{:S(2)}) collective-permute-start(bf16[384,1024]{1,0:T(8,128)(2,1)S(1)} %shard_map.58), channel_id=1, source_target_pairs={{0,8},{1,9},{2,10},{3,11},{4,12},{5,13},{6,14},{7,15},{8,0},{9,1},... | collective-permute-start | bytes 2359304 | tf_op jit(solution)/shard_map/ppermute | solution.py:157
  64.0 28.2 %collective-permute-start.18 = (bf16[1024,256]{1,0:T(8,128)(2,1)S(1)}, bf16[1024,256]{1,0:T(8,128)(2,1)S(1)}, u32[]{:S(2)}, u32[]{:S(2)}) collective-permute-start(bf16[1024,256]{1,0:T(8,128)(2,1)S(1)} %get-tuple-element.17), channel_id=1, source_target_pairs={{0,4},{1,5},{2,6},{3,7},{4,0},{5,1},{6,2},{7,3},{8,12},{9,13},{10,... | collective-permute-start | bytes 1572872 | tf_op jit(solution)/shard_map/ppermute | solution.py:157
  65.2 28.2 %collective-permute-start.22 = (bf16[1024,256]{1,0:T(8,128)(2,1)S(1)}, bf16[1024,256]{1,0:T(8,128)(2,1)S(1)}, u32[]{:S(2)}, u32[]{:S(2)}) collective-permute-start(bf16[1024,256]{1,0:T(8,128)(2,1)S(1)} %get-tuple-element.18), channel_id=1, source_target_pairs={{0,4},{1,5},{2,6},{3,7},{4,0},{5,1},{6,2},{7,3},{8,12},{9,13},{10,... | collective-permute-start | bytes 1572872 | tf_op jit(solution)/shard_map/ppermute | solution.py:157
  67.8 14.4 %collective-permute-start.6 = (bf16[384,512]{1,0:T(8,128)(2,1)S(1)}, bf16[384,512]{1,0:T(8,128)(2,1)S(1)}, u32[]{:S(2)}, u32[]{:S(2)}) collective-permute-start(bf16[384,512]{1,0:T(8,128)(2,1)S(1)} %convolution_convert_fusion.1), channel_id=1, source_target_pairs={{0,1},{1,0},{2,3},{3,2},{4,5},{5,4},{6,7},{7,6},{8,9},{9,8},{10,11... | collective-permute-start | bytes 1179656 | tf_op jit(solution)/shard_map/ppermute | solution.py:157
  80.2 5.7 %collective-permute-start.12 = (bf16[384,512]{1,0:T(8,128)(2,1)S(1)}, bf16[384,512]{1,0:T(8,128)(2,1)S(1)}, u32[]{:S(2)}, u32[]{:S(2)}) collective-permute-start(bf16[384,512]{1,0:T(8,128)(2,1)S(1)} %pad_maximum_fusion), channel_id=1, source_target_pairs={{0,1},{1,0},{2,3},{3,2},{4,5},{5,4},{6,7},{7,6},{8,9},{9,8},{10,11... | collective-permute-start | bytes 1179656 | tf_op jit(solution)/shard_map/ppermute | solution.py:157
  81.6 5.7 %collective-permute-start.15 = (bf16[384,512]{1,0:T(8,128)(2,1)S(1)}, bf16[384,512]{1,0:T(8,128)(2,1)S(1)}, u32[]{:S(2)}, u32[]{:S(2)}) collective-permute-start(bf16[384,512]{1,0:T(8,128)(2,1)S(1)} %convolution_convert_fusion), channel_id=1, source_target_pairs={{0,1},{1,0},{2,3},{3,2},{4,5},{5,4},{6,7},{7,6},{8,9},{9,8},{10,11... | collective-permute-start | bytes 1179656 | tf_op jit(solution)/shard_map/ppermute | solution.py:157
  82.8 15.2 %collective-permute-start.7 = (bf16[384,512]{1,0:T(8,128)(2,1)S(1)}, bf16[384,512]{1,0:T(8,128)(2,1)S(1)}, u32[]{:S(2)}, u32[]{:S(2)}) collective-permute-start(bf16[384,512]{1,0:T(8,128)(2,1)S(1)} %get-tuple-element.27), channel_id=1, source_target_pairs={{2,0},{3,1},{6,4},{7,5},{10,8},{11,9},{14,12},{15,13},{16,18},{17,... | collective-permute-start | bytes 1179656 | tf_op jit(solution)/shard_map/ppermute | solution.py:157
  86.0 12.7 %collective-permute-start.13 = (bf16[384,512]{1,0:T(8,128)(2,1)S(1)}, bf16[384,512]{1,0:T(8,128)(2,1)S(1)}, u32[]{:S(2)}, u32[]{:S(2)}) collective-permute-start(bf16[384,512]{1,0:T(8,128)(2,1)S(1)} %fusion.2), channel_id=1, source_target_pairs={{0,2},{1,3},{4,6},{5,7},{8,10},{9,11},{12,14},{13,15},{18,16},{19,... | collective-permute-start | bytes 1179656 | tf_op jit(solution)/shard_map/ppermute | solution.py:157
  87.9 17.5 %collective-permute-start.16 = (bf16[384,512]{1,0:T(8,128)(2,1)S(1)}, bf16[384,512]{1,0:T(8,128)(2,1)S(1)}, u32[]{:S(2)}, u32[]{:S(2)}) collective-permute-start(bf16[384,512]{1,0:T(8,128)(2,1)S(1)} %get-tuple-element.25), channel_id=1, source_target_pairs={{2,0},{3,1},{6,4},{7,5},{10,8},{11,9},{14,12},{15,13},{16,18},{17,... | collective-permute-start | bytes 1179656 | tf_op jit(solution)/shard_map/ppermute | solution.py:157
  94.9 11.3 %collective-permute-start.20 = (bf16[384,256]{1,0:T(8,128)(2,1)S(1)}, bf16[384,256]{1,0:T(8,128)(2,1)S(1)}, u32[]{:S(2)}, u32[]{:S(2)}) collective-permute-start(bf16[384,256]{1,0:T(8,128)(2,1)S(1)} %get-tuple-element.23), channel_id=1, source_target_pairs={{0,2},{1,3},{4,6},{5,7},{8,10},{9,11},{12,14},{13,15},{18,16},{19,... | collective-permute-start | bytes 589832 | tf_op jit(solution)/shard_map/ppermute | solution.py:157
  96.6 14.5 %collective-permute-start.24 = (bf16[384,256]{1,0:T(8,128)(2,1)S(1)}, bf16[384,256]{1,0:T(8,128)(2,1)S(1)}, u32[]{:S(2)}, u32[]{:S(2)}) collective-permute-start(bf16[384,256]{1,0:T(8,128)(2,1)S(1)} %get-tuple-element.21), channel_id=1, source_target_pairs={{0,2},{1,3},{4,6},{5,7},{8,10},{9,11},{12,14},{13,15},{18,16},{19,... | collective-permute-start | bytes 589832 | tf_op jit(solution)/shard_map/ppermute | solution.py:157
  98.1 20.2 %collective-permute-start.8 = (bf16[384,512]{1,0:T(8,128)(2,1)S(1)}, bf16[384,512]{1,0:T(8,128)(2,1)S(1)}, u32[]{:S(2)}, u32[]{:S(2)}) collective-permute-start(bf16[384,512]{1,0:T(8,128)(2,1)S(1)} %add_convert_fusion.2), channel_id=1, source_target_pairs={{1,8},{5,12},{8,1},{12,5},{19,26},{23,30},{26,19},{30,23}} | collective-permute-start | bytes 1179656 | tf_op jit(solution)/shard_map/ppermute | solution.py:157
  98.9 19.3 %collective-permute-start.14 = (bf16[384,512]{1,0:T(8,128)(2,1)S(1)}, bf16[384,512]{1,0:T(8,128)(2,1)S(1)}, u32[]{:S(2)}, u32[]{:S(2)}) collective-permute-start(bf16[384,512]{1,0:T(8,128)(2,1)S(1)} %add_convert_fusion.1), channel_id=1, source_target_pairs={{3,10},{7,14},{10,3},{14,7},{17,24},{21,28},{24,17},{28,21}} | collective-permute-start | bytes 1179656 | tf_op jit(solution)/shard_map/ppermute | solution.py:157
  105.6 12.8 %collective-permute-start.17 = (bf16[384,512]{1,0:T(8,128)(2,1)S(1)}, bf16[384,512]{1,0:T(8,128)(2,1)S(1)}, u32[]{:S(2)}, u32[]{:S(2)}) collective-permute-start(bf16[384,512]{1,0:T(8,128)(2,1)S(1)} %add_convert_fusion), channel_id=1, source_target_pairs={{1,8},{5,12},{8,1},{12,5},{19,26},{23,30},{26,19},{30,23}} | collective-permute-start | bytes 1179656 | tf_op jit(solution)/shard_map/ppermute | solution.py:157
  106.3 8.6 %collective-permute-start.21 = (bf16[384,256]{1,0:T(8,128)(2,1)S(1)}, bf16[384,256]{1,0:T(8,128)(2,1)S(1)}, u32[]{:S(2)}, u32[]{:S(2)}) collective-permute-start(bf16[384,256]{1,0:T(8,128)(2,1)S(1)} %add_convert_fusion.4), channel_id=1, source_target_pairs={{3,10},{7,14},{10,3},{14,7},{17,24},{21,28},{24,17},{28,21}} | collective-permute-start | bytes 589832 | tf_op jit(solution)/shard_map/ppermute | solution.py:157
  111.1 7.1 %collective-permute-start.25 = (bf16[384,256]{1,0:T(8,128)(2,1)S(1)}, bf16[384,256]{1,0:T(8,128)(2,1)S(1)}, u32[]{:S(2)}, u32[]{:S(2)}) collective-permute-start(bf16[384,256]{1,0:T(8,128)(2,1)S(1)} %add_convert_fusion.3), channel_id=1, source_target_pairs={{3,10},{7,14},{10,3},{14,7},{17,24},{21,28},{24,17},{28,21}} | collective-permute-start | bytes 589832 | tf_op jit(solution)/shard_map/ppermute | solution.py:157
  (5 other events, 45.4 us)

commit v6 on v5

--- a/solution.py
+++ b/solution.py
@@ -14,7 +14,7 @@
 RATIO = QH // KVH
 SCALE = 1.0 / HD**0.5
 LOW = -1e30
-STACK = 2
+STACK = 1
 
 
 def doc_ends(lengths):
@@ -235,9 +235,9 @@
         )
         return jnp.where(mine, total, over)
 
+    far_same = unit(weight_far, True)
     near_same = unit([out_weight], False)
     near_side = unit([weight_side], False)
-    far_same = unit(weight_far, True)
     far_side = [unit([w], True) for w in weight_far_side]
     far_side = jnp.concatenate(far_side, axis=1)
     is_near = half == level // 2

time: 120 us -> 120 us (level)
  transfers between devices with their start and end apart: 26 -> 26, of which waited for: 6 -> 7; matrix products, arithmetic and copies ran while one was open for 9% -> 9% of each run, Pallas kernels for 12% -> 13%
where the time goes in v6:
time: 120 us
  starting transfers between devices  61 us (51%)
  waiting for transfers between devices  28.4 us (24%)
  Pallas kernels  17.2 us (14%)
  other arithmetic  6.11 us (5%)
  matrix products  5.27 us (4%)
    ppermute x26, starting transfers between devices, moved(): return lax.ppermute(value, axes, pairs)  61 us
    ppermute x26, waiting for transfers between devices, moved(): return lax.ppermute(value, axes, pairs)  28.4 us
    pallas_call x3, Pallas kernels, attend(): pl.pallas_call(functools.partial(attend_kernel, count, own, resume, last)...  15.3 us
    dot_general x12, matrix products, product(): jnp.dot(lines, w, preferred_element_type=jnp.float32)  5.27 us
  transfers between devices with their start and end apart: 26, of which 7 were waited for; matrix products, arithmetic and copies ran while one was open for 9% of the time, Pallas kernels for 13%

profile of v6, /device:TPU:17, one launch (start us, length us, event | category | flops | bytes accessed | tf_op | source)
XLA Modules:
  0.0 119.6 jit_solution(13185154481619533356)
XLA Ops:
  0.0 1.9 %shard_map.55.refs_0_ = bf16[384,512]{1,0:T(8,128)(2,1)} custom-call(bf16[384,256]{1,0:T(8,128)(2,1)} %left.1, bf16[384,256]{1,0:T(8,128)(2,1)} %right.1), custom_call_target="tpu_custom_call" | custom-call | tf_op jit(solution)/shard_map/pallas_call | solution.py:168
  1.9 3.2 %collective-permute-start = (bf16[384,512]{1,0:T(8,128)(2,1)}, bf16[384,512]{1,0:T(8,128)(2,1)S(1)}, u32[]{:S(2)}, u32[]{:S(2)}) collective-permute-start(bf16[384,512]{1,0:T(8,128)(2,1)} %shard_map.55.refs_0_), channel_id=1, source_target_pairs={{0,8},{1,9},{2,10},{3,11},{4,12},{5,13},{6,14},{7,15},{8,16},{9,17... | collective-permute-start | bytes 1179656 | tf_op jit(solution)/shard_map/ppermute | solution.py:157
  6.3 3.0 %collective-permute-start.9 = (bf16[1024,512]{1,0:T(8,128)(2,1)}, bf16[1024,512]{1,0:T(8,128)(2,1)}, u32[]{:S(2)}, u32[]{:S(2)}) collective-permute-start(bf16[1024,512]{1,0:T(8,128)(2,1)} %param.9), channel_id=1, source_target_pairs={{16,0},{17,1},{18,2},{19,3},{20,4},{21,5},{22,6},{23,7},{24,8},{25... | collective-permute-start | bytes 3145736 | tf_op jit(solution)/shard_map/ppermute | solution.py:157
  10.1 3.9 %collective-permute-done.refs_1_ = bf16[384,512]{1,0:T(8,128)(2,1)S(1)} collective-permute-done((bf16[384,512]{1,0:T(8,128)(2,1)}, bf16[384,512]{1,0:T(8,128)(2,1)S(1)}, u32[]{:S(2)}, u32[]{:S(2)}) %collective-permute-start) | collective-permute-done | bytes 393248 | tf_op jit(solution)/shard_map/ppermute | solution.py:157
  13.9 3.2 %collective-permute-start.1 = (bf16[384,512]{1,0:T(8,128)(2,1)S(1)}, bf16[384,512]{1,0:T(8,128)(2,1)S(1)}, u32[]{:S(2)}, u32[]{:S(2)}) collective-permute-start(bf16[384,512]{1,0:T(8,128)(2,1)S(1)} %collective-permute-done.refs_1_), channel_id=1, source_target_pairs={{8,16},{9,17},{10,18},{11,19},{12,20},{13,21},{14,22},{15,23},{16,... | collective-permute-start | bytes 1179656 | tf_op jit(solution)/shard_map/ppermute | solution.py:157
  17.3 3.1 %collective-permute-start.3 = (bf16[384,512]{1,0:T(8,128)(2,1)S(1)}, bf16[384,512]{1,0:T(8,128)(2,1)S(1)}, u32[]{:S(2)}, u32[]{:S(2)}) collective-permute-start(bf16[384,512]{1,0:T(8,128)(2,1)S(1)} %collective-permute-done.refs_1_), channel_id=1, source_target_pairs={{8,12},{9,13},{10,14},{11,15},{12,8},{13,9},{14,10},{15,11},{16,20... | collective-permute-start | bytes 1179656 | tf_op jit(solution)/shard_map/ppermute | solution.py:157
  20.7 1.6 %collective-permute-start.11 = (bf16[1024,512]{1,0:T(8,128)(2,1)}, bf16[1024,512]{1,0:T(8,128)(2,1)}, u32[]{:S(2)}, u32[]{:S(2)}) collective-permute-start(bf16[1024,512]{1,0:T(8,128)(2,1)} %param.9), channel_id=1, source_target_pairs={{8,24},{9,25},{10,26},{11,27},{12,28},{13,29},{14,30},{15,31}} | collective-permute-start | bytes 3145736 | tf_op jit(solution)/shard_map/ppermute | solution.py:157
  22.3 2.6 %collective-permute-done.1.refs_1_ = bf16[384,512]{1,0:T(8,128)(2,1)S(1)} collective-permute-done((bf16[384,512]{1,0:T(8,128)(2,1)S(1)}, bf16[384,512]{1,0:T(8,128)(2,1)S(1)}, u32[]{:S(2)}, u32[]{:S(2)}) %collective-permute-start.1) | collective-permute-done | bytes 393248 | tf_op jit(solution)/shard_map/ppermute | solution.py:157
  25.9 2.1 %collective-permute-start.2 = (bf16[384,512]{1,0:T(8,128)(2,1)S(1)}, bf16[384,512]{1,0:T(8,128)(2,1)S(1)}, u32[]{:S(2)}, u32[]{:S(2)}) collective-permute-start(bf16[384,512]{1,0:T(8,128)(2,1)S(1)} %broadcast_select_fusion.2), channel_id=1, source_target_pairs={{0,4},{1,5},{2,6},{3,7},{8,12},{9,13},{10,14},{11,15},{16,20},{17,... | collective-permute-start | bytes 1179656 | tf_op jit(solution)/shard_map/ppermute | solution.py:157
  28.1 9.4 %collective-permute-done.3.refs_0_ = bf16[384,512]{1,0:T(8,128)(2,1)S(1)} collective-permute-done((bf16[384,512]{1,0:T(8,128)(2,1)S(1)}, bf16[384,512]{1,0:T(8,128)(2,1)S(1)}, u32[]{:S(2)}, u32[]{:S(2)}) %collective-permute-start.3) | collective-permute-done | bytes 393248 | tf_op jit(solution)/shard_map/ppermute | solution.py:157
  39.8 4.8 %shard_map.56 = (f32[384,2048]{1,0:T(8,128)S(1)}, f32[384,1024]{1,0:T(8,128)S(1)}) custom-call(s32[2]{0:T(128)S(1)} %pad_add_fusion.1.bases, bf16[384,1024]{1,0:T(8,128)(2,1)S(1)} %copy-done.1, s32[384,1]{1,0:T(8,128)S(1)} %broadcast_in_dim.38.start_ref, bf16[384,512]{1,0:T(8,128)(2,1)S(1)} %copy-done, bf16[384,512]{1,0:T(8,128)(2,1)S(1)} %collective-permute-done.refs_1_), custom_call_target="tpu_custom_call" | custom-call | flops 3623878656 | bytes 1572864 | tf_op jit(solution)/shard_map/pallas_call | solution.py:131
  44.6 6.5 %shard_map.57 = (f32[384,2048]{1,0:T(8,128)S(1)}, f32[384,1024]{1,0:T(8,128)S(1)}) custom-call(s32[2]{0:T(128)S(1)} %pad_add_fusion.bases, bf16[384,1024]{1,0:T(8,128)(2,1)S(1)} %copy-done.1, s32[384,1]{1,0:T(8,128)S(1)} %broadcast_in_dim.38.start_ref, bf16[384,512]{1,0:T(8,128)(2,1)S(1)} %collective-permute-done.3.refs_0_, ...), custom_call_target="tpu_custom_call" | custom-call | flops 3623878656 | bytes 1572864 | tf_op jit(solution)/shard_map/pallas_call | solution.py:131
  51.1 4.1 %shard_map.58 = bf16[384,1024]{1,0:T(8,128)(2,1)S(1)} custom-call(s32[1]{0:T(128)} %bitcast.bases, bf16[384,1024]{1,0:T(8,128)(2,1)S(1)} %copy-done.1, s32[384,1]{1,0:T(8,128)S(1)} %broadcast_in_dim.38.start_ref, bf16[384,512]{1,0:T(8,128)(2,1)S(1)} %collective-permute-done.2.refs_0_, f32[384,2048]{1,0:T(8,128)S(1)} %get-tuple-element.13.refs_1_, ...), custom_call_target="tpu_custom_call" | custom-call | flops 1811939328 | bytes 1572864 | tf_op jit(solution)/shard_map/pallas_call | solution.py:131
  55.4 6.6 %collective-permute-done.10 = bf16[1024,512]{1,0:T(8,128)(2,1)} collective-permute-done((bf16[1024,512]{1,0:T(8,128)(2,1)}, bf16[1024,512]{1,0:T(8,128)(2,1)}, u32[]{:S(2)}, u32[]{:S(2)}) %collective-permute-start.10) | collective-permute-done | bytes 1048608 | tf_op jit(solution)/shard_map/ppermute | solution.py:157
  62.0 2.0 %fusion.1 = (bf16[1024,256]{1,0:T(8,128)(2,1)S(1)}, bf16[1024,256]{1,0:T(8,128)(2,1)S(1)}) fusion(bf16[1024,512]{1,0:T(8,128)(2,1)} %collective-permute-done.11, bf16[1024,512]{1,0:T(8,128)(2,1)} %collective-permute-done.10, bf16[1024,512]{1,0:T(8,128)(2,1)} %collective-permute-done.9, pred[]{:T(512)S(6)} %eq.22, pred[]{:T(512)S(6)} %lt.21), kind=kLoop, calls=%fused_computation.20 | loop fusion | flops 1048576 | bytes 4194306 | tf_op jit(solution)/shard_map/jit(_where)/select_n | solution.py:197
  65.5 2.0 %collective-permute-done.5 = bf16[384,1024]{1,0:T(8,128)(2,1)S(1)} collective-permute-done((bf16[384,1024]{1,0:T(8,128)(2,1)S(1)}, bf16[384,1024]{1,0:T(8,128)(2,1)S(1)}, u32[]{:S(2)}, u32[]{:S(2)}) %collective-permute-start.5) | collective-permute-done | bytes 786464 | tf_op jit(solution)/shard_map/ppermute | solution.py:157
  68.9 11.9 %collective-permute-start.6 = (bf16[384,512]{1,0:T(8,128)(2,1)S(1)}, bf16[384,512]{1,0:T(8,128)(2,1)S(1)}, u32[]{:S(2)}, u32[]{:S(2)}) collective-permute-start(bf16[384,512]{1,0:T(8,128)(2,1)S(1)} %convolution_convert_fusion.1), channel_id=1, source_target_pairs={{0,1},{1,0},{2,3},{3,2},{4,5},{5,4},{6,7},{7,6},{8,9},{9,8},{10,11... | collective-permute-start | bytes 1179656 | tf_op jit(solution)/shard_map/ppermute | solution.py:157
  83.4 3.2 %collective-permute-start.7 = (bf16[384,512]{1,0:T(8,128)(2,1)S(1)}, bf16[384,512]{1,0:T(8,128)(2,1)S(1)}, u32[]{:S(2)}, u32[]{:S(2)}) collective-permute-start(bf16[384,512]{1,0:T(8,128)(2,1)S(1)} %get-tuple-element.27), channel_id=1, source_target_pairs={{2,0},{3,1},{6,4},{7,5},{10,8},{11,9},{14,12},{15,13},{16,18},{17,... | collective-permute-start | bytes 1179656 | tf_op jit(solution)/shard_map/ppermute | solution.py:157
  86.7 1.3 %collective-permute-start.13 = (bf16[384,512]{1,0:T(8,128)(2,1)S(1)}, bf16[384,512]{1,0:T(8,128)(2,1)S(1)}, u32[]{:S(2)}, u32[]{:S(2)}) collective-permute-start(bf16[384,512]{1,0:T(8,128)(2,1)S(1)} %fusion.2), channel_id=1, source_target_pairs={{0,2},{1,3},{4,6},{5,7},{8,10},{9,11},{12,14},{13,15},{18,16},{19,... | collective-permute-start | bytes 1179656 | tf_op jit(solution)/shard_map/ppermute | solution.py:157
  88.6 4.2 %collective-permute-start.16 = (bf16[384,512]{1,0:T(8,128)(2,1)S(1)}, bf16[384,512]{1,0:T(8,128)(2,1)S(1)}, u32[]{:S(2)}, u32[]{:S(2)}) collective-permute-start(bf16[384,512]{1,0:T(8,128)(2,1)S(1)} %get-tuple-element.25), channel_id=1, source_target_pairs={{2,0},{3,1},{6,4},{7,5},{10,8},{11,9},{14,12},{15,13},{16,18},{17,... | collective-permute-start | bytes 1179656 | tf_op jit(solution)/shard_map/ppermute | solution.py:157
  99.6 5.8 %collective-permute-start.14 = (bf16[384,512]{1,0:T(8,128)(2,1)S(1)}, bf16[384,512]{1,0:T(8,128)(2,1)S(1)}, u32[]{:S(2)}, u32[]{:S(2)}) collective-permute-start(bf16[384,512]{1,0:T(8,128)(2,1)S(1)} %add_convert_fusion.1), channel_id=1, source_target_pairs={{3,10},{7,14},{10,3},{14,7},{17,24},{21,28},{24,17},{28,21}} | collective-permute-start | bytes 1179656 | tf_op jit(solution)/shard_map/ppermute | solution.py:157
  106.3 4.7 %collective-permute-start.21 = (bf16[384,256]{1,0:T(8,128)(2,1)S(1)}, bf16[384,256]{1,0:T(8,128)(2,1)S(1)}, u32[]{:S(2)}, u32[]{:S(2)}) collective-permute-start(bf16[384,256]{1,0:T(8,128)(2,1)S(1)} %add_convert_fusion.4), channel_id=1, source_target_pairs={{3,10},{7,14},{10,3},{14,7},{17,24},{21,28},{24,17},{28,21}} | collective-permute-start | bytes 589832 | tf_op jit(solution)/shard_map/ppermute | solution.py:157
  111.1 3.7 %collective-permute-start.25 = (bf16[384,256]{1,0:T(8,128)(2,1)S(1)}, bf16[384,256]{1,0:T(8,128)(2,1)S(1)}, u32[]{:S(2)}, u32[]{:S(2)}) collective-permute-start(bf16[384,256]{1,0:T(8,128)(2,1)S(1)} %add_convert_fusion.3), channel_id=1, source_target_pairs={{3,10},{7,14},{10,3},{14,7},{17,24},{21,28},{24,17},{28,21}} | collective-permute-start | bytes 589832 | tf_op jit(solution)/shard_map/ppermute | solution.py:157
  114.9 3.3 %collective-permute-done.25 = bf16[384,256]{1,0:T(8,128)(2,1)S(1)} collective-permute-done((bf16[384,256]{1,0:T(8,128)(2,1)S(1)}, bf16[384,256]{1,0:T(8,128)(2,1)S(1)}, u32[]{:S(2)}, u32[]{:S(2)}) %collective-permute-start.25) | collective-permute-done | bytes 196640 | tf_op jit(solution)/shard_map/ppermute | solution.py:157
  (71 shorter events, 21.1 us)
Async XLA Ops:
  1.9 12.1 %collective-permute-start = (bf16[384,512]{1,0:T(8,128)(2,1)}, bf16[384,512]{1,0:T(8,128)(2,1)S(1)}, u32[]{:S(2)}, u32[]{:S(2)}) collective-permute-start(bf16[384,512]{1,0:T(8,128)(2,1)} %shard_map.55.refs_0_), channel_id=1, source_target_pairs={{0,8},{1,9},{2,10},{3,11},{4,12},{5,13},{6,14},{7,15},{8,16},{9,17... | collective-permute-start | bytes 1179656 | tf_op jit(solution)/shard_map/ppermute | solution.py:157
  5.1 46.0 %collective-permute-start.4 = (bf16[1024,512]{1,0:T(8,128)(2,1)}, bf16[1024,512]{1,0:T(8,128)(2,1)S(1)}, u32[]{:S(2)}, u32[]{:S(2)}) collective-permute-start(bf16[1024,512]{1,0:T(8,128)(2,1)} %param.9), channel_id=1, source_target_pairs={{0,4},{1,5},{2,6},{3,7},{4,0},{5,1},{6,2},{7,3},{8,12},{9,13},{10,... | collective-permute-start | bytes 3145736 | tf_op jit(solution)/shard_map/ppermute | solution.py:157
  6.3 49.0 %collective-permute-start.9 = (bf16[1024,512]{1,0:T(8,128)(2,1)}, bf16[1024,512]{1,0:T(8,128)(2,1)}, u32[]{:S(2)}, u32[]{:S(2)}) collective-permute-start(bf16[1024,512]{1,0:T(8,128)(2,1)} %param.9), channel_id=1, source_target_pairs={{16,0},{17,1},{18,2},{19,3},{20,4},{21,5},{22,6},{23,7},{24,8},{25... | collective-permute-start | bytes 3145736 | tf_op jit(solution)/shard_map/ppermute | solution.py:157
  13.9 10.9 %collective-permute-start.1 = (bf16[384,512]{1,0:T(8,128)(2,1)S(1)}, bf16[384,512]{1,0:T(8,128)(2,1)S(1)}, u32[]{:S(2)}, u32[]{:S(2)}) collective-permute-start(bf16[384,512]{1,0:T(8,128)(2,1)S(1)} %collective-permute-done.refs_1_), channel_id=1, source_target_pairs={{8,16},{9,17},{10,18},{11,19},{12,20},{13,21},{14,22},{15,23},{16,... | collective-permute-start | bytes 1179656 | tf_op jit(solution)/shard_map/ppermute | solution.py:157
  17.3 20.2 %collective-permute-start.3 = (bf16[384,512]{1,0:T(8,128)(2,1)S(1)}, bf16[384,512]{1,0:T(8,128)(2,1)S(1)}, u32[]{:S(2)}, u32[]{:S(2)}) collective-permute-start(bf16[384,512]{1,0:T(8,128)(2,1)S(1)} %collective-permute-done.refs_1_), channel_id=1, source_target_pairs={{8,12},{9,13},{10,14},{11,15},{12,8},{13,9},{14,10},{15,11},{16,20... | collective-permute-start | bytes 1179656 | tf_op jit(solution)/shard_map/ppermute | solution.py:157
  20.7 34.7 %collective-permute-start.11 = (bf16[1024,512]{1,0:T(8,128)(2,1)}, bf16[1024,512]{1,0:T(8,128)(2,1)}, u32[]{:S(2)}, u32[]{:S(2)}) collective-permute-start(bf16[1024,512]{1,0:T(8,128)(2,1)} %param.9), channel_id=1, source_target_pairs={{8,24},{9,25},{10,26},{11,27},{12,28},{13,29},{14,30},{15,31}} | collective-permute-start | bytes 3145736 | tf_op jit(solution)/shard_map/ppermute | solution.py:157
  25.9 25.1 %collective-permute-start.2 = (bf16[384,512]{1,0:T(8,128)(2,1)S(1)}, bf16[384,512]{1,0:T(8,128)(2,1)S(1)}, u32[]{:S(2)}, u32[]{:S(2)}) collective-permute-start(bf16[384,512]{1,0:T(8,128)(2,1)S(1)} %broadcast_select_fusion.2), channel_id=1, source_target_pairs={{0,4},{1,5},{2,6},{3,7},{8,12},{9,13},{10,14},{11,15},{16,20},{17,... | collective-permute-start | bytes 1179656 | tf_op jit(solution)/shard_map/ppermute | solution.py:157
  37.5 24.5 %collective-permute-start.10 = (bf16[1024,512]{1,0:T(8,128)(2,1)}, bf16[1024,512]{1,0:T(8,128)(2,1)}, u32[]{:S(2)}, u32[]{:S(2)}) collective-permute-start(bf16[1024,512]{1,0:T(8,128)(2,1)} %param.9), channel_id=1, source_target_pairs={{0,16},{1,17},{2,18},{3,19},{4,20},{5,21},{6,22},{7,23}} | collective-permute-start | bytes 3145736 | tf_op jit(solution)/shard_map/ppermute | solution.py:157
  55.1 12.3 %collective-permute-start.5 = (bf16[384,1024]{1,0:T(8,128)(2,1)S(1)}, bf16[384,1024]{1,0:T(8,128)(2,1)S(1)}, u32[]{:S(2)}, u32[]{:S(2)}) collective-permute-start(bf16[384,1024]{1,0:T(8,128)(2,1)S(1)} %shard_map.58), channel_id=1, source_target_pairs={{0,8},{1,9},{2,10},{3,11},{4,12},{5,13},{6,14},{7,15},{8,0},{9,1},... | collective-permute-start | bytes 2359304 | tf_op jit(solution)/shard_map/ppermute | solution.py:157
  64.0 28.9 %collective-permute-start.18 = (bf16[1024,256]{1,0:T(8,128)(2,1)S(1)}, bf16[1024,256]{1,0:T(8,128)(2,1)S(1)}, u32[]{:S(2)}, u32[]{:S(2)}) collective-permute-start(bf16[1024,256]{1,0:T(8,128)(2,1)S(1)} %get-tuple-element.17), channel_id=1, source_target_pairs={{0,4},{1,5},{2,6},{3,7},{4,0},{5,1},{6,2},{7,3},{8,12},{9,13},{10,... | collective-permute-start | bytes 1572872 | tf_op jit(solution)/shard_map/ppermute | solution.py:157
  65.2 28.9 %collective-permute-start.22 = (bf16[1024,256]{1,0:T(8,128)(2,1)S(1)}, bf16[1024,256]{1,0:T(8,128)(2,1)S(1)}, u32[]{:S(2)}, u32[]{:S(2)}) collective-permute-start(bf16[1024,256]{1,0:T(8,128)(2,1)S(1)} %get-tuple-element.18), channel_id=1, source_target_pairs={{0,4},{1,5},{2,6},{3,7},{4,0},{5,1},{6,2},{7,3},{8,12},{9,13},{10,... | collective-permute-start | bytes 1572872 | tf_op jit(solution)/shard_map/ppermute | solution.py:157
  68.9 13.9 %collective-permute-start.6 = (bf16[384,512]{1,0:T(8,128)(2,1)S(1)}, bf16[384,512]{1,0:T(8,128)(2,1)S(1)}, u32[]{:S(2)}, u32[]{:S(2)}) collective-permute-start(bf16[384,512]{1,0:T(8,128)(2,1)S(1)} %convolution_convert_fusion.1), channel_id=1, source_target_pairs={{0,1},{1,0},{2,3},{3,2},{4,5},{5,4},{6,7},{7,6},{8,9},{9,8},{10,11... | collective-permute-start | bytes 1179656 | tf_op jit(solution)/shard_map/ppermute | solution.py:157
  80.9 5.7 %collective-permute-start.12 = (bf16[384,512]{1,0:T(8,128)(2,1)S(1)}, bf16[384,512]{1,0:T(8,128)(2,1)S(1)}, u32[]{:S(2)}, u32[]{:S(2)}) collective-permute-start(bf16[384,512]{1,0:T(8,128)(2,1)S(1)} %pad_maximum_fusion), channel_id=1, source_target_pairs={{0,1},{1,0},{2,3},{3,2},{4,5},{5,4},{6,7},{7,6},{8,9},{9,8},{10,11... | collective-permute-start | bytes 1179656 | tf_op jit(solution)/shard_map/ppermute | solution.py:157
  82.3 5.7 %collective-permute-start.15 = (bf16[384,512]{1,0:T(8,128)(2,1)S(1)}, bf16[384,512]{1,0:T(8,128)(2,1)S(1)}, u32[]{:S(2)}, u32[]{:S(2)}) collective-permute-start(bf16[384,512]{1,0:T(8,128)(2,1)S(1)} %convolution_convert_fusion), channel_id=1, source_target_pairs={{0,1},{1,0},{2,3},{3,2},{4,5},{5,4},{6,7},{7,6},{8,9},{9,8},{10,11... | collective-permute-start | bytes 1179656 | tf_op jit(solution)/shard_map/ppermute | solution.py:157
  83.4 15.2 %collective-permute-start.7 = (bf16[384,512]{1,0:T(8,128)(2,1)S(1)}, bf16[384,512]{1,0:T(8,128)(2,1)S(1)}, u32[]{:S(2)}, u32[]{:S(2)}) collective-permute-start(bf16[384,512]{1,0:T(8,128)(2,1)S(1)} %get-tuple-element.27), channel_id=1, source_target_pairs={{2,0},{3,1},{6,4},{7,5},{10,8},{11,9},{14,12},{15,13},{16,18},{17,... | collective-permute-start | bytes 1179656 | tf_op jit(solution)/shard_map/ppermute | solution.py:157
  86.7 12.7 %collective-permute-start.13 = (bf16[384,512]{1,0:T(8,128)(2,1)S(1)}, bf16[384,512]{1,0:T(8,128)(2,1)S(1)}, u32[]{:S(2)}, u32[]{:S(2)}) collective-permute-start(bf16[384,512]{1,0:T(8,128)(2,1)S(1)} %fusion.2), channel_id=1, source_target_pairs={{0,2},{1,3},{4,6},{5,7},{8,10},{9,11},{12,14},{13,15},{18,16},{19,... | collective-permute-start | bytes 1179656 | tf_op jit(solution)/shard_map/ppermute | solution.py:157
  88.6 16.8 %collective-permute-start.16 = (bf16[384,512]{1,0:T(8,128)(2,1)S(1)}, bf16[384,512]{1,0:T(8,128)(2,1)S(1)}, u32[]{:S(2)}, u32[]{:S(2)}) collective-permute-start(bf16[384,512]{1,0:T(8,128)(2,1)S(1)} %get-tuple-element.25), channel_id=1, source_target_pairs={{2,0},{3,1},{6,4},{7,5},{10,8},{11,9},{14,12},{15,13},{16,18},{17,... | collective-permute-start | bytes 1179656 | tf_op jit(solution)/shard_map/ppermute | solution.py:157
  95.6 10.7 %collective-permute-start.20 = (bf16[384,256]{1,0:T(8,128)(2,1)S(1)}, bf16[384,256]{1,0:T(8,128)(2,1)S(1)}, u32[]{:S(2)}, u32[]{:S(2)}) collective-permute-start(bf16[384,256]{1,0:T(8,128)(2,1)S(1)} %get-tuple-element.23), channel_id=1, source_target_pairs={{0,2},{1,3},{4,6},{5,7},{8,10},{9,11},{12,14},{13,15},{18,16},{19,... | collective-permute-start | bytes 589832 | tf_op jit(solution)/shard_map/ppermute | solution.py:157
  97.3 13.8 %collective-permute-start.24 = (bf16[384,256]{1,0:T(8,128)(2,1)S(1)}, bf16[384,256]{1,0:T(8,128)(2,1)S(1)}, u32[]{:S(2)}, u32[]{:S(2)}) collective-permute-start(bf16[384,256]{1,0:T(8,128)(2,1)S(1)} %get-tuple-element.21), channel_id=1, source_target_pairs={{0,2},{1,3},{4,6},{5,7},{8,10},{9,11},{12,14},{13,15},{18,16},{19,... | collective-permute-start | bytes 589832 | tf_op jit(solution)/shard_map/ppermute | solution.py:157
  98.7 19.5 %collective-permute-start.8 = (bf16[384,512]{1,0:T(8,128)(2,1)S(1)}, bf16[384,512]{1,0:T(8,128)(2,1)S(1)}, u32[]{:S(2)}, u32[]{:S(2)}) collective-permute-start(bf16[384,512]{1,0:T(8,128)(2,1)S(1)} %add_convert_fusion.2), channel_id=1, source_target_pairs={{1,8},{5,12},{8,1},{12,5},{19,26},{23,30},{26,19},{30,23}} | collective-permute-start | bytes 1179656 | tf_op jit(solution)/shard_map/ppermute | solution.py:157
  99.6 18.7 %collective-permute-start.14 = (bf16[384,512]{1,0:T(8,128)(2,1)S(1)}, bf16[384,512]{1,0:T(8,128)(2,1)S(1)}, u32[]{:S(2)}, u32[]{:S(2)}) collective-permute-start(bf16[384,512]{1,0:T(8,128)(2,1)S(1)} %add_convert_fusion.1), channel_id=1, source_target_pairs={{3,10},{7,14},{10,3},{14,7},{17,24},{21,28},{24,17},{28,21}} | collective-permute-start | bytes 1179656 | tf_op jit(solution)/shard_map/ppermute | solution.py:157
  105.6 12.8 %collective-permute-start.17 = (bf16[384,512]{1,0:T(8,128)(2,1)S(1)}, bf16[384,512]{1,0:T(8,128)(2,1)S(1)}, u32[]{:S(2)}, u32[]{:S(2)}) collective-permute-start(bf16[384,512]{1,0:T(8,128)(2,1)S(1)} %add_convert_fusion), channel_id=1, source_target_pairs={{1,8},{5,12},{8,1},{12,5},{19,26},{23,30},{26,19},{30,23}} | collective-permute-start | bytes 1179656 | tf_op jit(solution)/shard_map/ppermute | solution.py:157
  106.3 8.6 %collective-permute-start.21 = (bf16[384,256]{1,0:T(8,128)(2,1)S(1)}, bf16[384,256]{1,0:T(8,128)(2,1)S(1)}, u32[]{:S(2)}, u32[]{:S(2)}) collective-permute-start(bf16[384,256]{1,0:T(8,128)(2,1)S(1)} %add_convert_fusion.4), channel_id=1, source_target_pairs={{3,10},{7,14},{10,3},{14,7},{17,24},{21,28},{24,17},{28,21}} | collective-permute-start | bytes 589832 | tf_op jit(solution)/shard_map/ppermute | solution.py:157
  111.1 7.1 %collective-permute-start.25 = (bf16[384,256]{1,0:T(8,128)(2,1)S(1)}, bf16[384,256]{1,0:T(8,128)(2,1)S(1)}, u32[]{:S(2)}, u32[]{:S(2)}) collective-permute-start(bf16[384,256]{1,0:T(8,128)(2,1)S(1)} %add_convert_fusion.3), channel_id=1, source_target_pairs={{3,10},{7,14},{10,3},{14,7},{17,24},{21,28},{24,17},{28,21}} | collective-permute-start | bytes 589832 | tf_op jit(solution)/shard_map/ppermute | solution.py:157
  (5 other events, 46.5 us)
